TPU v7x, 128 devices: a whole 4x4x4 slice. The times are simulated.
128 devices in a mesh: exp: 32 (over z, y, core), tp: 4 (over x).
Axes of the slice: x: 4, y: 4, z: 4, core: 2. Of those that a mesh axis runs over, the one named last changes fastest.
Arguments:
- layer_in: bfloat16 [32768, 768], P('exp'), may hold values from -6 to 6
- expert_ids: int32 [32768, 1], P('exp'), may hold values from 0 to 31; in each aligned block of 1024 rows (0 to 1023, 1024 to 2047, ...) at most 40 rows name the same one
- rel_buckets: int32 [2047], replicated, may hold values from 0 to 31
- first_gain: float32 [768], replicated, may hold values from 0.5 to 1.5
- query_weight: bfloat16 [768, 768], P(None, 'tp'), may hold values from -0.02734375 to 0.02734375
- key_weight: bfloat16 [768, 768], P(None, 'tp'), may hold values from -0.21875 to 0.21875
- value_weight: bfloat16 [768, 768], P(None, 'tp'), may hold values from -0.21875 to 0.21875
- proj_weight: bfloat16 [768, 768], P('tp'), may hold values from -2.5 to 2.5
- rel_table: float32 [32, 12], P(None, 'tp'), may hold values from -6 to 6
- second_gain: float32 [768], replicated, may hold values from 0.5 to 1.5
- router_weight: bfloat16 [768, 32], replicated, may hold values from -0.109375 to 0.109375
- expert_in: bfloat16 [32, 768, 3072], P('exp', None, 'tp'), may hold values from -0.21875 to 0.21875
- expert_out: bfloat16 [32, 3072, 768], P('exp', 'tp'), may hold values from -6 to 6
- cotangent: bfloat16 [32768, 768], P('exp'), may hold values from -6 to 6
Outputs:
- layer_out: bfloat16 [32768, 768], P('exp')
- input_grad: float32 [32768, 768], P('exp')
- first_gain_grad: float32 [768], replicated
- query_grad: float32 [768, 768], P(None, 'tp')
- key_grad: float32 [768, 768], P(None, 'tp')
- value_grad: float32 [768, 768], P(None, 'tp')
- proj_grad: float32 [768, 768], P('tp')
- table_grad: float32 [32, 12], P(None, 'tp')
- second_gain_grad: float32 [768], replicated
- router_grad: float32 [768, 32], replicated
- expert_in_grad: float32 [32, 768, 3072], P('exp', None, 'tp')
- expert_out_grad: float32 [32, 3072, 768], P('exp', 'tp')
Inputs may be any that keep to these rules, and one draw needn't show every extreme that they name: `expert_ids`: in the 1024 rows of one index of exp (aligned blocks) no expert is named by more than 40 rows, a bound that some block reaches. `rel_buckets`: entry m is the bucket of the offset m - 1023.
All inputs are finite; a program needn't handle non-finite values.
Results may differ from a plain program's by a relative error of at most 0.025.
Values may be sent and summed in bfloat16 or wider, within the bound.
A program may use at most 192 MiB of HBM per device.

v0:
```python
import functools

import jax
import jax.numpy as jnp
from jax import lax
from jax.experimental import pallas as pl
from jax.experimental.pallas import tpu as pltpu
from jax.sharding import PartitionSpec as P

epsilon = 1e-06
gelu_root = 0.7978845608028654
gelu_cube = 0.044715
BF = jnp.bfloat16
F32 = jnp.float32
BLOCK = 128
MIB = 1024 * 1024


def product(left, right):
    return jnp.dot(left, right, preferred_element_type=F32)


def rows_product(left, right):
    return lax.dot_general(left, right, (((0,), (0,)), ((), ())), preferred_element_type=F32)


def cols_product(left, right):
    return lax.dot_general(left, right, (((1,), (1,)), ((), ())), preferred_element_type=F32)


def inverse_rms(values):
    return lax.rsqrt(jnp.mean(values * values, axis=-1, keepdims=True) + epsilon)


def call(body, name, outs, scratch, *operands, mib=48):
    vmem = pl.BlockSpec(memory_space=pltpu.VMEM)
    return pl.pallas_call(
        body,
        name=name,
        out_shape=[jax.ShapeDtypeStruct(shape, dtype) for shape, dtype in outs],
        in_specs=[vmem] * len(operands),
        out_specs=[vmem] * len(outs),
        scratch_shapes=scratch,
        compiler_params=pltpu.CompilerParams(vmem_limit_bytes=mib * MIB),
    )(*operands)


def head_mask(head, head_width, width):
    lane = lax.broadcasted_iota(jnp.int32, (1, width), 1)
    return jnp.where(lane // head_width == head, 1.0, 0.0)


def fill_bias(bias, buckets, table):
    heads, block, width = bias.shape
    padded = buckets.shape[1]
    number = lax.broadcasted_iota(jnp.int32, (table.shape[0], padded), 0)
    hot = jnp.where(buckets[...] == number, 1.0, 0.0)
    offsets = lax.dot_general(
        table[...],
        hot,
        (((0,), (0,)), ((), ())),
        precision=lax.Precision.HIGHEST,
        preferred_element_type=F32,
    )
    for head in range(heads):
        spread = jnp.broadcast_to(offsets[head : head + 1, :], (block, padded))
        rolled = pltpu.roll(spread, padded - (block - 1), 1, stride=1, stride_axis=0)
        bias[head] = rolled[:, :width]


def attend_body(
    head_width, rows, gain, query_w, key_w, value_w, buckets, table,
    mixed, normed, query, query_t, key, key_t, value_t, logsum, bias, value,
):
    heads = bias.shape[0]
    tokens = rows.shape[0]
    width = query.shape[1]
    blocks = tokens // BLOCK
    inputs = rows[...].astype(F32)
    low = (inputs * inverse_rms(inputs) * gain[...]).astype(BF)
    normed[...] = low
    query_full = product(low, query_w[...])
    key_full = product(low, key_w[...])
    value_full = product(low, value_w[...])
    query[...] = query_full.astype(BF)
    key[...] = key_full.astype(BF)
    value[...] = value_full.astype(BF)
    query_t[...] = query_full.T.astype(BF)
    key_t[...] = key_full.T.astype(BF)
    value_t[...] = value_full.T.astype(BF)
    fill_bias(bias, buckets, table)

    def step(block, carry):
        first = pl.multiple_of(block * BLOCK, BLOCK)
        shift = pl.multiple_of((blocks - 1 - block) * BLOCK, BLOCK)
        query_rows = query[pl.ds(first, BLOCK), :]
        total = jnp.zeros((BLOCK, width), F32)
        for head in range(heads):
            mask = head_mask(head, head_width, width)
            scores = product(query_rows * mask.astype(BF), key_t[...])
            scores = scores + bias[head, :, pl.ds(shift, tokens)]
            highest = jnp.max(scores, axis=-1, keepdims=True)
            weights = jnp.exp(scores - highest)
            summed = jnp.sum(weights, axis=-1, keepdims=True)
            part = product(weights.astype(BF), value[...]) / summed
            total = total + part * mask
            logsum[pl.ds(first, BLOCK), head : head + 1] = highest + jnp.log(summed)
        mixed[pl.ds(first, BLOCK), :] = total.astype(BF)
        return carry

    lax.fori_loop(0, blocks, step, 0)


def pack(first, second, third, experts):
    half = third.shape[1] // 2
    split = third.reshape(experts, 8, 2 * half)
    split = jnp.concatenate([split[:, :, :half], split[:, :, half:]], axis=1)
    return first, second, split.reshape(experts * 16, half)


def unpack_third(tail, runs):
    half = tail.shape[1]
    split = tail.astype(F32).reshape(runs, 16, half)
    return jnp.concatenate([split[:, :8], split[:, 8:]], axis=2).reshape(runs * 8, 2 * half)


def slot_of_row(row, experts, capacity):
    body = 16 * experts
    first = (row // 16) * capacity + row % 16
    second = ((row - body) // 16) * capacity + 16 + (row - body) % 16
    third = ((row - 2 * body) // 8) * capacity + 32 + (row - 2 * body) % 8
    return jnp.where(row < body, first, jnp.where(row < 2 * body, second, third))


def route_body(
    capacity, rows, mixed, proj, gain, router_w, ids, ids_row, cotangent,
    residual, hidden, probs, send_rows, send_grads, slots, gates,
):
    tokens, width = rows.shape
    experts = router_w.shape[1]
    body = 16 * experts
    res = rows[...].astype(F32) + product(mixed[...], proj[...])
    residual[...] = res
    low = (res * inverse_rms(res) * gain[...]).astype(BF)
    hidden[...] = low
    logits = product(low, router_w[...])
    shifted = jnp.exp(logits - jnp.max(logits, axis=-1, keepdims=True))
    chances = shifted / jnp.sum(shifted, axis=-1, keepdims=True)
    probs[...] = chances
    hot = ids[...] == lax.broadcasted_iota(jnp.int32, (tokens, experts), 1)
    hot_t = ids_row[...] == lax.broadcasted_iota(jnp.int32, (experts, tokens), 0)
    gate = jnp.sum(jnp.where(hot, chances, 0.0), axis=1, keepdims=True)
    gates[...] = gate
    across = lax.broadcasted_iota(jnp.int32, (tokens, tokens), 0)
    along = lax.broadcasted_iota(jnp.int32, (tokens, tokens), 1)
    lower = jnp.where(across >= along, 1.0, 0.0).astype(BF)
    upper = jnp.where(across <= along, 1.0, 0.0).astype(BF)
    counts = product(lower, jnp.where(hot, 1.0, 0.0).astype(BF))
    counts_t = product(jnp.where(hot_t, 1.0, 0.0).astype(BF), upper)
    position = jnp.sum(jnp.where(hot, counts - 1.0, 0.0), axis=1, keepdims=True)
    position_t = jnp.sum(jnp.where(hot_t, counts_t - 1.0, 0.0), axis=0, keepdims=True)
    slots[...] = ids[...] * capacity + position.astype(jnp.int32)
    slots_t = ids_row[...] * capacity + position_t.astype(jnp.int32)
    grads = (gate * cotangent[...].astype(F32)).astype(BF)

    def group(begin, count):
        number = slot_of_row(
            lax.broadcasted_iota(jnp.int32, (count, 1), 0) + begin, experts, capacity
        )
        return jnp.where(number == slots_t, 1.0, 0.0).astype(BF)

    for begin, count, lane in ((0, body, 0), (body, body, width)):
        place = group(begin, count)
        send_rows[:, lane : lane + width] = product(place, low).astype(BF)
        send_grads[:, lane : lane + width] = product(place, grads).astype(BF)
    place = group(2 * body, body // 2)
    send_rows[:, 2 * width :] = pack(0, 0, product(place, low), experts)[2].astype(BF)
    send_grads[:, 2 * width :] = pack(0, 0, product(place, grads), experts)[2].astype(BF)


def expert_body(
    rows, grads, weight_in, weight_out,
    value, back, in_grad, out_grad, tail_rows, tail_grads, tail_value, tail_back, tail_dot,
):
    width = weight_in.shape[0]
    body = rows.shape[0]
    runs = body // 16
    tail_rows[...] = unpack_third(rows[:, 2 * width :], runs).astype(BF)
    tail_grads[...] = unpack_third(grads[:, 2 * width :], runs).astype(BF)
    in_grad[...] = jnp.zeros(in_grad.shape, F32)
    out_grad[...] = jnp.zeros(out_grad.shape, F32)

    def chunk(x, g):
        pre = product(x, weight_in[...])
        inner = jnp.tanh(gelu_root * (pre + gelu_cube * pre * pre * pre))
        act = (0.5 * pre * (1.0 + inner)).astype(BF)
        slope = 0.5 * (1.0 + inner) + 0.5 * pre * (1.0 - inner * inner) * (
            gelu_root * (1.0 + 3.0 * gelu_cube * pre * pre)
        )
        out = product(act, weight_out[...])
        dots = jnp.sum(out * g.astype(F32), axis=1, keepdims=True)
        out_grad[...] += rows_product(act, g)
        act_grad = cols_product(g, weight_out[...])
        pre_grad = (act_grad * slope).astype(BF)
        in_grad[...] += rows_product(x, pre_grad)
        rows_back = cols_product(pre_grad, weight_in[...])
        return out, dots, rows_back

    lane = lax.broadcasted_iota(jnp.int32, (1, 128), 1)
    part = 256
    for begin in range(0, body, part):
        spot = pl.ds(begin, part)
        marks = jnp.zeros((part, 128), F32)
        for side in (0, 1):
            lanes = slice(side * width, (side + 1) * width)
            out, dots, rows_back = chunk(rows[spot, lanes], grads[spot, lanes])
            value[spot, lanes] = out.astype(BF)
            back[spot, lanes] = rows_back.astype(BF)
            marks = marks + jnp.where(lane == side, dots, 0.0)
        back[spot, 2 * width + width // 2 :] = marks.astype(BF)
    out, dots, rows_back = chunk(tail_rows[...], tail_grads[...])
    value[:, 2 * width :] = pack(0, 0, out, runs)[2].astype(BF)
    back[:, 2 * width : 2 * width + width // 2] = pack(0, 0, rows_back, runs)[2].astype(BF)
    spread = jnp.where(lane == 2, dots, 0.0).reshape(runs, 8, 128)
    spread = jnp.concatenate([spread, jnp.zeros_like(spread)], axis=1).reshape(body, 128)
    marks = back[:, 2 * width + width // 2 :].astype(F32) + spread
    back[:, 2 * width + width // 2 :] = marks.astype(BF)


def place_of(slots, experts, capacity, rows):
    number = slot_of_row(lax.broadcasted_iota(jnp.int32, (1, rows), 1), experts, capacity)
    return jnp.where(slots == number, 1.0, 0.0).astype(BF)


def token_body(
    capacity, returned, back, slots, gates, residual, hidden, probs, ids, gain, router_w,
    cotangent, mixed, proj,
    output, router_grad, gain_grad, residual_grad, proj_grad, mixed_grad, mixed_grad_t,
):
    tokens, width = residual.shape
    experts = router_w.shape[1]
    body = 16 * experts
    place = place_of(slots[...], experts, capacity, 5 * body // 2)

    def fetch(ref):
        picked = product(place[:, :body], ref[:, :width])
        picked = picked + product(place[:, body : 2 * body], ref[:, width : 2 * width])
        tail = unpack_third(ref[:, 2 * width : 2 * width + width // 2], experts).astype(BF)
        return picked + product(place[:, 2 * body :], tail)

    token_rows = fetch(returned)
    upstream = cotangent[...].astype(F32)
    res = residual[...]
    output[...] = (res + gates[...] * token_rows).astype(BF)
    marks = back[:, 2 * width + width // 2 :]
    lane = lax.broadcasted_iota(jnp.int32, (1, 128), 1)
    tail = marks.astype(F32).reshape(experts, 16, 128)[:, :8].reshape(experts * 8, 128).astype(BF)
    dots = jnp.where(lane == 0, product(place[:, :body], marks), 0.0)
    dots = dots + jnp.where(lane == 1, product(place[:, body : 2 * body], marks), 0.0)
    dots = dots + jnp.where(lane == 2, product(place[:, 2 * body :], tail), 0.0)
    weighted = jnp.sum(dots, axis=1, keepdims=True)
    hot = ids[...] == lax.broadcasted_iota(jnp.int32, (tokens, experts), 1)
    logit_grad = (jnp.where(hot, weighted, 0.0) - probs[...] * weighted).astype(BF)
    router_grad[...] = rows_product(hidden[...], logit_grad).astype(BF)
    hidden_grad = fetch(back) + cols_product(logit_grad, router_w[...])
    scale = inverse_rms(res)
    gain_grad[...] = jnp.sum(hidden_grad * res * scale, axis=0, keepdims=True).astype(BF)
    scaled = gain[...] * hidden_grad
    middle = jnp.mean(scaled * res, axis=-1, keepdims=True)
    total = upstream + scale * scaled - res * (scale * scale * scale * middle)
    low = total.astype(BF)
    residual_grad[...] = total
    proj_grad[...] = rows_product(mixed[...], low).astype(BF)
    mixed_grad[...] = cols_product(low, proj[...]).astype(BF)
    mixed_grad_t[...] = cols_product(proj[...], low).astype(BF)


def attend_back_body(
    head_width, normed, query, query_t, key, key_t, value_t, logsum, grad, grad_t,
    query_w, key_w, value_w, buckets, table,
    normed_part, query_grad, key_grad, value_grad, table_grad,
    bias, sums, query_back, key_acc, value_acc,
):
    heads = bias.shape[0]
    tokens, width = query.shape
    blocks = tokens // BLOCK
    fill_bias(bias, buckets, table)
    sums[...] = jnp.zeros(sums.shape, F32)
    key_acc[...] = jnp.zeros(key_acc.shape, F32)
    value_acc[...] = jnp.zeros(value_acc.shape, F32)

    def step(block, carry):
        first = pl.multiple_of(block * BLOCK, BLOCK)
        shift = pl.multiple_of((blocks - 1 - block) * BLOCK, BLOCK)
        query_rows = query[pl.ds(first, BLOCK), :]
        grad_rows = grad[pl.ds(first, BLOCK), :]
        total = jnp.zeros((BLOCK, width), F32)
        for head in range(heads):
            mask = head_mask(head, head_width, width)
            span = slice(head * head_width, (head + 1) * head_width)
            scores = product(query_rows * mask.astype(BF), key_t[...])
            scores = scores + bias[head, :, pl.ds(shift, tokens)]
            probs = jnp.exp(scores - logsum[pl.ds(first, BLOCK), head : head + 1])
            prob_grad = product(grad_rows * mask.astype(BF), value_t[...])
            middle = jnp.sum(probs * prob_grad, axis=-1, keepdims=True)
            score_grad = probs * (prob_grad - middle)
            low = score_grad.astype(BF)
            sums[head, :, pl.ds(shift, tokens)] += score_grad
            total = total + product(low, key[...]) * mask
            key_acc[span, :] += product(query_t[span, pl.ds(first, BLOCK)], low)
            value_acc[span, :] += product(grad_t[span, pl.ds(first, BLOCK)], probs.astype(BF))
        query_back[pl.ds(first, BLOCK), :] = total.astype(BF)
        return carry

    lax.fori_loop(0, blocks, step, 0)
    key_back = key_acc[...].T.astype(BF)
    value_back = value_acc[...].T.astype(BF)
    normed_part[...] = (
        cols_product(query_back[...], query_w[...])
        + cols_product(key_back, key_w[...])
        + cols_product(value_back, value_w[...])
    ).astype(BF)
    query_grad[...] = rows_product(normed[...], query_back[...]).astype(BF)
    key_grad[...] = rows_product(normed[...], key_back).astype(BF)
    value_grad[...] = rows_product(normed[...], value_back).astype(BF)

    padded = buckets.shape[1]
    lines = []
    for head in range(heads):
        wide = jnp.concatenate(
            [sums[head], jnp.zeros((BLOCK, padded - sums.shape[2]), F32)], axis=1
        )
        gathered = jnp.zeros((8, padded), F32)
        for part in range(BLOCK // 8):
            piece = wide[part * 8 : part * 8 + 8, :]
            gathered = gathered + pltpu.roll(piece, (BLOCK - 1 - part * 8) % padded, 1)
        line = jnp.zeros((1, padded), F32)
        for row in range(8):
            line = line + pltpu.roll(gathered, (padded - row) % padded, 1)[row : row + 1, :]
        lines.append(line)
    number = lax.broadcasted_iota(jnp.int32, (table.shape[0], padded), 0)
    hot = buckets[...] == number
    for head in range(heads):
        table_grad[:, head : head + 1] = jnp.sum(
            jnp.where(hot, lines[head], 0.0), axis=1, keepdims=True
        ).astype(BF)


def per_device(
    layer_in, expert_ids, rel_buckets, first_gain, query_weight, key_weight, value_weight,
    proj_weight, rel_table, second_gain, router_weight, expert_in, expert_out, cotangent,
):
    tokens, width = layer_in.shape
    heads = rel_table.shape[1]
    here = query_weight.shape[1]
    head_width = here // heads
    experts = router_weight.shape[1]
    capacity = 5 * tokens // (4 * experts)
    body = 16 * experts
    packed = 2 * width + width // 2
    padded = rel_buckets.shape[0] + 1
    span = 2 * tokens - BLOCK
    gain_one = first_gain[None, :]
    gain_two = second_gain[None, :]
    buckets = jnp.pad(rel_buckets, (0, 1), constant_values=-1)[None, :]
    proj_full = lax.all_gather(proj_weight, "tp", axis=0, tiled=True)

    mixed, normed, query, query_t, key, key_t, value_t, logsum = call(
        functools.partial(attend_body, head_width),
        "attend",
        [
            ((tokens, here), BF),
            ((tokens, width), BF),
            ((tokens, here), BF),
            ((here, tokens), BF),
            ((tokens, here), BF),
            ((here, tokens), BF),
            ((here, tokens), BF),
            ((tokens, 128), F32),
        ],
        [pltpu.VMEM((heads, BLOCK, span), F32), pltpu.VMEM((tokens, here), BF)],
        layer_in, gain_one, query_weight, key_weight, value_weight, buckets, rel_table,
    )
    mixed_full = lax.all_gather(mixed, "tp", axis=1, tiled=True)
    residual, hidden, probs, send_rows, send_grads, slots, gates = call(
        functools.partial(route_body, capacity),
        "route",
        [
            ((tokens, width), F32),
            ((tokens, width), BF),
            ((tokens, experts), F32),
            ((body, packed), BF),
            ((body, packed), BF),
            ((tokens, 1), jnp.int32),
            ((tokens, 1), F32),
        ],
        [],
        layer_in, mixed_full, proj_full, gain_two, router_weight, expert_ids,
        expert_ids.reshape(1, tokens), cotangent,
    )

    def exchange(array):
        split = array.reshape(experts, 16, array.shape[1])
        moved = lax.all_to_all(split, "exp", split_axis=0, concat_axis=0, tiled=True)
        return moved.reshape(array.shape)

    value, back, in_grad, out_grad = call(
        expert_body,
        "expert",
        [
            ((body, packed), BF),
            ((body, packed + 128), BF),
            ((width, expert_in.shape[2]), F32),
            ((expert_out.shape[1], width), F32),
        ],
        [pltpu.VMEM((body // 2, width), BF)] * 2 + [pltpu.VMEM((8, 128), F32)] * 3,
        exchange(send_rows), exchange(send_grads), expert_in[0], expert_out[0],
    )
    back_sum = exchange(lax.psum(back, "tp"))
    value_sum = exchange(lax.psum(value, "tp"))
    (
        output, router_grad, second_gain_grad, residual_grad, proj_grad, mixed_grad, mixed_grad_t
    ) = call(
        functools.partial(token_body, capacity),
        "token",
        [
            ((tokens, width), BF),
            ((width, experts), BF),
            ((1, width), BF),
            ((tokens, width), F32),
            ((here, width), BF),
            ((tokens, here), BF),
            ((here, tokens), BF),
        ],
        [],
        value_sum, back_sum, slots, gates, residual, hidden, probs, expert_ids, gain_two,
        router_weight, cotangent, mixed, proj_weight,
    )
    normed_part, query_grad, key_grad, value_grad, table_grad = call(
        functools.partial(attend_back_body, head_width),
        "attend_back",
        [
            ((tokens, width), BF),
            ((width, here), BF),
            ((width, here), BF),
            ((width, here), BF),
            ((rel_table.shape[0], heads), BF),
        ],
        [
            pltpu.VMEM((heads, BLOCK, span), F32),
            pltpu.VMEM((heads, BLOCK, span), F32),
            pltpu.VMEM((tokens, here), BF),
            pltpu.VMEM((here, tokens), F32),
            pltpu.VMEM((here, tokens), F32),
        ],
        normed, query, query_t, key, key_t, value_t, logsum, mixed_grad, mixed_grad_t,
        query_weight, key_weight, value_weight, buckets, rel_table,
    )
    normed_grad = lax.psum(normed_part, "tp").astype(F32)
    inputs = layer_in.astype(F32)
    scale = inverse_rms(inputs)
    first_gain_grad = jnp.sum(normed_grad * inputs * scale, axis=0)
    scaled = normed_grad * first_gain
    middle = jnp.mean(scaled * inputs, axis=-1, keepdims=True)
    input_grad = residual_grad + scale * scaled - inputs * (scale * scale * scale * middle)

    def over_batch(part):
        return lax.psum(part.astype(BF), "exp").astype(F32)

    return (
        output,
        input_grad,
        over_batch(first_gain_grad),
        over_batch(query_grad),
        over_batch(key_grad),
        over_batch(value_grad),
        over_batch(proj_grad),
        over_batch(table_grad),
        over_batch(second_gain_grad)[0],
        over_batch(router_grad),
        in_grad[None],
        out_grad[None],
    )


def solution(mesh):
    return jax.shard_map(
        per_device,
        mesh=mesh,
        in_specs=(
            P("exp", None),
            P("exp", None),
            P(),
            P(),
            P(None, "tp"),
            P(None, "tp"),
            P(None, "tp"),
            P("tp", None),
            P(None, "tp"),
            P(),
            P(),
            P("exp", None, "tp"),
            P("exp", "tp", None),
            P("exp", None),
        ),
        out_specs=(
            P("exp", None),
            P("exp", None),
            P(),
            P(None, "tp"),
            P(None, "tp"),
            P(None, "tp"),
            P("tp", None),
            P(None, "tp"),
            P(),
            P(),
            P("exp", None, "tp"),
            P("exp", "tp", None),
        ),
        check_vma=False,
    )
```

profile of v0, /device:TPU:1, one launch (start us, length us, event | category | flops | bytes accessed | tf_op | source)
XLA Modules:
  0.0 673.1 jit_solution(6149532350049706427)
XLA Ops:
  7.2 1.1 copy.43.query_w
  8.4 1.1 copy.44.key_w
  9.5 1.1 copy.45.value_w
  10.6 0.8 copy.46.table
  11.4 0.7 broadcast_in_dim.18.gain
  12.1 13.6 %attend.1 = (bf16[1024,192]{1,0:T(8,128)(2,1)S(1)}, bf16[1024,768]{1,0:T(8,128)(2,1)S(1)}, bf16[1024,192]{1,0:T(8,128)(2,1)S(1)}, bf16[192,1024]{1,0:T(8,128)(2,...) custom-call(bf16[1024,768]{1,0:T(8,128)(2,1)} %rows.3, ...), custom_call_target="tpu_custom_call" | custom-call | tf_op jit(solution)/shard_map/attend/pallas_call | solution.py:37
  25.8 1.1 copy-done.1
  26.9 0.7 copy-done.16
  27.7 0.7 copy-done.18
  28.4 0.7 copy-done.20
  29.2 0.9 copy.47
  30.2 0.7 all-gather.5.cloned.1.call-update
  30.9 0.2 copy.50.ids
  31.2 0.2 copy.49.router_w
  31.4 28.6 %all-gather.3.cloned.1.call-done = bf16[1024,768]{0,1:T(8,128)(2,1)} async-done(((bf16[1024,192]{0,1:T(8,128)(2,1)}), bf16[1024,768]{0,1:T(8,128)(2,1)}) %all-gather.3.cloned.1.call-update) | async-done | bytes 1572880 | tf_op jit(solution)/shard_map/all_gather | solution.py:384
  60.0 2.6 copy.48.mixed
  62.6 22.6 %all-gather.5.cloned.1.call-done.proj = bf16[768,768]{1,0:T(8,128)(2,1)} async-done(((bf16[192,768]{1,0:T(8,128)(2,1)}), bf16[768,768]{1,0:T(8,128)(2,1)}) %all-gather.5.cloned.1.call-update) | async-done | bytes 1179664 | tf_op jit(solution)/shard_map/all_gather | solution.py:366
  85.2 1.3 copy-done.7
  86.4 11.6 %route.1 = (f32[1024,768]{1,0:T(8,128)}, bf16[1024,768]{1,0:T(8,128)(2,1)S(1)}, f32[1024,32]{1,0:T(8,128)S(1)}, bf16[512,1920]{1,0:T(8,128)(2,1)}, bf16[512,1920...) custom-call(bf16[1024,768]{1,0:T(8,128)(2,1)} %rows.3, bf16[1024,768]{1,0:T(8,128)(2,1)} %copy.48.mixed, ...), custom_call_target="tpu_custom_call" | custom-call | tf_op jit(solution)/shard_map/route/pallas_call | solution.py:37
  98.1 0.8 copy-done.10
  98.9 0.8 copy-done.12
  99.7 0.8 copy-done.14
  100.5 36.0 %all_to_all.20 = bf16[32,16,1920]{2,1,0:T(8,128)(2,1)} all-to-all(bf16[32,16,1920]{2,1,0:T(8,128)(2,1)} %bitcast.26), channel_id=1, replica_groups=mesh['exp'=32,'tp'=4] {'exp'}, dimensions={0} | all-to-all | bytes 3932160 | tf_op jit(solution)/shard_map/all_to_all | solution.py:404
  136.5 31.2 %all_to_all.21 = bf16[32,16,1920]{2,1,0:T(8,128)(2,1)} all-to-all(bf16[32,16,1920]{2,1,0:T(8,128)(2,1)S(1)} %bitcast.25), channel_id=1, replica_groups=mesh['exp'=32,'tp'=4] {'exp'}, dimensions={0} | all-to-all | bytes 3932160 | tf_op jit(solution)/shard_map/all_to_all | solution.py:404
  167.7 14.9 %expert.1 = (bf16[512,1920]{1,0:T(8,128)(2,1)S(1)}, bf16[512,2048]{1,0:T(8,128)(2,1)}, f32[768,768]{1,0:T(8,128)}, f32[768,768]{1,0:T(8,128)}) custom-call(bf16[512,1920]{1,0:T(8,128)(2,1)} %bitcast.22, bf16[512,1920]{1,0:T(8,128)(2,1)} %bitcast.23, bf16[768,768]{1,0:T(8,128)(2,1)S(1)} %bitcast.15, bf16[768,768]{1,0:T(8,128)(2,1)S(1)} %bitcast.16), custom_call_target="tpu_custom_call" | custom-call | tf_op jit(solution)/shard_map/expert/pallas_call | solution.py:37
  182.6 1.3 copy-done
  184.0 87.5 %all-reduce.12.cloned.1.call-done = (bf16[32,16,1920]{2,1,0:T(8,128)(2,1)}, bf16[32,16,2048]{2,1,0:T(8,128)(2,1)}) async-done(((bf16[32,16,1920]{2,1,0:T(8,128)(2,1)}, bf16[32,16,2048]{2,1,0:T(8,128)(2,1)}), (bf16[32,16,1920]{2,1,0:T(8,128)(2,1)}, bf16[32,16,2048]{2,1,0:T(8,128)(2,1)})) %all-reduce.12.cloned.1.call-update) | async-done | bytes 4063248 | tf_op jit(solution)/shard_map/psum | solution.py:420
  271.5 34.9 %all_to_all.22 = bf16[32,16,1920]{2,1,0:T(8,128)(2,1)} all-to-all(bf16[32,16,1920]{2,1,0:T(8,128)(2,1)} %get-tuple-element.108), channel_id=1, replica_groups=mesh['exp'=32,'tp'=4] {'exp'}, dimensions={0} | all-to-all | bytes 3932160 | tf_op jit(solution)/shard_map/all_to_all | solution.py:404
  306.5 32.8 %all_to_all.23 = bf16[32,16,2048]{2,1,0:T(8,128)(2,1)} all-to-all(bf16[32,16,2048]{2,1,0:T(8,128)(2,1)S(1)} %copy-done.26), channel_id=1, replica_groups=mesh['exp'=32,'tp'=4] {'exp'}, dimensions={0} | all-to-all | bytes 4194304 | tf_op jit(solution)/shard_map/all_to_all | solution.py:404
  339.3 13.6 %token_.1 = (bf16[1024,768]{1,0:T(8,128)(2,1)}, bf16[768,32]{1,0:T(8,128)(2,1)S(1)}, bf16[1,768]{1,0:T(2,128)(2,1)S(1)}, f32[1024,768]{1,0:T(8,128)}, bf16[192,7...) custom-call(bf16[512,1920]{1,0:T(8,128)(2,1)} %bitcast.21, ...), custom_call_target="tpu_custom_call" | custom-call | tf_op jit(solution)/shard_map/token/pallas_call | solution.py:37
  352.9 0.7 copy-done.22
  353.6 21.9 %attend_back.1 = (bf16[1024,768]{1,0:T(8,128)(2,1)}, bf16[768,192]{1,0:T(8,128)(2,1)}, bf16[768,192]{1,0:T(8,128)(2,1)}, bf16[768,192]{1,0:T(8,128)(2,1)}, bf16[32,3]{1,0:T(8,128)(2,1)S(1)}) custom-call(bf16[1024,768]{1,0:T(8,128)(2,1)} %copy-done.1, bf16[1024,192]{1,0:T(8,128)(2,1)S(1)} %get-tuple-element.56.query, bf16[192,1024]{1,0:T(8,128)(2,1)S(1)} %copy-done.17, ...), custom_call_target="tpu_custom_call" | custom-call | tf_op jit(solution)/shard_map/attend_back/pallas_call | solution.py:37
  375.6 0.5 all-reduce.8.cloned.1.call-update
  376.2 0.8 copy-done.25
  376.9 0.4 fusion.3
  377.4 101.0 %all-reduce.10.cloned.1.call-done = (bf16[768,192]{1,0:T(8,128)(2,1)}, bf16[768,192]{1,0:T(8,128)(2,1)}, bf16[768,192]{1,0:T(8,128)(2,1)}, bf16[192,768]{1,0:T(8,128)(2,1)}) async-done(((bf16[768,192]{1,0:T(8,128)(2,1)}, bf16[768,192]{1,0:T(8,128)(2,1)}, bf16[768,192]{1,0:T(8,128)(2,1)}, bf16[192,768]{1,0:T(8,128)(2,1)}), (bf16[768,192]{1,0:T(8,128)(2,1)}, bf16[768,192]{1,0:T(8,128)(2,1)}, ...) | async-done | bytes 1179664 | tf_op jit(solution)/shard_map/psum | solution.py:468
  478.4 1.9 convert_element_type.38
  480.2 2.0 copy.57
  482.2 1.0 copy.58
  483.2 1.0 copy.59
  484.2 46.9 %all-reduce.8.cloned.1.call-done = bf16[1024,768]{1,0:T(8,128)(2,1)} async-done(((bf16[1024,768]{1,0:T(8,128)(2,1)}), bf16[1024,768]{1,0:T(8,128)(2,1)}) %all-reduce.8.cloned.1.call-update) | async-done | bytes 1572880 | tf_op jit(solution)/shard_map/psum | solution.py:459
  531.1 2.8 fusion.6
  533.9 124.9 %all-reduce.1 = (bf16[32,3]{1,0:T(8,128)(2,1)S(1)}, bf16[768,32]{1,0:T(8,128)(2,1)S(1)}, bf16[768]{0:T(1024)(128)(2,1)S(1)}, bf16[768]{0:T(1024)(128)(2,1)S(1)}) all-reduce(bf16[32,3]{1,0:T(8,128)(2,1)S(1)} %get-tuple-element.69, bf16[768,32]{1,0:T(8,128)(2,1)S(1)} %copy-done.23, ...), channel_id=1, replica_groups=mesh['exp'=32,'tp'=4] {'exp'}, use_global_device_ids=true, to_apply=%region_11.12 | all-reduce | flops 26208 | bytes 104832 | tf_op jit(solution)/shard_map/psum | solution.py:468
  658.8 0.8 copy.61
  659.5 0.6 convert_element_type.34
  660.1 0.6 squeeze.15
  660.7 0.7 copy.60
  661.4 4.8 fusion.2
  (70 shorter events, 0.4 us)
Async XLA Ops:
  7.2 4.9 copy-start.32
  7.2 52.8 %all-gather.3.cloned.1.call-start = ((), (), s32[]{:S(2)}) async-start(), calls=%async_computation.4 | async-start | bytes 1966080 | tf_op jit(solution)/shard_map/all_gather | solution.py:384
  12.1 18.8 %copy-start.24 = (s32[1024,1]{0,1:T(1,128)S(1)}, s32[1024,1]{0,1:T(1,128)}, u32[]{:S(2)}) copy-start(s32[1024,1]{0,1:T(1,128)} %param.15) | copy-start | bytes 12292
  12.1 19.1 %copy-start.30 = (bf16[768,32]{0,1:T(8,128)(2,1)S(1)}, bf16[768,32]{0,1:T(8,128)(2,1)}, u32[]{:S(2)}) copy-start(bf16[768,32]{0,1:T(8,128)(2,1)} %param.24) | copy-start | bytes 147460
  12.1 19.2 %copy-start.33 = (f32[768]{0:T(1024)S(1)}, f32[768]{0:T(1024)}, u32[]{:S(2)}) copy-start(f32[768]{0:T(1024)} %param.23) | copy-start | bytes 9220
  25.8 1.1 copy-start.1
  26.9 0.7 copy-start.16
  27.7 0.7 copy-start.18
  28.4 0.7 copy-start.20
  29.2 1.7 copy-start.8
  30.1 55.0 %all-gather.5.cloned.1.call-start = ((), (), s32[]{:S(2)}) async-start(), calls=%async_computation.5 | async-start | bytes 1474560 | tf_op jit(solution)/shard_map/all_gather | solution.py:366
  30.9 240.6 %all-reduce.12.cloned.1.call-start = ((), (), s32[]{:S(2)}) async-start(), calls=%async_computation.8 | async-start | bytes 8126464 | tf_op jit(solution)/shard_map/psum | solution.py:420
  85.2 1.3 copy-start.7
  98.1 0.8 copy-start.10
  98.9 0.8 copy-start.12
  99.7 0.8 copy-start.14
  100.5 67.2 %copy-start.2 = (bf16[1024,768]{1,0:T(8,128)(2,1)}, bf16[1024,768]{1,0:T(8,128)(2,1)S(1)}, u32[]{:S(2)}) copy-start(bf16[1024,768]{1,0:T(8,128)(2,1)S(1)} %get-tuple-element.51.hidden) | copy-start | bytes 4718596
  100.5 36.0 %copy-start.27 = (bf16[512,1920]{1,0:T(8,128)(2,1)S(1)}, bf16[512,1920]{1,0:T(8,128)(2,1)}, u32[]{:S(2)}) copy-start(bf16[512,1920]{1,0:T(8,128)(2,1)} %get-tuple-element.45) | copy-start | bytes 5898244
  136.5 31.2 %copy-start.5 = (bf16[1,768,768]{2,1,0:T(8,128)(2,1)S(1)}, bf16[1,768,768]{2,1,0:T(8,128)(2,1)}, u32[]{:S(2)}) copy-start(bf16[1,768,768]{2,1,0:T(8,128)(2,1)} %param.25) | copy-start | bytes 3538948
  136.5 31.2 %copy-start.6 = (bf16[1,768,768]{2,1,0:T(8,128)(2,1)S(1)}, bf16[1,768,768]{2,1,0:T(8,128)(2,1)}, u32[]{:S(2)}) copy-start(bf16[1,768,768]{2,1,0:T(8,128)(2,1)} %param.26) | copy-start | bytes 3538948
  182.6 1.3 copy-start
  183.9 294.4 %all-reduce.10.cloned.1.call-start = ((), (), s32[]{:S(2)}) async-start(), calls=%async_computation.7 | async-start | bytes 2949120 | tf_op jit(solution)/shard_map/psum | solution.py:468
  271.5 35.0 %copy-start.26 = (bf16[32,16,2048]{2,1,0:T(8,128)(2,1)S(1)}, bf16[32,16,2048]{2,1,0:T(8,128)(2,1)}, u32[]{:S(2)}) copy-start(bf16[32,16,2048]{2,1,0:T(8,128)(2,1)} %get-tuple-element.109) | copy-start | bytes 6291460
  306.4 32.8 %copy-start.3 = (bf16[1024,768]{1,0:T(8,128)(2,1)S(1)}, bf16[1024,768]{1,0:T(8,128)(2,1)}, u32[]{:S(2)}) copy-start(bf16[1024,768]{1,0:T(8,128)(2,1)} %copy-done.2) | copy-start | bytes 4718596
  306.4 32.8 %copy-start.4 = (bf16[192,768]{1,0:T(8,128)(2,1)S(1)}, bf16[192,768]{1,0:T(8,128)(2,1)}, u32[]{:S(2)}) copy-start(bf16[192,768]{1,0:T(8,128)(2,1)} %proj.1) | copy-start | bytes 884740
  306.4 32.8 %copy-start.11 = (f32[1024,32]{1,0:T(8,128)S(1)}, f32[1024,32]{1,0:T(8,128)}, u32[]{:S(2)}) copy-start(f32[1024,32]{1,0:T(8,128)} %copy-done.10) | copy-start | bytes 393220
  306.4 32.8 %copy-start.13 = (s32[1024,1]{1,0:T(8,128)S(1)}, s32[1024,1]{1,0:T(8,128)}, u32[]{:S(2)}) copy-start(s32[1024,1]{1,0:T(8,128)} %copy-done.12) | copy-start | bytes 12292
  306.4 32.8 %copy-start.15 = (f32[1024,1]{1,0:T(8,128)S(1)}, f32[1024,1]{1,0:T(8,128)}, u32[]{:S(2)}) copy-start(f32[1024,1]{1,0:T(8,128)} %copy-done.14) | copy-start | bytes 12292
  339.2 14.4 %copy-start.9 = (f32[1024,128]{1,0:T(8,128)S(1)}, f32[1024,128]{1,0:T(8,128)}, u32[]{:S(2)}) copy-start(f32[1024,128]{1,0:T(8,128)} %copy-done.8) | copy-start | bytes 1572868
  339.3 14.3 %copy-start.17 = (bf16[192,1024]{1,0:T(8,128)(2,1)S(1)}, bf16[192,1024]{1,0:T(8,128)(2,1)}, u32[]{:S(2)}) copy-start(bf16[192,1024]{1,0:T(8,128)(2,1)} %copy-done.16) | copy-start | bytes 1179652
  339.3 14.3 %copy-start.19 = (bf16[192,1024]{1,0:T(8,128)(2,1)S(1)}, bf16[192,1024]{1,0:T(8,128)(2,1)}, u32[]{:S(2)}) copy-start(bf16[192,1024]{1,0:T(8,128)(2,1)} %copy-done.18) | copy-start | bytes 1179652
  339.3 14.3 %copy-start.21 = (bf16[192,1024]{1,0:T(8,128)(2,1)S(1)}, bf16[192,1024]{1,0:T(8,128)(2,1)}, u32[]{:S(2)}) copy-start(bf16[192,1024]{1,0:T(8,128)(2,1)} %copy-done.20) | copy-start | bytes 1179652
  352.9 0.7 copy-start.22
  375.5 1.4 copy-start.25
  375.6 155.5 %all-reduce.8.cloned.1.call-start = ((), (), s32[]{:S(2)}) async-start(), calls=%async_computation.6 | async-start | bytes 3145728 | tf_op jit(solution)/shard_map/psum | solution.py:459
  377.3 153.8 %copy-start.31 = (f32[768]{0:T(1024)S(1)}, f32[768]{0:T(1024)}, u32[]{:S(2)}) copy-start(f32[768]{0:T(1024)} %param.17) | copy-start | bytes 9220
  478.4 3.9 copy-start.29
  478.4 4.8 copy-start.28
  483.2 50.7 %copy-start.23 = (bf16[768,32]{1,0:T(8,128)(2,1)S(1)}, bf16[768,32]{1,0:T(8,128)(2,1)}, u32[]{:S(2)}) copy-start(bf16[768,32]{1,0:T(8,128)(2,1)} %copy-done.22) | copy-start | bytes 147460
Sparse Core Ops, SparseCore 0:
  30.2 29.6 all-gather.2
  61.6 23.4 all-gather.4
  184.1 87.3 all-reduce.11
  375.7 102.6 all-reduce.9
  481.3 49.7 all-reduce.7
where the time goes:
time: 686 us; the launch traced here: 673 us
  waiting for transfers between devices  288 us (42%)
  blocking collectives  260 us (38%)
  Pallas kernels  75.7 us (11%)
  local copies, waits for them, and re-layouts  24 us (3%)
  between operations  14.5 us (2%)
  other arithmetic  11 us (2%)
    all_to_all x4, blocking collectives, exchange(): lax.all_to_all(split, 'exp', split_axis=0, concat_axis=0, tiled=True)  135 us
    psum x1, blocking collectives, over_batch(): return lax.psum(part.astype(BF), 'exp').astype(F32)  125 us
    psum x1, waiting for transfers between devices, over_batch(): return lax.psum(part.astype(BF), 'exp').astype(F32)  101 us
    psum x1, waiting for transfers between devices, per_device(): value_sum = exchange(lax.psum(value, 'tp'))  87.5 us
    pallas_call x5, Pallas kernels, call(): pl.pallas_call(body, name=name, out_shape=[jax.ShapeDtypeStruct(shape, dt...  75.7 us
    psum x1, waiting for transfers between devices, per_device(): normed_grad = lax.psum(normed_part, 'tp').astype(F32)  46.9 us
    all_gather x1, waiting for transfers between devices, per_device(): mixed_full = lax.all_gather(mixed, 'tp', axis=1, tiled=True)  28.6 us
    all_gather x1, waiting for transfers between devices, per_device(): proj_full = lax.all_gather(proj_weight, 'tp', axis=0, tiled=True)  22.6 us
  transfers between devices with their start and end apart: 5, of which 5 were waited for; matrix products, arithmetic and copies ran while one was open for 1% of the time, Pallas kernels for 0%

commit v1 on v0

v1 whole, which is shorter than its diff:
```python
import functools

import jax
import jax.numpy as jnp
from jax import lax
from jax.experimental import pallas as pl
from jax.experimental.pallas import tpu as pltpu
from jax.sharding import PartitionSpec as P

epsilon = 1e-06
gelu_root = 0.7978845608028654
gelu_cube = 0.044715
BF = jnp.bfloat16
F32 = jnp.float32
BLOCK = 128
MIB = 1024 * 1024
GROUPS = 4
MESH = pl.DeviceIdType.MESH


def product(left, right):
    return jnp.dot(left, right, preferred_element_type=F32)


def rows_product(left, right):
    return lax.dot_general(left, right, (((0,), (0,)), ((), ())), preferred_element_type=F32)


def cols_product(left, right):
    return lax.dot_general(left, right, (((1,), (1,)), ((), ())), preferred_element_type=F32)


def inverse_rms(values):
    return lax.rsqrt(jnp.mean(values * values, axis=-1, keepdims=True) + epsilon)


def call(body, name, outs, scratch, *operands, mib=48, number=None):
    vmem = pl.BlockSpec(memory_space=pltpu.VMEM)
    extra = {} if number is None else {"collective_id": number, "has_side_effects": True}
    return pl.pallas_call(
        body,
        name=name,
        out_shape=[jax.ShapeDtypeStruct(shape, dtype) for shape, dtype in outs],
        in_specs=[vmem] * len(operands),
        out_specs=[vmem] * len(outs),
        scratch_shapes=scratch,
        compiler_params=pltpu.CompilerParams(vmem_limit_bytes=mib * MIB, **extra),
    )(*operands)


def remote(source, target, send, receive, **where):
    return pltpu.make_async_remote_copy(
        src_ref=source,
        dst_ref=target,
        send_sem=send,
        recv_sem=receive,
        device_id=where,
        device_id_type=MESH,
    )


def ring(ring_size):
    here = lax.axis_index("tp")
    return here, lax.rem(here + 1, ring_size), lax.rem(here + ring_size - 1, ring_size)


def greet(ring_size, batch_size, opposite=False):
    barrier = pltpu.get_barrier_semaphore()
    here, right, left = ring(ring_size)
    for side in (right, left):
        pl.semaphore_signal(barrier, inc=1, device_id={"tp": side}, device_id_type=MESH)
    if opposite:
        side = lax.rem(here + 2, ring_size)
        pl.semaphore_signal(barrier, inc=1, device_id={"tp": side}, device_id_type=MESH)
    if batch_size:
        me = lax.axis_index("exp")

        def hello(step, carry):
            peer = lax.rem(me + step, batch_size)
            pl.semaphore_signal(barrier, inc=1, device_id={"exp": peer}, device_id_type=MESH)
            return carry

        lax.fori_loop(1, batch_size, hello, 0)
    return 2 + int(opposite) + max(batch_size - 1, 0)


def meet(signals):
    pl.semaphore_wait(pltpu.get_barrier_semaphore(), signals)


class Gather:
    def __init__(self, region, half, sems):
        self.region, self.half, self.sems = region, half, sems
        self.here, self.right, self.left = ring(4)
        self.far = lax.rem(self.here + 2, 4)

    def first(self, k):
        own = self.region(k, self.here)
        return (
            remote(own, own, self.sems.at[k, 0], self.sems.at[k, 1], tp=self.right),
            remote(own, own, self.sems.at[k, 2], self.sems.at[k, 3], tp=self.left),
        )

    def second(self, k):
        low, high = self.half(k, self.left, 0), self.half(k, self.right, 1)
        return (
            remote(low, low, self.sems.at[k, 4], self.sems.at[k, 5], tp=self.right),
            remote(high, high, self.sems.at[k, 6], self.sems.at[k, 7], tp=self.left),
        )

    def start(self, k):
        for copy in self.first(k):
            copy.start()

    def forward(self, k):
        for side, copy, arrived in zip(
            (self.left, self.right), self.second(k), (1, 3), strict=True
        ):
            whole = self.region(k, side)
            remote(whole, whole, self.sems.at[k, 0], self.sems.at[k, arrived], tp=self.right).wait_recv()
            copy.start()

    def finish(self, k):
        for half, sent, arrived in ((0, 4, 5), (1, 6, 7)):
            part = self.half(k, self.far, half)
            remote(part, part, self.sems.at[k, sent], self.sems.at[k, arrived], tp=self.right).wait_recv()

    def drain(self, k):
        for copy in self.first(k) + self.second(k):
            copy.wait_send()


class Reduce:
    def __init__(self, piece, in_left, in_right, out_right, out_left, mid_left, mid_right, sems):
        self.piece, self.sems = piece, sems
        self.in_left, self.in_right = in_left, in_right
        self.out_right, self.out_left = out_right, out_left
        self.mid_left, self.mid_right = mid_left, mid_right
        self.here, self.right, self.left = ring(4)
        self.far = lax.rem(self.here + 2, 4)

    def first(self, k):
        return (
            remote(self.piece(k, self.far, 0), self.in_left.at[k], self.sems.at[k, 0], self.sems.at[k, 1], tp=self.right),
            remote(self.piece(k, self.far, 1), self.in_right.at[k], self.sems.at[k, 2], self.sems.at[k, 3], tp=self.left),
        )

    def second(self, k):
        return (
            remote(self.out_right.at[k], self.mid_left.at[k], self.sems.at[k, 4], self.sems.at[k, 5], tp=self.right),
            remote(self.out_left.at[k], self.mid_right.at[k], self.sems.at[k, 6], self.sems.at[k, 7], tp=self.left),
        )

    def start(self, k):
        for copy in self.first(k):
            copy.start()

    def middle(self, k):
        by_left, by_right = self.first(k)
        to_right, to_left = self.second(k)
        by_left.wait_recv()
        summed = self.piece(k, self.right, 0)[...].astype(F32) + self.in_left[k].astype(F32)
        self.out_right[k, 0] = summed.astype(BF)
        self.out_right[k, 1] = self.piece(k, self.right, 1)[...]
        to_right.start()
        by_right.wait_recv()
        summed = self.piece(k, self.left, 1)[...].astype(F32) + self.in_right[k].astype(F32)
        self.out_left[k, 1] = summed.astype(BF)
        self.out_left[k, 0] = self.piece(k, self.left, 0)[...]
        to_left.start()

    def finish(self, k):
        for copy in self.second(k):
            copy.wait_recv()
        return [
            self.piece(k, self.here, half)[...].astype(F32)
            + self.mid_left[k, half].astype(F32)
            + self.mid_right[k, half].astype(F32)
            for half in (0, 1)
        ]

    def drain(self, k):
        for copy in self.first(k) + self.second(k):
            copy.wait_send()


def reduce_scratch(groups, rows, lanes):
    return [pltpu.VMEM((groups, rows, lanes), BF)] * 2 + [
        pltpu.VMEM((groups, 2, rows, lanes), BF)
    ] * 4


def sems(*dims):
    return pltpu.SemaphoreType.DMA(dims)


def dispatch_body(batch_size, lanes, source, out, send, arrive, ring_sems):
    signals = greet(4, batch_size)
    me = lax.axis_index("exp")
    here = lax.axis_index("tp")
    part = batch_size // GROUPS
    mine = pl.ds(pl.multiple_of(here * lanes, 128), lanes)
    tail = pl.ds(4 * lanes, lanes)
    own = pl.ds(pl.multiple_of(me * 16, 16), 16)
    out[:, own, mine] = source[:, own, mine]
    out[:, own, tail] = source[:, own, tail]
    meet(signals)

    def arriving(k):
        return lax.rem(me // part + GROUPS - k, GROUPS) * (part * 16)

    def span(k, who, begin, rows, array=slice(None)):
        spot = pl.ds(pl.multiple_of(arriving(k) + begin, 16), rows)
        return out.at[array, spot, pl.ds(pl.multiple_of(who * lanes, 128), lanes)]

    gather = Gather(
        lambda k, who: span(k, who, 0, part * 16),
        lambda k, who, half: span(k, who, 0, part * 16, pl.ds(half, 1)),
        ring_sems,
    )

    def scatter(columns, send_sem, sem_of):
        for k in range(GROUPS):

            def step(j, carry):
                peer = lax.rem(me // part + k, GROUPS) * part + lax.rem(me + j, part)
                rows = pl.ds(pl.multiple_of(peer * 16, 16), 16)
                remote(source.at[:, rows, columns], out.at[:, own, columns], send_sem, sem_of(k), exp=peer).start()
                return carry

            lax.fori_loop(1 if k == 0 else 0, part, step, 0)

    scatter(mine, send.at[0], lambda k: arrive.at[k])
    scatter(tail, send.at[1], lambda k: arrive.at[GROUPS])
    for k in range(GROUPS):
        rows = (part - 1 if k == 0 else part) * 16
        block = span(k, here, 0, rows)
        remote(block, block, send.at[0], arrive.at[k], exp=me).wait_recv()
        gather.start(k)
        if k:
            gather.forward(k - 1)
    gather.forward(GROUPS - 1)
    whole = out.at[:, pl.ds(0, (batch_size - 1) * 16), tail]
    remote(whole, whole, send.at[1], arrive.at[GROUPS], exp=me).wait_recv()
    for k in range(GROUPS):
        gather.finish(k)
    remote(whole, whole, send.at[0], arrive.at[0], exp=me).wait_send()
    remote(whole, whole, send.at[1], arrive.at[0], exp=me).wait_send()
    for k in range(GROUPS):
        gather.drain(k)


def return_parts(batch_size, lanes, source, out, stage, buffers, send, arrive, sum_sems, ring_sems):
    me = lax.axis_index("exp")
    here = lax.axis_index("tp")
    part = batch_size // GROUPS
    mine = pl.ds(pl.multiple_of(here * lanes, 128), lanes)
    own = pl.ds(pl.multiple_of(me * 16, 16), 16)

    def leaving(k):
        return lax.rem(me // part + k, GROUPS) * (part * 16)

    def arriving(k):
        return lax.rem(me // part + GROUPS - k, GROUPS) * (part * 16)

    def span(ref, base, who, begin, rows):
        spot = pl.ds(pl.multiple_of(base + begin, 16), rows)
        return ref.at[spot, pl.ds(pl.multiple_of(who * lanes, 128), lanes)]

    half_rows = part * 8
    reduce = Reduce(
        lambda k, who, half: span(source, leaving(k), who, half * half_rows, half_rows),
        *buffers,
        sum_sems,
    )
    gather = Gather(
        lambda k, who: span(out, arriving(k), who, 0, part * 16),
        lambda k, who, half: span(out, arriving(k), who, half * half_rows, half_rows),
        ring_sems,
    )

    def scatter(k):
        first, second = reduce.finish(k)
        spot = pl.multiple_of(leaving(k), 16)
        stage[pl.ds(spot, half_rows), :] = first.astype(BF)
        stage[pl.ds(pl.multiple_of(spot + half_rows, 16), half_rows), :] = second.astype(BF)
        if k == 0:
            out[own, mine] = stage[own, :]

        def step(j, carry):
            peer = lax.rem(me // part + k, GROUPS) * part + lax.rem(me + j, part)
            rows = pl.ds(pl.multiple_of(peer * 16, 16), 16)
            remote(stage.at[rows, :], out.at[own, mine], send.at[0], arrive.at[k], exp=peer).start()
            return carry

        lax.fori_loop(1 if k == 0 else 0, part, step, 0)

    def collect(k):
        rows = (part - 1 if k == 0 else part) * 16
        block = span(out, arriving(k), here, 0, rows)
        remote(block, block, send.at[0], arrive.at[k], exp=me).wait_recv()
        gather.start(k)

    def drain():
        whole = stage.at[pl.ds(0, (batch_size - 1) * 16), :]
        remote(whole, whole, send.at[0], arrive.at[0], exp=me).wait_send()
        for k in range(GROUPS):
            reduce.drain(k)
            gather.drain(k)

    return reduce, gather, scatter, collect, drain


def return_body(batch_size, lanes, source, out, stage, *rest):
    buffers, (send, arrive, sum_sems, ring_sems) = rest[:6], rest[6:]
    signals = greet(4, batch_size)
    reduce, gather, scatter, collect, drain = return_parts(
        batch_size, lanes, source, out, stage, buffers, send, arrive, sum_sems, ring_sems
    )
    meet(signals)
    for k in range(GROUPS):
        reduce.start(k)
    for k in range(GROUPS):
        reduce.middle(k)
        if k:
            scatter(k - 1)
    scatter(GROUPS - 1)
    for k in range(GROUPS):
        collect(k)
        if k:
            gather.forward(k - 1)
    gather.forward(GROUPS - 1)
    for k in range(GROUPS):
        gather.finish(k)
    drain()


def return_scratch(batch_size, lanes):
    return [
        pltpu.VMEM((batch_size * 16, lanes), BF),
        *reduce_scratch(GROUPS, batch_size * 8 // GROUPS, lanes),
        sems(1),
        sems(GROUPS),
        sems(GROUPS, 8),
        sems(GROUPS, 8),
    ]


def final_body(
    batch_size, part_in, large, small, residual_grad, rows, gain,
    input_grad, query_grad, key_grad, value_grad, proj_grad, router_grad, gain_grad, first_grad,
    table_grad,
    summed, large_in, small_in, large_out, small_out, lines, *rest,
):
    buffers, (send, arrive, line_sems, sum_sems, ring_sems) = rest[:6], rest[6:]
    signals = greet(4, batch_size, opposite=True)
    me = lax.axis_index("exp")
    here, right, left = ring(4)
    tokens, width = part_in.shape
    chunk = tokens // 4
    groups = buffers[0].shape[0]
    half_rows = chunk // groups // 2
    tall, wide = large_in.shape[1:]
    across = width // wide
    small_across = small.shape[1] // 128

    def spot(ref, who, k, begin, count):
        first = who * chunk + k * (2 * half_rows) + begin
        return ref.at[pl.ds(pl.multiple_of(first, 16), count), :]

    reduce = Reduce(
        lambda k, who, half: spot(part_in, who, k, half * half_rows, half_rows), *buffers, sum_sems
    )
    gather = Gather(
        lambda k, who: spot(summed, who, k, 0, 2 * half_rows),
        lambda k, who, half: spot(summed, who, k, half * half_rows, half_rows),
        ring_sems,
    )

    def large_part(ref, who):
        down = pl.ds(pl.multiple_of(who // across * tall, 16), tall)
        return ref.at[down, pl.ds(pl.multiple_of(lax.rem(who, across) * wide, 128), wide)]

    def small_part(ref, who):
        down = pl.ds(pl.multiple_of(who // small_across * 16, 16), 16)
        return ref.at[down, pl.ds(pl.multiple_of(lax.rem(who, small_across) * 128, 128), 128)]

    meet(signals)
    for k in range(groups):
        reduce.start(k)

    def scatter(step, carry):
        peer = lax.rem(me + step, batch_size)
        remote(large_part(large, peer), large_in.at[step], send.at[0], arrive.at[0], exp=peer).start()
        remote(small_part(small, peer), small_in.at[step], send.at[1], arrive.at[1], exp=peer).start()
        return carry

    lax.fori_loop(1, batch_size, scatter, 0)
    large_in[0] = large_part(large, me)[...]
    small_in[0] = small_part(small, me)[...]
    for k in range(groups):
        reduce.middle(k)
    for k in range(groups):
        pieces = reduce.finish(k)
        for half in (0, 1):
            target = spot(summed, here, k, half * half_rows, half_rows)
            target[...] = pieces[half].astype(BF)
        gather.start(k)
    large_rest = large_in.at[pl.ds(1, batch_size - 1)]
    small_rest = small_in.at[pl.ds(1, batch_size - 1)]
    remote(large_rest, large_rest, send.at[0], arrive.at[0], exp=me).wait_recv()
    remote(small_rest, small_rest, send.at[1], arrive.at[1], exp=me).wait_recv()

    def add(step, carry):
        return carry[0] + large_in[step].astype(F32), carry[1] + small_in[step].astype(F32)

    zero = (jnp.zeros((tall, wide), F32), jnp.zeros((16, 128), F32))
    large_sum, small_sum = lax.fori_loop(0, batch_size, add, zero)
    large_part(large_out, me)[...] = large_sum.astype(BF)
    small_part(small_out, me)[...] = small_sum.astype(BF)

    def spread(step, carry):
        peer = lax.rem(me + step, batch_size)
        own = large_part(large_out, me)
        remote(own, own, send.at[2], arrive.at[2], exp=peer).start()
        own = small_part(small_out, me)
        remote(own, own, send.at[3], arrive.at[3], exp=peer).start()
        return carry

    lax.fori_loop(1, batch_size, spread, 0)
    for k in range(groups):
        gather.forward(k)
    for k in range(groups):
        gather.finish(k)
    inputs = rows[...].astype(F32)
    scale = inverse_rms(inputs)
    scaled = summed[...].astype(F32) * gain[...]
    middle = jnp.mean(scaled * inputs, axis=-1, keepdims=True)
    input_grad[...] = (
        residual_grad[...] + scale * scaled - inputs * (scale * scale * scale * middle)
    )
    remote(large_rest, large_rest, send.at[2], arrive.at[2], exp=me).wait_recv()
    remote(small_rest, small_rest, send.at[3], arrive.at[3], exp=me).wait_recv()
    line = small_out.at[pl.ds(32, 16), pl.ds(0, width)]
    others = (right, left, lax.rem(here + 2, 4))
    copies = [
        remote(line, lines.at[i], line_sems.at[i, 0], line_sems.at[i, 1], tp=side)
        for i, side in enumerate(others)
    ]
    for copy in copies:
        copy.start()
    high = query_grad.shape[0]
    for i, ref in enumerate((query_grad, key_grad, value_grad, proj_grad)):
        ref[...] = large_out[i * high : (i + 1) * high, :].astype(F32)
    router_grad[...] = small_out[0 : router_grad.shape[0], 0:width].astype(F32)
    gain_grad[...] = small_out[32:48, 0:width].astype(F32)[0:1]
    table_grad[...] = small_out[48:64, 0:128].astype(F32)[0:3, 0:32]
    for copy in copies:
        copy.wait_recv()
    total = small_out[32:48, 0:width].astype(F32)
    for i in range(3):
        total = total + lines[i].astype(F32)
    first_grad[...] = total[8:9]
    for copy in copies:
        copy.wait_send()
    for i, ref in enumerate((large_rest, small_rest, large_rest, small_rest)):
        remote(ref, ref, send.at[i], arrive.at[0], exp=me).wait_send()
    for k in range(groups):
        reduce.drain(k)
        gather.drain(k)


def head_mask(head, head_width, width):
    lane = lax.broadcasted_iota(jnp.int32, (1, width), 1)
    return jnp.where(lane // head_width == head, 1.0, 0.0)


def fill_bias(bias, buckets, table):
    heads, block, width = bias.shape
    padded = buckets.shape[1]
    number = lax.broadcasted_iota(jnp.int32, (table.shape[1], padded), 0)
    hot = jnp.where(buckets[...] == number, 1.0, 0.0)
    offsets = jnp.dot(
        table[...], hot, precision=lax.Precision.HIGHEST, preferred_element_type=F32
    )
    for head in range(heads):
        spread = jnp.broadcast_to(offsets[head : head + 1, :], (block, padded))
        rolled = pltpu.roll(spread, padded - (block - 1), 1, stride=1, stride_axis=0)
        bias[head] = rolled[:, :width]


def attend_body(
    head_width, rows, gain, query_w, key_w, value_w, proj, buckets, table,
    mixed, mixed_all, proj_all, normed, query, query_t, key, key_t, value_t, logsum,
    bias, value, ring_sems, proj_sems,
):
    heads = bias.shape[0]
    tokens = rows.shape[0]
    width = query.shape[1]
    blocks = tokens // BLOCK
    pairs = blocks // 2
    signals = greet(4, 0)
    here = lax.axis_index("tp")
    inputs = rows[...].astype(F32)
    low = (inputs * inverse_rms(inputs) * gain[...]).astype(BF)
    normed[...] = low
    proj_all[here] = proj[...]
    meet(signals)
    gather = Gather(
        lambda k, who: mixed_all.at[who, pl.ds(pl.multiple_of(k * BLOCK, BLOCK), BLOCK), :],
        lambda k, who, half: mixed_all.at[
            who, pl.ds(pl.multiple_of(k * BLOCK + half * (BLOCK // 2), 16), BLOCK // 2), :
        ],
        ring_sems,
    )
    half_rows = proj.shape[0] // 2
    weights_gather = Gather(
        lambda k, who: proj_all.at[who],
        lambda k, who, half: proj_all.at[who, pl.ds(half * half_rows, half_rows), :],
        proj_sems,
    )
    weights_gather.start(0)
    query[...] = cols_product(low, query_w[...]).astype(BF)
    key[...] = cols_product(low, key_w[...]).astype(BF)
    value[...] = cols_product(low, value_w[...]).astype(BF)
    query_t[...] = cols_product(query_w[...], low).astype(BF)
    key_t[...] = cols_product(key_w[...], low).astype(BF)
    value_t[...] = cols_product(value_w[...], low).astype(BF)
    fill_bias(bias, buckets, table)
    weights_gather.forward(0)

    def step(pair, carry):
        for side in (0, 1):
            block = pair + side * pairs
            first = pl.multiple_of(block * BLOCK, BLOCK)
            shift = pl.multiple_of((blocks - 1 - block) * BLOCK, BLOCK)
            query_rows = query[pl.ds(first, BLOCK), :]
            total = jnp.zeros((BLOCK, width), F32)
            for head in range(heads):
                mask = head_mask(head, head_width, width)
                scores = product(query_rows * mask.astype(BF), key_t[...])
                scores = scores + bias[head, :, pl.ds(shift, tokens)]
                highest = jnp.max(scores, axis=-1, keepdims=True)
                weights = jnp.exp(scores - highest)
                summed = jnp.sum(weights, axis=-1, keepdims=True)
                part = product(weights.astype(BF), value[...]) / summed
                total = total + part * mask
                logsum[pl.ds(first, BLOCK), head : head + 1] = highest + jnp.log(summed)
            spot = pl.ds(pl.multiple_of(pair * BLOCK, BLOCK), BLOCK)
            mixed[pl.ds(first, BLOCK), :] = total.astype(BF)
            mixed_all[here, spot, side * width : (side + 1) * width] = total.astype(BF)
        gather.start(pair)

        @pl.when(pair > 0)
        def _():
            gather.forward(pair - 1)

        return carry

    lax.fori_loop(0, pairs, step, 0)
    weights_gather.finish(0)
    gather.forward(pairs - 1)
    for k in range(pairs):
        gather.finish(k)
    weights_gather.drain(0)
    for k in range(pairs):
        gather.drain(k)


def pack_third(third, experts):
    half = third.shape[1] // 2
    split = third.reshape(experts, 8, 2 * half)
    split = jnp.concatenate([split[:, :, :half], split[:, :, half:]], axis=1)
    return split.reshape(experts * 16, half)


def unpack_third(tail, runs):
    half = tail.shape[1]
    split = tail.astype(F32).reshape(runs, 16, half)
    return jnp.concatenate([split[:, :8], split[:, 8:]], axis=2).reshape(runs * 8, 2 * half)


def slot_of_row(row, experts, capacity):
    body = 16 * experts
    first = (row // 16) * capacity + row % 16
    second = ((row - body) // 16) * capacity + 16 + (row - body) % 16
    third = ((row - 2 * body) // 8) * capacity + 32 + (row - 2 * body) % 8
    return jnp.where(row < body, first, jnp.where(row < 2 * body, second, third))


def route_body(
    capacity, rows, mixed, proj, gain, router_w, ids_row, cotangent,
    residual, hidden, probs, send, slots, gates,
):
    tokens, width = rows.shape
    experts = router_w.shape[0]
    body = 16 * experts
    half, here = mixed.shape[1], mixed.shape[2] // 2
    for side in (0, 1):
        spot = slice(side * half, (side + 1) * half)
        total = rows[spot, :].astype(F32)
        for i in range(mixed.shape[0]):
            total = total + product(mixed[i, :, side * here : (side + 1) * here], proj[i])
        residual[spot, :] = total
    res = residual[...]
    low = (res * inverse_rms(res) * gain[...]).astype(BF)
    hidden[...] = low
    logits = cols_product(low, router_w[...])
    shifted = jnp.exp(logits - jnp.max(logits, axis=-1, keepdims=True))
    chances = shifted / jnp.sum(shifted, axis=-1, keepdims=True)
    probs[...] = chances
    number = lax.broadcasted_iota(jnp.int32, (experts, tokens), 0)
    hot_t = ids_row[...] == number
    ones_t = jnp.where(hot_t, 1.0, 0.0)
    hot = ones_t.T > 0.5
    gate = jnp.sum(jnp.where(hot, chances, 0.0), axis=1, keepdims=True)
    gates[...] = gate
    across = lax.broadcasted_iota(jnp.int32, (tokens, tokens), 0)
    along = lax.broadcasted_iota(jnp.int32, (tokens, tokens), 1)
    lower = jnp.where(across >= along, 1.0, 0.0).astype(BF)
    upper = jnp.where(across <= along, 1.0, 0.0).astype(BF)
    counts = product(lower, jnp.where(hot, 1.0, 0.0).astype(BF))
    counts_t = product(ones_t.astype(BF), upper)
    position = jnp.sum(jnp.where(hot, counts - 1.0, 0.0), axis=1, keepdims=True)
    position_t = jnp.sum(jnp.where(hot_t, counts_t - 1.0, 0.0), axis=0, keepdims=True)
    expert = lax.broadcasted_iota(jnp.int32, (tokens, experts), 1)
    chosen = jnp.sum(jnp.where(hot, expert.astype(F32), 0.0), axis=1, keepdims=True)
    slots[...] = chosen.astype(jnp.int32) * capacity + position.astype(jnp.int32)
    slots_t = ids_row[...] * capacity + position_t.astype(jnp.int32)
    grads = (gate * cotangent[...].astype(F32)).astype(BF)

    def group(begin, count):
        number = slot_of_row(
            lax.broadcasted_iota(jnp.int32, (count, 1), 0) + begin, experts, capacity
        )
        return jnp.where(number == slots_t, 1.0, 0.0).astype(BF)

    for begin, count, lane in ((0, body, 0), (body, body, width)):
        place = group(begin, count)
        send[0, :, lane : lane + width] = product(place, low).astype(BF)
        send[1, :, lane : lane + width] = product(place, grads).astype(BF)
    place = group(2 * body, body // 2)
    send[0, :, 2 * width :] = pack_third(product(place, low), experts).astype(BF)
    send[1, :, 2 * width :] = pack_third(product(place, grads), experts).astype(BF)


def expert_body(
    packed, weight_in, weight_out,
    value, back, in_grad, out_grad, tail_rows, tail_grads,
):
    width = weight_in.shape[0]
    rows, grads = packed.at[0], packed.at[1]
    body = packed.shape[1]
    runs = body // 16
    tail_rows[...] = unpack_third(rows[:, 2 * width :], runs).astype(BF)
    tail_grads[...] = unpack_third(grads[:, 2 * width :], runs).astype(BF)
    in_grad[...] = jnp.zeros(in_grad.shape, F32)
    out_grad[...] = jnp.zeros(out_grad.shape, F32)

    def chunk(x, g):
        pre = product(x, weight_in[...])
        inner = jnp.tanh(gelu_root * (pre + gelu_cube * pre * pre * pre))
        act = (0.5 * pre * (1.0 + inner)).astype(BF)
        slope = 0.5 * (1.0 + inner) + 0.5 * pre * (1.0 - inner * inner) * (
            gelu_root * (1.0 + 3.0 * gelu_cube * pre * pre)
        )
        out = product(act, weight_out[...])
        dots = jnp.sum(out * g.astype(F32), axis=1, keepdims=True)
        out_grad[...] += rows_product(act, g)
        act_grad = cols_product(g, weight_out[...])
        pre_grad = (act_grad * slope).astype(BF)
        in_grad[...] += rows_product(x, pre_grad)
        rows_back = cols_product(pre_grad, weight_in[...])
        return out, dots, rows_back

    lane = lax.broadcasted_iota(jnp.int32, (1, 128), 1)
    part = 256
    for begin in range(0, body, part):
        spot = pl.ds(begin, part)
        marks = jnp.zeros((part, 128), F32)
        for side in (0, 1):
            lanes = slice(side * width, (side + 1) * width)
            out, dots, rows_back = chunk(rows[spot, lanes], grads[spot, lanes])
            value[spot, lanes] = out.astype(BF)
            back[spot, lanes] = rows_back.astype(BF)
            marks = marks + jnp.where(lane == side, dots, 0.0)
        back[spot, 2 * width + width // 2 :] = marks.astype(BF)
    out, dots, rows_back = chunk(tail_rows[...], tail_grads[...])
    value[:, 2 * width + width // 2 :] = jnp.zeros((body, 128), BF)
    value[:, 2 * width : 2 * width + width // 2] = pack_third(out, runs).astype(BF)
    back[:, 2 * width : 2 * width + width // 2] = pack_third(rows_back, runs).astype(BF)
    spread = jnp.where(lane == 2, dots, 0.0).reshape(runs, 8, 128)
    spread = jnp.concatenate([spread, jnp.zeros_like(spread)], axis=1).reshape(body, 128)
    marks = back[:, 2 * width + width // 2 :].astype(F32) + spread
    back[:, 2 * width + width // 2 :] = marks.astype(BF)


def place_of(slots, experts, capacity, rows):
    number = slot_of_row(lax.broadcasted_iota(jnp.int32, (1, rows), 1), experts, capacity)
    return jnp.where(slots == number, 1.0, 0.0).astype(BF)


def token_body(
    capacity, returned, back, slots, gates, residual, hidden, probs, gain, router_w,
    cotangent, mixed, proj,
    output, router_grad, gain_grad, residual_grad, proj_grad, mixed_grad, mixed_grad_t,
):
    tokens, width = residual.shape
    experts = router_w.shape[0]
    body = 16 * experts
    place = place_of(slots[...], experts, capacity, 5 * body // 2)

    def fetch(ref):
        picked = product(place[:, :body], ref[:, :width])
        picked = picked + product(place[:, body : 2 * body], ref[:, width : 2 * width])
        tail = unpack_third(ref[:, 2 * width : 2 * width + width // 2], experts).astype(BF)
        return picked + product(place[:, 2 * body :], tail)

    token_rows = fetch(returned)
    upstream = cotangent[...].astype(F32)
    res = residual[...]
    output[...] = (res + gates[...] * token_rows).astype(BF)
    marks = back[:, 2 * width + width // 2 :]
    lane = lax.broadcasted_iota(jnp.int32, (1, 128), 1)
    tail = marks.astype(F32).reshape(experts, 16, 128)[:, :8].reshape(experts * 8, 128).astype(BF)
    dots = jnp.where(lane == 0, product(place[:, :body], marks), 0.0)
    dots = dots + jnp.where(lane == 1, product(place[:, body : 2 * body], marks), 0.0)
    dots = dots + jnp.where(lane == 2, product(place[:, 2 * body :], tail), 0.0)
    weighted = jnp.sum(dots, axis=1, keepdims=True)
    hot = slots[...] // capacity == lax.broadcasted_iota(jnp.int32, (tokens, experts), 1)
    logit_grad = (jnp.where(hot, weighted, 0.0) - probs[...] * weighted).astype(BF)
    router_grad[...] = rows_product(logit_grad, hidden[...]).astype(BF)
    hidden_grad = fetch(back) + product(logit_grad, router_w[...])
    scale = inverse_rms(res)
    gain_grad[...] = jnp.sum(hidden_grad * res * scale, axis=0, keepdims=True).astype(BF)
    scaled = gain[...] * hidden_grad
    middle = jnp.mean(scaled * res, axis=-1, keepdims=True)
    total = upstream + scale * scaled - res * (scale * scale * scale * middle)
    low = total.astype(BF)
    residual_grad[...] = total
    proj_grad[...] = rows_product(mixed[...], low).astype(BF)
    mixed_grad[...] = cols_product(low, proj[...]).astype(BF)
    mixed_grad_t[...] = cols_product(proj[...], low).astype(BF)


def attend_back_body(
    head_width, normed, query, query_t, key, key_t, value_t, logsum, grad, grad_t,
    query_w, key_w, value_w, buckets, table, rows, proj_grad, router_grad, gain_grad,
    normed_part, large, small,
    bias, sums, query_back, key_acc, value_acc,
):
    heads = bias.shape[0]
    tokens, width = query.shape
    blocks = tokens // BLOCK
    fill_bias(bias, buckets, table)
    sums[...] = jnp.zeros(sums.shape, F32)
    key_acc[...] = jnp.zeros(key_acc.shape, F32)
    value_acc[...] = jnp.zeros(value_acc.shape, F32)

    def step(block, carry):
        first = pl.multiple_of(block * BLOCK, BLOCK)
        shift = pl.multiple_of((blocks - 1 - block) * BLOCK, BLOCK)
        query_rows = query[pl.ds(first, BLOCK), :]
        grad_rows = grad[pl.ds(first, BLOCK), :]
        total = jnp.zeros((BLOCK, width), F32)
        for head in range(heads):
            mask = head_mask(head, head_width, width)
            span = slice(head * head_width, (head + 1) * head_width)
            scores = product(query_rows * mask.astype(BF), key_t[...])
            scores = scores + bias[head, :, pl.ds(shift, tokens)]
            probs = jnp.exp(scores - logsum[pl.ds(first, BLOCK), head : head + 1])
            prob_grad = product(grad_rows * mask.astype(BF), value_t[...])
            middle = jnp.sum(probs * prob_grad, axis=-1, keepdims=True)
            score_grad = probs * (prob_grad - middle)
            low = score_grad.astype(BF)
            sums[head, :, pl.ds(shift, tokens)] += score_grad
            total = total + product(low, key[...]) * mask
            key_acc[span, :] += product(query_t[span, pl.ds(first, BLOCK)], low)
            value_acc[span, :] += product(grad_t[span, pl.ds(first, BLOCK)], probs.astype(BF))
        query_back[pl.ds(first, BLOCK), :] = total.astype(BF)
        return carry

    lax.fori_loop(0, blocks, step, 0)
    backs = [query_back[...], key_acc[...].T.astype(BF), value_acc[...].T.astype(BF)]
    backs_t = [query_back[...].astype(F32).T.astype(BF)]
    backs_t += [key_acc[...].astype(BF), value_acc[...].astype(BF)]
    part = product(backs[0], query_w[...])
    part = part + product(backs[1], key_w[...]) + product(backs[2], value_w[...])
    normed_part[...] = part.astype(BF)
    for i in range(3):
        large[i * width : (i + 1) * width, :] = product(backs_t[i], normed[...]).astype(BF)
    large[3 * width :, :] = proj_grad[...]
    full = rows.shape[1]
    inputs = rows[...].astype(F32)
    line = jnp.sum(part * inputs * inverse_rms(inputs), axis=0, keepdims=True)
    small[...] = jnp.zeros(small.shape, BF)
    small[0 : router_grad.shape[0], 0:full] = router_grad[...]
    row = lax.broadcasted_iota(jnp.int32, (16, 1), 0)
    pair = jnp.where(row == 0, gain_grad[...].astype(F32), jnp.where(row == 8, line, 0.0))
    small[32:48, 0:full] = pair.astype(BF)

    padded = buckets.shape[1]
    lines = []
    for head in range(heads):
        wide = jnp.concatenate(
            [sums[head], jnp.zeros((BLOCK, padded - sums.shape[2]), F32)], axis=1
        )
        gathered = jnp.zeros((8, padded), F32)
        for part in range(BLOCK // 8):
            piece = wide[part * 8 : part * 8 + 8, :]
            gathered = gathered + pltpu.roll(piece, (BLOCK - 1 - part * 8) % padded, 1)
        line = jnp.zeros((1, padded), F32)
        for row in range(8):
            line = line + pltpu.roll(gathered, (padded - row) % padded, 1)[row : row + 1, :]
        lines.append(line)
    number = lax.broadcasted_iota(jnp.int32, (table.shape[1], padded), 0)
    hot = jnp.where(buckets[...] == number, 1.0, 0.0)
    stacked = jnp.concatenate(lines + [jnp.zeros((16 - heads, padded), F32)], axis=0)
    sums_of = lax.dot_general(
        stacked,
        hot,
        (((1,), (1,)), ((), ())),
        precision=lax.Precision.HIGHEST,
        preferred_element_type=F32,
    )
    blank = jnp.zeros((16, 128 - table.shape[1]), F32)
    small[48:64, 0:128] = jnp.concatenate([sums_of, blank], axis=1).astype(BF)


def per_device(
    layer_in, expert_ids, rel_buckets, first_gain, query_weight, key_weight, value_weight,
    proj_weight, rel_table, second_gain, router_weight, expert_in, expert_out, cotangent,
):
    tokens, width = layer_in.shape
    heads = rel_table.shape[1]
    here = query_weight.shape[1]
    head_width = here // heads
    experts = router_weight.shape[1]
    capacity = 5 * tokens // (4 * experts)
    body = 16 * experts
    packed = 2 * width + width // 2
    quarter = width // 2
    span = 2 * tokens - BLOCK
    ring_size = width // here
    gain_one = first_gain[None, :]
    gain_two = second_gain[None, :]
    buckets = jnp.pad(rel_buckets, (0, 1), constant_values=-1)[None, :]
    weights = (query_weight.T, key_weight.T, value_weight.T)
    table = rel_table.T
    router = router_weight.T

    mixed, mixed_all, proj_all, normed, query, query_t, key, key_t, value_t, logsum = call(
        functools.partial(attend_body, head_width),
        "attend",
        [
            ((tokens, here), BF),
            ((ring_size, tokens // 2, 2 * here), BF),
            ((ring_size, here, width), BF),
            ((tokens, width), BF),
            ((tokens, here), BF),
            ((here, tokens), BF),
            ((tokens, here), BF),
            ((here, tokens), BF),
            ((here, tokens), BF),
            ((tokens, 128), F32),
        ],
        [
            pltpu.VMEM((heads, BLOCK, span), F32),
            pltpu.VMEM((tokens, here), BF),
            sems(tokens // BLOCK // 2, 8),
            sems(1, 8),
        ],
        layer_in, gain_one, *weights, proj_weight, buckets, table,
        number=1,
    )
    residual, hidden, probs, leaving, slots, gates = call(
        functools.partial(route_body, capacity),
        "route",
        [
            ((tokens, width), F32),
            ((tokens, width), BF),
            ((tokens, experts), F32),
            ((2, body, packed), BF),
            ((tokens, 1), jnp.int32),
            ((tokens, 1), F32),
        ],
        [],
        layer_in, mixed_all, proj_all, gain_two, router, expert_ids.reshape(1, tokens), cotangent,
    )
    (arrived,) = call(
        functools.partial(dispatch_body, experts, quarter),
        "dispatch",
        [((2, body, packed), BF)],
        [sems(2), sems(GROUPS + 1), sems(GROUPS, 8)],
        leaving,
        number=2,
    )
    value, back, in_grad, out_grad = call(
        expert_body,
        "expert",
        [
            ((body, packed + 128), BF),
            ((body, packed + 128), BF),
            ((width, expert_in.shape[2]), F32),
            ((expert_out.shape[1], width), F32),
        ],
        [pltpu.VMEM((body // 2, width), BF)] * 2,
        arrived, expert_in[0], expert_out[0],
    )

    def give_back(array, number):
        return call(
            functools.partial(return_body, experts, (packed + 128) // 4),
            "give_back",
            [((body, packed + 128), BF)],
            return_scratch(experts, (packed + 128) // 4),
            array,
            number=number,
        )[0]

    (
        output, router_grad, second_gain_grad, residual_grad, proj_grad, mixed_grad, mixed_grad_t
    ) = call(
        functools.partial(token_body, capacity),
        "token",
        [
            ((tokens, width), BF),
            ((experts, width), BF),
            ((1, width), BF),
            ((tokens, width), F32),
            ((here, width), BF),
            ((tokens, here), BF),
            ((here, tokens), BF),
        ],
        [],
        give_back(value, 3), give_back(back, 3), slots, gates, residual, hidden, probs, gain_two,
        router, cotangent, mixed, proj_weight,
    )
    normed_part, large, small = call(
        functools.partial(attend_back_body, head_width),
        "attend_back",
        [((tokens, width), BF), ((4 * here, width), BF), ((64, 1024), BF)],
        [
            pltpu.VMEM((heads, BLOCK, span), F32),
            pltpu.VMEM((heads, BLOCK, span), F32),
            pltpu.VMEM((tokens, here), BF),
            pltpu.VMEM((here, tokens), F32),
            pltpu.VMEM((here, tokens), F32),
        ],
        normed, query, query_t, key, key_t, value_t, logsum, mixed_grad, mixed_grad_t,
        *weights, buckets, table, layer_in, proj_grad, router_grad, second_gain_grad,
    )
    tall, wide = 2 * 4 * here // experts, width // 2
    (
        input_grad, query_grad, key_grad, value_grad, proj_total, router_total, gain_total,
        first_total, table_total,
    ) = call(
        functools.partial(final_body, experts),
        "final",
        [
            ((tokens, width), F32),
            ((here, width), F32),
            ((here, width), F32),
            ((here, width), F32),
            ((here, width), F32),
            ((experts, width), F32),
            ((1, width), F32),
            ((1, width), F32),
            (table.shape, F32),
        ],
        [
            pltpu.VMEM((tokens, width), BF),
            pltpu.VMEM((experts, tall, wide), BF),
            pltpu.VMEM((experts, 16, 128), BF),
            pltpu.VMEM((4 * here, width), BF),
            pltpu.VMEM((64, 1024), BF),
            pltpu.VMEM((3, 16, width), BF),
            *reduce_scratch(4, tokens // 32, width),
            sems(4),
            sems(4),
            sems(3, 2),
            sems(4, 8),
            sems(4, 8),
        ],
        normed_part, large, small, residual_grad, layer_in, gain_one,
        number=4,
    )
    return (
        output,
        input_grad,
        first_total[0],
        query_grad.T,
        key_grad.T,
        value_grad.T,
        proj_total,
        table_total.T,
        gain_total[0],
        router_total.T,
        in_grad[None],
        out_grad[None],
    )


def solution(mesh):
    return jax.shard_map(
        per_device,
        mesh=mesh,
        in_specs=(
            P("exp", None),
            P("exp", None),
            P(),
            P(),
            P(None, "tp"),
            P(None, "tp"),
            P(None, "tp"),
            P("tp", None),
            P(None, "tp"),
            P(),
            P(),
            P("exp", None, "tp"),
            P("exp", "tp", None),
            P("exp", None),
        ),
        out_specs=(
            P("exp", None),
            P("exp", None),
            P(),
            P(None, "tp"),
            P(None, "tp"),
            P(None, "tp"),
            P("tp", None),
            P(None, "tp"),
            P(),
            P(),
            P("exp", None, "tp"),
            P("exp", "tp", None),
        ),
        check_vma=False,
    )
```

time: 686 us -> 306 us (0.45); the launches traced: 673 us -> 302 us
  waiting for transfers between devices: 288 us -> 0 us
  blocking collectives: 260 us -> 0 us
  Pallas kernels: 75.7 us -> 279 us
  between operations: 14.5 us -> 1.05 us
  other arithmetic: 11 us -> 1.21 us
    psum x3 -> x0, waiting for transfers between devices: 235 us -> none  [the longest x1 101 us: over_batch(): return lax.psum(part.astype(BF), 'exp').astype(F32)]
    pallas_call x5 -> x9, Pallas kernels: 75.7 us -> 279 us  [call(): pl.pallas_call(body, name=name, out_shape=[jax.ShapeDtypeStruct(shape, dt...]
    all_to_all x4 -> x0, blocking collectives: 135 us -> none  [exchange(): lax.all_to_all(split, 'exp', split_axis=0, concat_axis=0, tiled=True)]
    psum x1 -> x0, blocking collectives: 125 us -> none  [over_batch(): return lax.psum(part.astype(BF), 'exp').astype(F32)]
    all_gather x2 -> x0, waiting for transfers between devices: 51.2 us -> none  [the longest x1 28.6 us: per_device(): mixed_full = lax.all_gather(mixed, 'tp', axis=1, tiled=True)]
    unnamed x79 -> x47, local copies, waits for them, and re-layouts: 19.8 us -> 18.7 us
  transfers between devices with their start and end apart: 5 -> 0, of which waited for: 5 -> 0; matrix products, arithmetic and copies ran while one was open for 1% -> 0% of each run, Pallas kernels for 0% -> 0%
where the time goes in v1:
time: 306 us; the launch traced here: 302 us
  Pallas kernels  279 us (91%)
  local copies, waits for them, and re-layouts  20.9 us (7%)
    pallas_call x9, Pallas kernels, call(): pl.pallas_call(body, name=name, out_shape=[jax.ShapeDtypeStruct(shape, dt...  279 us
    unnamed x47, local copies, waits for them, and re-layouts  18.7 us

profile of v1, /device:TPU:1, one launch (start us, length us, event | category | flops | bytes accessed | tf_op | source)
XLA Modules:
  0.0 302.0 jit_solution(11226639948347351393)
XLA Ops:
  0.6 0.0 copy-start
  0.7 0.8 broadcast_in_dim.15.gain
  1.5 0.7 broadcast_in_dim.17.gain
  2.2 0.7 pad.4
  2.9 0.0 copy-start.6
  2.9 1.0 copy-done.6
  3.8 0.0 copy-start.8
  3.8 1.0 copy-done.8
  4.8 1.0 copy-done.10
  5.7 1.0 copy-done.12
  6.7 0.7 copy-done.17
  7.4 32.2 %attend.1 = (bf16[1024,192]{1,0:T(8,128)(2,1)S(1)}, bf16[4,512,384]{2,1,0:T(8,128)(2,1)}, bf16[4,192,768]{2,1,0:T(8,128)(2,1)S(1)}, bf16[1024,768]{1,0:T(8,128)(...) custom-call(bf16[1024,768]{1,0:T(8,128)(2,1)} %rows.7, ...), custom_call_target="tpu_custom_call" | custom-call | tf_op jit(solution)/shard_map/attend/pallas_call | solution.py:40
  39.6 0.0 copy-done
  39.6 0.0 copy-done.16
  39.6 0.0 copy-done.19
  39.7 11.9 %route.1 = (f32[1024,768]{1,0:T(8,128)}, bf16[1024,768]{1,0:T(8,128)(2,1)S(1)}, f32[1024,32]{1,0:T(8,128)S(1)}, bf16[2,512,1920]{2,1,0:T(8,128)(2,1)}, s32[1024,1]{1,0:T(8,128)S(1)}, /*index=5*/f32[1024,1]{1,0:T(8,128)S(1)}) custom-call(bf16[1024,768]{1,0:T(8,128)(2,1)S(1)} %copy-done, bf16[4,512,384]{2,1,0:T(8,128)(2,1)} %get-tuple-element.51.mixed, ...), custom_call_target="tpu_custom_call" | custom-call | tf_op jit(solution)/shard_map/route/pallas_call | solution.py:40
  51.6 45.7 %dispatch.1.packed = bf16[2,512,1920]{2,1,0:T(8,128)(2,1)S(1)} custom-call(bf16[2,512,1920]{2,1,0:T(8,128)(2,1)} %get-tuple-element.53.source), custom_call_target="tpu_custom_call" | custom-call | tf_op jit(solution)/shard_map/dispatch/pallas_call | solution.py:40
  97.2 0.0 copy-start.1
  97.2 1.8 copy-done.1
  99.1 0.0 copy-done.14
  99.1 0.0 copy-done.15
  99.1 15.1 %expert.1 = (bf16[512,2048]{1,0:T(8,128)(2,1)S(1)}, bf16[512,2048]{1,0:T(8,128)(2,1)}, f32[768,768]{1,0:T(8,128)}, f32[768,768]{1,0:T(8,128)}) custom-call(bf16[2,512,1920]{2,1,0:T(8,128)(2,1)} %copy-done.1, bf16[768,768]{1,0:T(8,128)(2,1)S(1)} %bitcast.22, bf16[768,768]{1,0:T(8,128)(2,1)S(1)} %bitcast.23), custom_call_target="tpu_custom_call" | custom-call | tf_op jit(solution)/shard_map/expert/pallas_call | solution.py:40
  114.1 41.6 %give_back.2.returned = bf16[512,2048]{1,0:T(8,128)(2,1)S(1)} custom-call(bf16[512,2048]{1,0:T(8,128)(2,1)S(1)} %get-tuple-element.54.source), custom_call_target="tpu_custom_call" | custom-call | tf_op jit(solution)/shard_map/give_back/pallas_call | solution.py:40
  155.8 0.0 copy-start.2
  155.8 1.3 copy-done.2
  157.1 0.0 copy-done.4
  157.1 43.8 %give_back.3.back = bf16[512,2048]{1,0:T(8,128)(2,1)S(1)} custom-call(bf16[512,2048]{1,0:T(8,128)(2,1)S(1)} %copy-done.4), custom_call_target="tpu_custom_call" | custom-call | tf_op jit(solution)/shard_map/give_back/pallas_call | solution.py:40
  201.0 0.0 copy-start.3
  201.0 1.3 copy-done.3
  202.3 0.0 copy-done.7
  202.3 0.0 copy-start.18
  202.3 13.9 %token_.1 = (bf16[1024,768]{1,0:T(8,128)(2,1)}, bf16[32,768]{1,0:T(8,128)(2,1)S(1)}, bf16[1,768]{1,0:T(2,128)(2,1)S(1)}, f32[1024,768]{1,0:T(8,128)}, bf16[192,7...) custom-call(bf16[512,2048]{1,0:T(8,128)(2,1)} %copy-done.2, ...), custom_call_target="tpu_custom_call" | custom-call | tf_op jit(solution)/shard_map/token/pallas_call | solution.py:40
  216.2 0.0 copy-done.9
  216.2 0.0 copy-done.11
  216.3 0.0 copy-done.13
  216.3 0.0 copy-done.18
  216.3 21.8 %attend_back.1 = (bf16[1024,768]{1,0:T(8,128)(2,1)}, bf16[768,768]{1,0:T(8,128)(2,1)S(1)}, bf16[64,1024]{1,0:T(8,128)(2,1)S(1)}) custom-call(bf16[1024,768]{1,0:T(8,128)(2,1)} %get-tuple-element.63.normed, bf16[1024,192]{1,0:T(8,128)(2,1)S(1)} %get-tuple-element.64.query, bf16[192,1024]{1,0:T(8,128)(2,1)S(1)} %get-tuple-element.65.query_t, ...), custom_call_target="tpu_custom_call" | custom-call | tf_op jit(solution)/shard_map/attend_back/pallas_call | solution.py:40
  238.0 1.4 copy-done.5
  239.4 52.9 %final.1 = (f32[1024,768]{1,0:T(8,128)}, f32[192,768]{1,0:T(8,128)S(1)}, f32[192,768]{1,0:T(8,128)S(1)}, f32[192,768]{1,0:T(8,128)S(1)}, f32[192,768]{1,0:T(8,12...) custom-call(bf16[1024,768]{1,0:T(8,128)(2,1)S(1)} %copy-done.5, ...), custom_call_target="tpu_custom_call" | custom-call | tf_op jit(solution)/shard_map/final/pallas_call | solution.py:40
  292.3 0.6 reduce
  292.9 0.6 reduce.1
  293.5 3.8 %copy.33 = f32[1024,768]{1,0:T(8,128)} copy(f32[1024,768]{1,0:T(8,128)} %get-tuple-element.103) | data formatting | bytes 6291456
  297.3 0.8 copy.34
  298.1 0.8 copy.35
  298.9 0.8 copy.36
  299.7 0.8 copy.37
  300.5 0.6 copy.38
  301.1 0.6 copy.39
  (13 shorter events, 0.0 us)
Async XLA Ops:
  0.6 39.0 %copy-start = (bf16[1024,768]{1,0:T(8,128)(2,1)S(1)}, bf16[1024,768]{1,0:T(8,128)(2,1)}, u32[]{:S(2)}) copy-start(bf16[1024,768]{1,0:T(8,128)(2,1)} %rows.7) | copy-start | bytes 4718596
  2.9 1.0 copy-start.6
  3.8 1.0 copy-start.8
  4.8 1.0 copy-start.10
  5.7 1.0 copy-start.12
  6.7 0.7 copy-start.17
  7.4 32.3 %copy-start.16 = (bf16[768,32]{0,1:T(8,128)(2,1)S(1)}, bf16[768,32]{0,1:T(8,128)(2,1)}, u32[]{:S(2)}) copy-start(bf16[768,32]{0,1:T(8,128)(2,1)} %param.24) | copy-start | bytes 147460
  7.4 32.3 %copy-start.19 = (s32[1024,1]{0,1:T(1,128)S(1)}, s32[1024,1]{0,1:T(1,128)}, u32[]{:S(2)}) copy-start(s32[1024,1]{0,1:T(1,128)} %param.15) | copy-start | bytes 12292
  51.6 47.5 %copy-start.14 = (bf16[1,768,768]{2,1,0:T(8,128)(2,1)S(1)}, bf16[1,768,768]{2,1,0:T(8,128)(2,1)}, u32[]{:S(2)}) copy-start(bf16[1,768,768]{2,1,0:T(8,128)(2,1)} %param.25) | copy-start | bytes 3538948
  51.6 47.5 %copy-start.15 = (bf16[1,768,768]{2,1,0:T(8,128)(2,1)S(1)}, bf16[1,768,768]{2,1,0:T(8,128)(2,1)}, u32[]{:S(2)}) copy-start(bf16[1,768,768]{2,1,0:T(8,128)(2,1)} %param.26) | copy-start | bytes 3538948
  97.2 1.9 copy-start.1
  114.1 43.0 %copy-start.4 = (bf16[512,2048]{1,0:T(8,128)(2,1)S(1)}, bf16[512,2048]{1,0:T(8,128)(2,1)}, u32[]{:S(2)}) copy-start(bf16[512,2048]{1,0:T(8,128)(2,1)} %get-tuple-element.55.source) | copy-start | bytes 6291460
  155.8 1.4 copy-start.2
  157.1 45.2 %copy-start.7 = (bf16[192,768]{1,0:T(8,128)(2,1)S(1)}, bf16[192,768]{1,0:T(8,128)(2,1)}, u32[]{:S(2)}) copy-start(bf16[192,768]{1,0:T(8,128)(2,1)} %proj.3) | copy-start | bytes 884740
  201.0 1.3 copy-start.3
  202.3 13.9 %copy-start.9 = (bf16[768,192]{0,1:T(8,128)(2,1)S(1)}, bf16[768,192]{0,1:T(8,128)(2,1)}, u32[]{:S(2)}) copy-start(bf16[768,192]{0,1:T(8,128)(2,1)} %param.18) | copy-start | bytes 884740
  202.3 13.9 %copy-start.11 = (bf16[768,192]{0,1:T(8,128)(2,1)S(1)}, bf16[768,192]{0,1:T(8,128)(2,1)}, u32[]{:S(2)}) copy-start(bf16[768,192]{0,1:T(8,128)(2,1)} %param.19) | copy-start | bytes 884740
  202.3 13.9 %copy-start.13 = (bf16[768,192]{0,1:T(8,128)(2,1)S(1)}, bf16[768,192]{0,1:T(8,128)(2,1)}, u32[]{:S(2)}) copy-start(bf16[768,192]{0,1:T(8,128)(2,1)} %param.20) | copy-start | bytes 884740
  202.3 13.9 %copy-start.18 = (f32[32,3]{0,1:T(4,128)S(1)}, f32[32,3]{0,1:T(4,128)}, u32[]{:S(2)}) copy-start(f32[32,3]{0,1:T(4,128)} %param.22) | copy-start | bytes 1156
  238.0 1.4 copy-start.5

commit v2 on v1

--- a/solution.py
+++ b/solution.py
@@ -64,7 +64,7 @@
     return here, lax.rem(here + 1, ring_size), lax.rem(here + ring_size - 1, ring_size)
 
 
-def greet(ring_size, batch_size, opposite=False):
+def greet(ring_size, batch_size, opposite=False, same_core=False):
     barrier = pltpu.get_barrier_semaphore()
     here, right, left = ring(ring_size)
     for side in (right, left):
@@ -72,16 +72,22 @@
     if opposite:
         side = lax.rem(here + 2, ring_size)
         pl.semaphore_signal(barrier, inc=1, device_id={"tp": side}, device_id_type=MESH)
-    if batch_size:
-        me = lax.axis_index("exp")
-
-        def hello(step, carry):
-            peer = lax.rem(me + step, batch_size)
-            pl.semaphore_signal(barrier, inc=1, device_id={"exp": peer}, device_id_type=MESH)
-            return carry
-
-        lax.fori_loop(1, batch_size, hello, 0)
-    return 2 + int(opposite) + max(batch_size - 1, 0)
+    if not batch_size:
+        return 2 + int(opposite)
+    me = lax.axis_index("exp")
+    stride = 2 if same_core else 1
+    peers = batch_size // stride
+
+    def hello(step, carry):
+        peer = lax.rem(me + step * stride, batch_size)
+        pl.semaphore_signal(barrier, inc=1, device_id={"exp": peer}, device_id_type=MESH)
+        return carry
+
+    lax.fori_loop(1, peers, hello, 0)
+    if same_core:
+        sibling = me + 1 - 2 * lax.rem(me, 2)
+        pl.semaphore_signal(barrier, inc=1, device_id={"exp": sibling}, device_id_type=MESH)
+    return 2 + int(opposite) + peers - 1 + int(same_core)
 
 
 def meet(signals):
@@ -347,22 +353,23 @@
 
 
 def final_body(
-    batch_size, part_in, large, small, residual_grad, rows, gain,
-    input_grad, query_grad, key_grad, value_grad, proj_grad, router_grad, gain_grad, first_grad,
-    table_grad,
-    summed, large_in, small_in, large_out, small_out, lines, *rest,
+    batch_size, capacity, part_in, large, small, returned, slots, gates, residual,
+    summed, large_out, small_out, lines, output,
+    large_side, small_side, large_in, small_in, *rest,
 ):
     buffers, (send, arrive, line_sems, sum_sems, ring_sems) = rest[:6], rest[6:]
-    signals = greet(4, batch_size, opposite=True)
+    signals = greet(4, batch_size, opposite=True, same_core=True)
     me = lax.axis_index("exp")
+    core = lax.rem(me, 2)
+    sibling = me + 1 - 2 * core
     here, right, left = ring(4)
     tokens, width = part_in.shape
     chunk = tokens // 4
     groups = buffers[0].shape[0]
     half_rows = chunk // groups // 2
-    tall, wide = large_in.shape[1:]
-    across = width // wide
-    small_across = small.shape[1] // 128
+    peers, tall, wide = large_in.shape
+    half_lanes = small.shape[1] // 2
+    small_across = half_lanes // 128
 
     def spot(ref, who, k, begin, count):
         first = who * chunk + k * (2 * half_rows) + begin
@@ -377,71 +384,104 @@
         ring_sems,
     )
 
-    def large_part(ref, who):
-        down = pl.ds(pl.multiple_of(who // across * tall, 16), tall)
-        return ref.at[down, pl.ds(pl.multiple_of(lax.rem(who, across) * wide, 128), wide)]
-
-    def small_part(ref, who):
+    def large_half(ref, side):
+        return ref.at[:, pl.ds(pl.multiple_of(side * wide, 128), wide)]
+
+    def small_half(ref, side):
+        return ref.at[:, pl.ds(pl.multiple_of(side * half_lanes, 128), half_lanes)]
+
+    def large_rows(ref, who):
+        return ref.at[pl.ds(pl.multiple_of(who * tall, 16), tall), :]
+
+    def small_rows(ref, who):
         down = pl.ds(pl.multiple_of(who // small_across * 16, 16), 16)
         return ref.at[down, pl.ds(pl.multiple_of(lax.rem(who, small_across) * 128, 128), 128)]
 
+    def large_final(who):
+        down = pl.ds(pl.multiple_of(who * tall, 16), tall)
+        return large_out.at[down, pl.ds(pl.multiple_of(core * wide, 128), wide)]
+
+    def small_final(who):
+        down = pl.ds(pl.multiple_of(who // small_across * 16, 16), 16)
+        lane = core * half_lanes + lax.rem(who, small_across) * 128
+        return small_out.at[down, pl.ds(pl.multiple_of(lane, 128), 128)]
+
     meet(signals)
+    pair = [
+        remote(large_half(large, 1 - core), large_side, send.at[0], arrive.at[0], exp=sibling),
+        remote(small_half(small, 1 - core), small_side, send.at[1], arrive.at[1], exp=sibling),
+    ]
+    for copy in pair:
+        copy.start()
     for k in range(groups):
         reduce.start(k)
+    for copy in pair:
+        copy.wait_recv()
+    both = large_side[...].astype(F32) + large_half(large, core)[...].astype(F32)
+    large_side[...] = both.astype(BF)
+    both = small_side[...].astype(F32) + small_half(small, core)[...].astype(F32)
+    small_side[...] = both.astype(BF)
+    mine = me // 2
 
     def scatter(step, carry):
-        peer = lax.rem(me + step, batch_size)
-        remote(large_part(large, peer), large_in.at[step], send.at[0], arrive.at[0], exp=peer).start()
-        remote(small_part(small, peer), small_in.at[step], send.at[1], arrive.at[1], exp=peer).start()
+        peer = lax.rem(mine + step, peers)
+        to = peer * 2 + core
+        remote(large_rows(large_side, peer), large_in.at[step], send.at[2], arrive.at[2], exp=to).start()
+        remote(small_rows(small_side, peer), small_in.at[step], send.at[3], arrive.at[3], exp=to).start()
         return carry
 
-    lax.fori_loop(1, batch_size, scatter, 0)
-    large_in[0] = large_part(large, me)[...]
-    small_in[0] = small_part(small, me)[...]
+    lax.fori_loop(1, peers, scatter, 0)
+    large_in[0] = large_rows(large_side, mine)[...]
+    small_in[0] = small_rows(small_side, mine)[...]
     for k in range(groups):
         reduce.middle(k)
+
+    experts = batch_size
+    body = 16 * experts
+    place = place_of(slots[...], experts, capacity, 5 * body // 2)
+    token_rows = fetch(place, returned, width, experts)
+    output[...] = (residual[...] + gates[...] * token_rows).astype(BF)
+
+    large_rest = large_in.at[pl.ds(1, peers - 1)]
+    small_rest = small_in.at[pl.ds(1, peers - 1)]
+    remote(large_rest, large_rest, send.at[2], arrive.at[2], exp=me).wait_recv()
+    remote(small_rest, small_rest, send.at[3], arrive.at[3], exp=me).wait_recv()
+
+    def add(step, carry):
+        return carry[0] + large_in[step].astype(F32), carry[1] + small_in[step].astype(F32)
+
+    zero = (jnp.zeros((tall, wide), F32), jnp.zeros((16, 128), F32))
+    large_sum, small_sum = lax.fori_loop(0, peers, add, zero)
+    large_final(mine)[...] = large_sum.astype(BF)
+    small_final(mine)[...] = small_sum.astype(BF)
+
+    def spread(step, carry):
+        to = lax.rem(mine + step, peers) * 2 + core
+        own = large_final(mine)
+        remote(own, own, send.at[4], arrive.at[4], exp=to).start()
+        own = small_final(mine)
+        remote(own, own, send.at[5], arrive.at[5], exp=to).start()
+        return carry
+
+    lax.fori_loop(1, peers, spread, 0)
     for k in range(groups):
         pieces = reduce.finish(k)
         for half in (0, 1):
             target = spot(summed, here, k, half * half_rows, half_rows)
             target[...] = pieces[half].astype(BF)
         gather.start(k)
-    large_rest = large_in.at[pl.ds(1, batch_size - 1)]
-    small_rest = small_in.at[pl.ds(1, batch_size - 1)]
-    remote(large_rest, large_rest, send.at[0], arrive.at[0], exp=me).wait_recv()
-    remote(small_rest, small_rest, send.at[1], arrive.at[1], exp=me).wait_recv()
-
-    def add(step, carry):
-        return carry[0] + large_in[step].astype(F32), carry[1] + small_in[step].astype(F32)
-
-    zero = (jnp.zeros((tall, wide), F32), jnp.zeros((16, 128), F32))
-    large_sum, small_sum = lax.fori_loop(0, batch_size, add, zero)
-    large_part(large_out, me)[...] = large_sum.astype(BF)
-    small_part(small_out, me)[...] = small_sum.astype(BF)
-
-    def spread(step, carry):
-        peer = lax.rem(me + step, batch_size)
-        own = large_part(large_out, me)
-        remote(own, own, send.at[2], arrive.at[2], exp=peer).start()
-        own = small_part(small_out, me)
-        remote(own, own, send.at[3], arrive.at[3], exp=peer).start()
-        return carry
-
-    lax.fori_loop(1, batch_size, spread, 0)
+    remote(large_rest, large_rest, send.at[4], arrive.at[4], exp=me).wait_recv()
+    remote(small_rest, small_rest, send.at[5], arrive.at[5], exp=me).wait_recv()
+    back = []
+    for i, half in ((6, large_half(large_out, core)), (7, small_half(small_out, core))):
+        back.append(remote(half, half, send.at[i], arrive.at[i], exp=sibling))
+    for copy in back:
+        copy.start()
     for k in range(groups):
         gather.forward(k)
-    for k in range(groups):
-        gather.finish(k)
-    inputs = rows[...].astype(F32)
-    scale = inverse_rms(inputs)
-    scaled = summed[...].astype(F32) * gain[...]
-    middle = jnp.mean(scaled * inputs, axis=-1, keepdims=True)
-    input_grad[...] = (
-        residual_grad[...] + scale * scaled - inputs * (scale * scale * scale * middle)
-    )
-    remote(large_rest, large_rest, send.at[2], arrive.at[2], exp=me).wait_recv()
-    remote(small_rest, small_rest, send.at[3], arrive.at[3], exp=me).wait_recv()
-    line = small_out.at[pl.ds(32, 16), pl.ds(0, width)]
+    for i, half in ((6, large_half(large_out, 1 - core)), (7, small_half(small_out, 1 - core))):
+        remote(half, half, send.at[i], arrive.at[i], exp=sibling).wait_recv()
+    line = small_out.at[pl.ds(32, 16), :]
     others = (right, left, lax.rem(here + 2, 4))
     copies = [
         remote(line, lines.at[i], line_sems.at[i, 0], line_sems.at[i, 1], tp=side)
@@ -449,25 +489,44 @@
     ]
     for copy in copies:
         copy.start()
-    high = query_grad.shape[0]
-    for i, ref in enumerate((query_grad, key_grad, value_grad, proj_grad)):
-        ref[...] = large_out[i * high : (i + 1) * high, :].astype(F32)
-    router_grad[...] = small_out[0 : router_grad.shape[0], 0:width].astype(F32)
-    gain_grad[...] = small_out[32:48, 0:width].astype(F32)[0:1]
-    table_grad[...] = small_out[48:64, 0:128].astype(F32)[0:3, 0:32]
+    for k in range(groups):
+        gather.finish(k)
     for copy in copies:
         copy.wait_recv()
-    total = small_out[32:48, 0:width].astype(F32)
-    for i in range(3):
-        total = total + lines[i].astype(F32)
-    first_grad[...] = total[8:9]
-    for copy in copies:
+    for copy in copies + pair + back:
         copy.wait_send()
-    for i, ref in enumerate((large_rest, small_rest, large_rest, small_rest)):
+    for i, ref in ((2, large_rest), (3, small_rest), (4, large_rest), (5, small_rest)):
         remote(ref, ref, send.at[i], arrive.at[0], exp=me).wait_send()
     for k in range(groups):
         reduce.drain(k)
         gather.drain(k)
+
+
+def finish_body(
+    summed, rows, residual_grad, gain, large, small, lines,
+    input_grad, query_grad, key_grad, value_grad, proj_grad, router_grad, gain_grad, first_grad,
+    table_grad,
+):
+    inputs = rows[...].astype(F32)
+    scale = inverse_rms(inputs)
+    scaled = summed[...].astype(F32) * gain[...]
+    middle = jnp.mean(scaled * inputs, axis=-1, keepdims=True)
+    input_grad[...] = (
+        residual_grad[...] + scale * scaled - inputs * (scale * scale * scale * middle)
+    )
+
+    @pl.when(pl.program_id(0) == 0)
+    def _():
+        high, width = query_grad.shape
+        for i, ref in enumerate((query_grad, key_grad, value_grad, proj_grad)):
+            ref[...] = large[i * high : (i + 1) * high, :].astype(F32)
+        router_grad[...] = small[0 : router_grad.shape[0], 0:width].astype(F32)
+        total = small[32:48, 0:width].astype(F32)
+        gain_grad[...] = total[0:1]
+        table_grad[...] = small[48:64, 0:128].astype(F32)[0:3, 0:32]
+        for i in range(3):
+            total = total + lines[i][:, 0:width].astype(F32)
+        first_grad[...] = total[8:9]
 
 
 def head_mask(head, head_width, width):
@@ -700,27 +759,39 @@
     return jnp.where(slots == number, 1.0, 0.0).astype(BF)
 
 
-def token_body(
-    capacity, returned, back, slots, gates, residual, hidden, probs, gain, router_w,
-    cotangent, mixed, proj,
-    output, router_grad, gain_grad, residual_grad, proj_grad, mixed_grad, mixed_grad_t,
+def fetch(place, ref, width, experts):
+    body = 16 * experts
+    picked = product(place[:, :body], ref[:, :width])
+    picked = picked + product(place[:, body : 2 * body], ref[:, width : 2 * width])
+    tail = unpack_third(ref[:, 2 * width : 2 * width + width // 2], experts).astype(BF)
+    return picked + product(place[:, 2 * body :], tail)
+
+
+def backward_body(
+    batch_size, capacity, head_width, lanes,
+    value_in, back, slots, residual, hidden, probs, gain, router_w, cotangent, mixed, proj,
+    normed, query, query_t, key, key_t, value_t, logsum,
+    query_w, key_w, value_w, buckets, table, rows,
+    returned, residual_grad, normed_part, large, small,
+    grad, grad_t, bias, sums, query_back, key_acc, value_acc, stage, *rest,
 ):
-    tokens, width = residual.shape
+    buffers, (send, arrive, sum_sems, ring_sems) = rest[:6], rest[6:]
+    signals = greet(4, batch_size)
+    reduce, gather, scatter, collect, drain = return_parts(
+        batch_size, lanes, value_in, returned, stage, buffers, send, arrive, sum_sems, ring_sems
+    )
+    tokens, full = residual.shape
     experts = router_w.shape[0]
     body = 16 * experts
+    heads = bias.shape[0]
+    width = query.shape[1]
+    blocks = tokens // BLOCK
     place = place_of(slots[...], experts, capacity, 5 * body // 2)
-
-    def fetch(ref):
-        picked = product(place[:, :body], ref[:, :width])
-        picked = picked + product(place[:, body : 2 * body], ref[:, width : 2 * width])
-        tail = unpack_third(ref[:, 2 * width : 2 * width + width // 2], experts).astype(BF)
-        return picked + product(place[:, 2 * body :], tail)
-
-    token_rows = fetch(returned)
-    upstream = cotangent[...].astype(F32)
-    res = residual[...]
-    output[...] = (res + gates[...] * token_rows).astype(BF)
-    marks = back[:, 2 * width + width // 2 :]
+    meet(signals)
+    for k in range(GROUPS):
+        reduce.start(k)
+
+    marks = back[:, 2 * full + full // 2 :]
     lane = lax.broadcasted_iota(jnp.int32, (1, 128), 1)
     tail = marks.astype(F32).reshape(experts, 16, 128)[:, :8].reshape(experts * 8, 128).astype(BF)
     dots = jnp.where(lane == 0, product(place[:, :body], marks), 0.0)
@@ -729,29 +800,24 @@
     weighted = jnp.sum(dots, axis=1, keepdims=True)
     hot = slots[...] // capacity == lax.broadcasted_iota(jnp.int32, (tokens, experts), 1)
     logit_grad = (jnp.where(hot, weighted, 0.0) - probs[...] * weighted).astype(BF)
-    router_grad[...] = rows_product(logit_grad, hidden[...]).astype(BF)
-    hidden_grad = fetch(back) + product(logit_grad, router_w[...])
+    router_grad = rows_product(logit_grad, hidden[...])
+    hidden_grad = fetch(place, back, full, experts) + product(logit_grad, router_w[...])
+    for k in range(GROUPS // 2):
+        reduce.middle(k)
+    res = residual[...]
     scale = inverse_rms(res)
-    gain_grad[...] = jnp.sum(hidden_grad * res * scale, axis=0, keepdims=True).astype(BF)
+    gain_grad = jnp.sum(hidden_grad * res * scale, axis=0, keepdims=True)
     scaled = gain[...] * hidden_grad
     middle = jnp.mean(scaled * res, axis=-1, keepdims=True)
-    total = upstream + scale * scaled - res * (scale * scale * scale * middle)
+    total = cotangent[...].astype(F32) + scale * scaled - res * (scale * scale * scale * middle)
     low = total.astype(BF)
     residual_grad[...] = total
-    proj_grad[...] = rows_product(mixed[...], low).astype(BF)
-    mixed_grad[...] = cols_product(low, proj[...]).astype(BF)
-    mixed_grad_t[...] = cols_product(proj[...], low).astype(BF)
-
-
-def attend_back_body(
-    head_width, normed, query, query_t, key, key_t, value_t, logsum, grad, grad_t,
-    query_w, key_w, value_w, buckets, table, rows, proj_grad, router_grad, gain_grad,
-    normed_part, large, small,
-    bias, sums, query_back, key_acc, value_acc,
-):
-    heads = bias.shape[0]
-    tokens, width = query.shape
-    blocks = tokens // BLOCK
+    for k in range(GROUPS // 2, GROUPS):
+        reduce.middle(k)
+    large[3 * width :, :] = rows_product(mixed[...], low).astype(BF)
+    grad[...] = cols_product(low, proj[...]).astype(BF)
+    grad_t[...] = cols_product(proj[...], low).astype(BF)
+
     fill_bias(bias, buckets, table)
     sums[...] = jnp.zeros(sums.shape, F32)
     key_acc[...] = jnp.zeros(key_acc.shape, F32)
@@ -762,25 +828,45 @@
         shift = pl.multiple_of((blocks - 1 - block) * BLOCK, BLOCK)
         query_rows = query[pl.ds(first, BLOCK), :]
         grad_rows = grad[pl.ds(first, BLOCK), :]
-        total = jnp.zeros((BLOCK, width), F32)
+        acc = jnp.zeros((BLOCK, width), F32)
         for head in range(heads):
             mask = head_mask(head, head_width, width)
             span = slice(head * head_width, (head + 1) * head_width)
             scores = product(query_rows * mask.astype(BF), key_t[...])
             scores = scores + bias[head, :, pl.ds(shift, tokens)]
-            probs = jnp.exp(scores - logsum[pl.ds(first, BLOCK), head : head + 1])
+            chances = jnp.exp(scores - logsum[pl.ds(first, BLOCK), head : head + 1])
             prob_grad = product(grad_rows * mask.astype(BF), value_t[...])
-            middle = jnp.sum(probs * prob_grad, axis=-1, keepdims=True)
-            score_grad = probs * (prob_grad - middle)
-            low = score_grad.astype(BF)
+            centre = jnp.sum(chances * prob_grad, axis=-1, keepdims=True)
+            score_grad = chances * (prob_grad - centre)
+            score_low = score_grad.astype(BF)
             sums[head, :, pl.ds(shift, tokens)] += score_grad
-            total = total + product(low, key[...]) * mask
-            key_acc[span, :] += product(query_t[span, pl.ds(first, BLOCK)], low)
-            value_acc[span, :] += product(grad_t[span, pl.ds(first, BLOCK)], probs.astype(BF))
-        query_back[pl.ds(first, BLOCK), :] = total.astype(BF)
+            acc = acc + product(score_low, key[...]) * mask
+            key_acc[span, :] += product(query_t[span, pl.ds(first, BLOCK)], score_low)
+            value_acc[span, :] += product(grad_t[span, pl.ds(first, BLOCK)], chances.astype(BF))
+        query_back[pl.ds(first, BLOCK), :] = acc.astype(BF)
         return carry
 
-    lax.fori_loop(0, blocks, step, 0)
+    def run(begin, end):
+        lax.fori_loop(begin, end, step, 0)
+
+    run(0, 2)
+    scatter(0)
+    scatter(1)
+    run(2, 3)
+    scatter(2)
+    scatter(3)
+    run(3, 5)
+    collect(0)
+    collect(1)
+    run(5, 6)
+    collect(2)
+    collect(3)
+    run(6, 7)
+    gather.forward(0)
+    gather.forward(1)
+    run(7, blocks)
+    gather.forward(2)
+    gather.forward(3)
     backs = [query_back[...], key_acc[...].T.astype(BF), value_acc[...].T.astype(BF)]
     backs_t = [query_back[...].astype(F32).T.astype(BF)]
     backs_t += [key_acc[...].astype(BF), value_acc[...].astype(BF)]
@@ -789,14 +875,12 @@
     normed_part[...] = part.astype(BF)
     for i in range(3):
         large[i * width : (i + 1) * width, :] = product(backs_t[i], normed[...]).astype(BF)
-    large[3 * width :, :] = proj_grad[...]
-    full = rows.shape[1]
     inputs = rows[...].astype(F32)
     line = jnp.sum(part * inputs * inverse_rms(inputs), axis=0, keepdims=True)
     small[...] = jnp.zeros(small.shape, BF)
-    small[0 : router_grad.shape[0], 0:full] = router_grad[...]
+    small[0:experts, 0:full] = router_grad.astype(BF)
     row = lax.broadcasted_iota(jnp.int32, (16, 1), 0)
-    pair = jnp.where(row == 0, gain_grad[...].astype(F32), jnp.where(row == 8, line, 0.0))
+    pair = jnp.where(row == 0, gain_grad, jnp.where(row == 8, line, 0.0))
     small[32:48, 0:full] = pair.astype(BF)
 
     padded = buckets.shape[1]
@@ -806,25 +890,28 @@
             [sums[head], jnp.zeros((BLOCK, padded - sums.shape[2]), F32)], axis=1
         )
         gathered = jnp.zeros((8, padded), F32)
-        for part in range(BLOCK // 8):
-            piece = wide[part * 8 : part * 8 + 8, :]
-            gathered = gathered + pltpu.roll(piece, (BLOCK - 1 - part * 8) % padded, 1)
+        for piece_at in range(0, BLOCK, 8):
+            piece = wide[piece_at : piece_at + 8, :]
+            gathered = gathered + pltpu.roll(piece, (BLOCK - 1 - piece_at) % padded, 1)
         line = jnp.zeros((1, padded), F32)
-        for row in range(8):
-            line = line + pltpu.roll(gathered, (padded - row) % padded, 1)[row : row + 1, :]
+        for i in range(8):
+            line = line + pltpu.roll(gathered, (padded - i) % padded, 1)[i : i + 1, :]
         lines.append(line)
     number = lax.broadcasted_iota(jnp.int32, (table.shape[1], padded), 0)
-    hot = jnp.where(buckets[...] == number, 1.0, 0.0)
+    matches = jnp.where(buckets[...] == number, 1.0, 0.0)
     stacked = jnp.concatenate(lines + [jnp.zeros((16 - heads, padded), F32)], axis=0)
     sums_of = lax.dot_general(
         stacked,
-        hot,
+        matches,
         (((1,), (1,)), ((), ())),
         precision=lax.Precision.HIGHEST,
         preferred_element_type=F32,
     )
     blank = jnp.zeros((16, 128 - table.shape[1]), F32)
     small[48:64, 0:128] = jnp.concatenate([sums_of, blank], axis=1).astype(BF)
+    for k in range(GROUPS):
+        gather.finish(k)
+    drain()
 
 
 def per_device(
@@ -908,83 +995,94 @@
         arrived, expert_in[0], expert_out[0],
     )
 
-    def give_back(array, number):
-        return call(
-            functools.partial(return_body, experts, (packed + 128) // 4),
-            "give_back",
-            [((body, packed + 128), BF)],
-            return_scratch(experts, (packed + 128) // 4),
-            array,
-            number=number,
-        )[0]
-
-    (
-        output, router_grad, second_gain_grad, residual_grad, proj_grad, mixed_grad, mixed_grad_t
-    ) = call(
-        functools.partial(token_body, capacity),
-        "token",
+    (back_sum,) = call(
+        functools.partial(return_body, experts, (packed + 128) // 4),
+        "give_back",
+        [((body, packed + 128), BF)],
+        return_scratch(experts, (packed + 128) // 4),
+        back,
+        number=3,
+    )
+    returned, residual_grad, normed_part, large, small = call(
+        functools.partial(backward_body, experts, capacity, head_width, (packed + 128) // 4),
+        "backward",
         [
+            ((body, packed + 128), BF),
+            ((tokens, width), F32),
             ((tokens, width), BF),
-            ((experts, width), BF),
-            ((1, width), BF),
-            ((tokens, width), F32),
-            ((here, width), BF),
-            ((tokens, here), BF),
-            ((here, tokens), BF),
+            ((4 * here, width), BF),
+            ((64, 1024), BF),
         ],
-        [],
-        give_back(value, 3), give_back(back, 3), slots, gates, residual, hidden, probs, gain_two,
-        router, cotangent, mixed, proj_weight,
-    )
-    normed_part, large, small = call(
-        functools.partial(attend_back_body, head_width),
-        "attend_back",
-        [((tokens, width), BF), ((4 * here, width), BF), ((64, 1024), BF)],
         [
+            pltpu.VMEM((tokens, here), BF),
+            pltpu.VMEM((here, tokens), BF),
             pltpu.VMEM((heads, BLOCK, span), F32),
             pltpu.VMEM((heads, BLOCK, span), F32),
             pltpu.VMEM((tokens, here), BF),
             pltpu.VMEM((here, tokens), F32),
             pltpu.VMEM((here, tokens), F32),
+            *return_scratch(experts, (packed + 128) // 4),
         ],
-        normed, query, query_t, key, key_t, value_t, logsum, mixed_grad, mixed_grad_t,
-        *weights, buckets, table, layer_in, proj_grad, router_grad, second_gain_grad,
-    )
-    tall, wide = 2 * 4 * here // experts, width // 2
-    (
-        input_grad, query_grad, key_grad, value_grad, proj_total, router_total, gain_total,
-        first_total, table_total,
-    ) = call(
-        functools.partial(final_body, experts),
+        value, back_sum, slots, residual, hidden, probs, gain_two, router, cotangent, mixed,
+        proj_weight, normed, query, query_t, key, key_t, value_t, logsum, *weights, buckets, table,
+        layer_in,
+        number=5,
+        mib=58,
+    )
+    peers = experts // 2
+    tall, wide = 4 * here // peers, width // 2
+    summed, large_sum, small_sum, lines, output = call(
+        functools.partial(final_body, experts, capacity),
         "final",
         [
-            ((tokens, width), F32),
-            ((here, width), F32),
-            ((here, width), F32),
-            ((here, width), F32),
-            ((here, width), F32),
-            ((experts, width), F32),
-            ((1, width), F32),
-            ((1, width), F32),
-            (table.shape, F32),
+            ((tokens, width), BF),
+            ((4 * here, width), BF),
+            ((64, 1024), BF),
+            ((3, 16, 1024), BF),
+            ((tokens, width), BF),
         ],
         [
-            pltpu.VMEM((tokens, width), BF),
-            pltpu.VMEM((experts, tall, wide), BF),
-            pltpu.VMEM((experts, 16, 128), BF),
-            pltpu.VMEM((4 * here, width), BF),
-            pltpu.VMEM((64, 1024), BF),
-            pltpu.VMEM((3, 16, width), BF),
+            pltpu.VMEM((4 * here, wide), BF),
+            pltpu.VMEM((64, 512), BF),
+            pltpu.VMEM((peers, tall, wide), BF),
+            pltpu.VMEM((peers, 16, 128), BF),
             *reduce_scratch(4, tokens // 32, width),
-            sems(4),
-            sems(4),
+            sems(8),
+            sems(8),
             sems(3, 2),
             sems(4, 8),
             sems(4, 8),
         ],
-        normed_part, large, small, residual_grad, layer_in, gain_one,
+        normed_part, large, small, returned, slots, gates, residual,
         number=4,
     )
+
+    def whole(array):
+        return pl.BlockSpec(array.shape, lambda i: (0,) * len(array.shape))
+
+    def strip(array):
+        return pl.BlockSpec((128, array.shape[1]), lambda i: (i, 0))
+
+    results = [
+        jax.ShapeDtypeStruct(shape, F32)
+        for shape in [(tokens, width)] + [(here, width)] * 4
+        + [(experts, width), (1, width), (1, width), table.shape]
+    ]
+    (
+        input_grad, query_grad, key_grad, value_grad, proj_total, router_total, gain_total,
+        first_total, table_total,
+    ) = pl.pallas_call(
+        finish_body,
+        name="finish",
+        grid=(tokens // 128,),
+        out_shape=results,
+        in_specs=[
+            strip(summed), strip(layer_in), strip(residual_grad), whole(gain_one),
+            whole(large_sum), whole(small_sum), whole(lines),
+        ],
+        out_specs=[strip(results[0])] + [whole(result) for result in results[1:]],
+        compiler_params=pltpu.CompilerParams(vmem_limit_bytes=32 * MIB),
+    )(summed, layer_in, residual_grad, gain_one, large_sum, small_sum, lines)
     return (
         output,
         input_grad,

time: 306 us -> 274 us (0.90)
  Pallas kernels: 279 us -> 247 us
    pallas_call x9 -> x7, Pallas kernels: 279 us -> 242 us  [call(): pl.pallas_call(body, name=name, out_shape=[jax.ShapeDtypeStruct(shape, dt...]
    pallas_call x0 -> x1, Pallas kernels: none -> 4.85 us  [per_device(): pl.pallas_call(finish_body, name='finish', grid=(tokens // 128,), out_sha...]
    unnamed x47 -> x65, local copies, waits for them, and re-layouts: 18.7 us -> 18.4 us
where the time goes in v2:
time: 274 us; the launch traced here: 270 us
  Pallas kernels  247 us (90%)
  local copies, waits for them, and re-layouts  20.6 us (8%)
    pallas_call x7, Pallas kernels, call(): pl.pallas_call(body, name=name, out_shape=[jax.ShapeDtypeStruct(shape, dt...  242 us
    unnamed x65, local copies, waits for them, and re-layouts  18.4 us

profile of v2, /device:TPU:1, one launch (start us, length us, event | category | flops | bytes accessed | tf_op | source)
XLA Modules:
  0.0 270.1 jit_solution(3082565999781594479)
XLA Ops:
  0.6 0.0 copy-start
  0.7 0.8 broadcast_in_dim.15.gain
  1.5 0.7 broadcast_in_dim.17.gain
  2.2 0.7 pad.4
  2.9 1.0 copy-done.13
  3.8 1.0 copy-done.14
  4.8 1.0 copy-done.15
  5.8 1.0 copy-done.16
  6.7 0.7 copy-done.29
  7.4 31.2 %attend.1 = (bf16[1024,192]{1,0:T(8,128)(2,1)S(1)}, bf16[4,512,384]{2,1,0:T(8,128)(2,1)}, bf16[4,192,768]{2,1,0:T(8,128)(2,1)S(1)}, bf16[1024,768]{1,0:T(8,128)(...) custom-call(bf16[1024,768]{1,0:T(8,128)(2,1)} %rows.7, ...), custom_call_target="tpu_custom_call" | custom-call | tf_op jit(solution)/shard_map/attend/pallas_call | solution.py:40
  38.6 0.0 copy-start.17
  38.6 0.8 copy-done.17
  39.4 0.8 copy-done.20
  40.2 0.8 copy-done.24
  41.0 0.0 copy-done
  41.0 0.0 copy-done.25
  41.0 0.0 copy-done.30
  41.0 12.6 %route.1 = (f32[1024,768]{1,0:T(8,128)}, bf16[1024,768]{1,0:T(8,128)(2,1)S(1)}, f32[1024,32]{1,0:T(8,128)S(1)}, bf16[2,512,1920]{2,1,0:T(8,128)(2,1)}, s32[1024,1]{1,0:T(8,128)S(1)}, /*index=5*/f32[1024,1]{1,0:T(8,128)S(1)}) custom-call(bf16[1024,768]{1,0:T(8,128)(2,1)S(1)} %copy-done, bf16[4,512,384]{2,1,0:T(8,128)(2,1)} %get-tuple-element.51.mixed, ...), custom_call_target="tpu_custom_call" | custom-call | tf_op jit(solution)/shard_map/route/pallas_call | solution.py:40
  53.6 0.0 copy-done.28
  53.6 0.0 copy-done.27
  53.6 0.0 copy-done.18
  53.6 0.0 copy-done.19
  53.6 0.0 copy-done.22
  53.6 0.0 copy-done.23
  53.6 0.0 copy-start.9
  53.7 1.1 copy-done.9
  54.8 0.8 copy-done.21
  55.6 46.3 %dispatch.1.packed = bf16[2,512,1920]{2,1,0:T(8,128)(2,1)S(1)} custom-call(bf16[2,512,1920]{2,1,0:T(8,128)(2,1)} %get-tuple-element.53.source), custom_call_target="tpu_custom_call" | custom-call | tf_op jit(solution)/shard_map/dispatch/pallas_call | solution.py:40
  101.9 0.0 copy-done.6
  101.9 0.0 copy-start.2
  101.9 1.9 copy-done.2
  103.8 0.0 copy-done.11
  103.8 0.0 copy-done.12
  103.8 15.5 %expert.1 = (bf16[512,2048]{1,0:T(8,128)(2,1)S(1)}, bf16[512,2048]{1,0:T(8,128)(2,1)}, f32[768,768]{1,0:T(8,128)}, f32[768,768]{1,0:T(8,128)}) custom-call(bf16[2,512,1920]{2,1,0:T(8,128)(2,1)} %copy-done.2, bf16[768,768]{1,0:T(8,128)(2,1)S(1)} %bitcast.16, bf16[768,768]{1,0:T(8,128)(2,1)S(1)} %bitcast.17), custom_call_target="tpu_custom_call" | custom-call | tf_op jit(solution)/shard_map/expert/pallas_call | solution.py:40
  119.3 1.3 copy-done.5
  120.6 1.6 copy-done.8
  122.2 41.7 %give_back.1.back = bf16[512,2048]{1,0:T(8,128)(2,1)S(1)} custom-call(bf16[512,2048]{1,0:T(8,128)(2,1)S(1)} %copy-done.8), custom_call_target="tpu_custom_call" | custom-call | tf_op jit(solution)/shard_map/give_back/pallas_call | solution.py:40
  163.9 0.0 copy-start.3
  164.0 1.4 copy-done.3
  165.3 56.9 %backward.1 = (bf16[512,2048]{1,0:T(8,128)(2,1)}, f32[1024,768]{1,0:T(8,128)}, bf16[1024,768]{1,0:T(8,128)(2,1)}, bf16[768,768]{1,0:T(8,128)(2,1)}, bf16[64,1024]{1,0:T(8,128)(2,1)}) custom-call(bf16[512,2048]{1,0:T(8,128)(2,1)} %copy-done.5, bf16[512,2048]{1,0:T(8,128)(2,1)} %copy-done.3, s32[1024,1]{1,0:T(8,128)} %copy-done.6, ...), custom_call_target="tpu_custom_call" | custom-call | tf_op jit(solution)/shard_map/backward/pallas_call | solution.py:40
  222.3 1.3 copy-done.10
  223.5 0.9 copy-done.26
  224.4 38.2 %final.1 = (bf16[1024,768]{1,0:T(8,128)(2,1)S(1)}, bf16[768,768]{1,0:T(8,128)(2,1)S(1)}, bf16[64,1024]{1,0:T(8,128)(2,1)S(1)}, bf16[3,16,1024]{2,1,0:T(8,128)(2,1)S(1)}, bf16[1024,768]{1,0:T(8,128)(2,1)}) custom-call(bf16[1024,768]{1,0:T(8,128)(2,1)} %get-tuple-element.68.part_in, bf16[768,768]{1,0:T(8,128)(2,1)S(1)} %copy-done.10, ...), custom_call_target="tpu_custom_call" | custom-call | tf_op jit(solution)/shard_map/final/pallas_call | solution.py:40
  262.7 4.8 %finish.1 = (f32[1024,768]{1,0:T(8,128)}, f32[192,768]{1,0:T(8,128)}, f32[192,768]{1,0:T(8,128)}, f32[192,768]{1,0:T(8,128)}, f32[192,768]{1,0:T(8,128)}, /*inde...) custom-call(bf16[1024,768]{1,0:T(8,128)(2,1)S(1)} %get-tuple-element.74.summed, ...), custom_call_target="tpu_custom_call" | custom-call | tf_op jit(solution)/shard_map/finish/pallas_call | solution.py:1074
  267.5 0.6 reduce
  268.1 0.6 reduce.1
  268.7 0.0 copy-done.31
  268.7 1.1 copy.27
  (30 shorter events, 0.0 us)
Async XLA Ops:
  0.6 40.4 %copy-start = (bf16[1024,768]{1,0:T(8,128)(2,1)S(1)}, bf16[1024,768]{1,0:T(8,128)(2,1)}, u32[]{:S(2)}) copy-start(bf16[1024,768]{1,0:T(8,128)(2,1)} %rows.7) | copy-start | bytes 4718596
  2.2 51.5 %copy-start.28 = (f32[1,768]{1,0:T(1,128)}, f32[1,768]{1,0:T(1,128)S(1)}, u32[]{:S(2)}) copy-start(f32[1,768]{1,0:T(1,128)S(1)} %broadcast_in_dim.17.gain) | copy-start | bytes 9220
  2.9 50.8 %copy-start.27 = (s32[2048]{0:T(1024)}, s32[2048]{0:T(1024)S(1)}, u32[]{:S(2)}) copy-start(s32[2048]{0:T(1024)S(1)} %pad.4) | copy-start | bytes 24580
  2.9 1.0 copy-start.13
  3.8 1.0 copy-start.14
  4.8 1.0 copy-start.15
  5.8 1.0 copy-start.16
  6.7 0.7 copy-start.29
  7.4 33.6 %copy-start.25 = (bf16[768,32]{0,1:T(8,128)(2,1)S(1)}, bf16[768,32]{0,1:T(8,128)(2,1)}, u32[]{:S(2)}) copy-start(bf16[768,32]{0,1:T(8,128)(2,1)} %param.24) | copy-start | bytes 147460
  7.4 33.6 %copy-start.30 = (s32[1024,1]{0,1:T(1,128)S(1)}, s32[1024,1]{0,1:T(1,128)}, u32[]{:S(2)}) copy-start(s32[1024,1]{0,1:T(1,128)} %param.15) | copy-start | bytes 12292
  38.6 0.8 copy-start.17
  39.4 0.8 copy-start.20
  40.2 0.8 copy-start.24
  41.0 12.6 %copy-start.18 = (bf16[1024,192]{1,0:T(8,128)(2,1)}, bf16[1024,192]{1,0:T(8,128)(2,1)S(1)}, u32[]{:S(2)}) copy-start(bf16[1024,192]{1,0:T(8,128)(2,1)S(1)} %get-tuple-element.62.query) | copy-start | bytes 1179652
  41.0 12.6 %copy-start.19 = (bf16[1024,192]{1,0:T(8,128)(2,1)}, bf16[1024,192]{1,0:T(8,128)(2,1)S(1)}, u32[]{:S(2)}) copy-start(bf16[1024,192]{1,0:T(8,128)(2,1)S(1)} %get-tuple-element.64.key) | copy-start | bytes 1179652
  41.0 12.6 %copy-start.22 = (bf16[192,1024]{1,0:T(8,128)(2,1)}, bf16[192,1024]{1,0:T(8,128)(2,1)S(1)}, u32[]{:S(2)}) copy-start(bf16[192,1024]{1,0:T(8,128)(2,1)S(1)} %get-tuple-element.63.query_t) | copy-start | bytes 1179652
  41.0 12.6 %copy-start.23 = (bf16[192,1024]{1,0:T(8,128)(2,1)}, bf16[192,1024]{1,0:T(8,128)(2,1)S(1)}, u32[]{:S(2)}) copy-start(bf16[192,1024]{1,0:T(8,128)(2,1)S(1)} %get-tuple-element.65.key_t) | copy-start | bytes 1179652
  53.6 1.1 copy-start.9
  54.8 0.8 copy-start.21
  55.6 46.3 %copy-start.6 = (s32[1024,1]{1,0:T(8,128)}, s32[1024,1]{1,0:T(8,128)S(1)}, u32[]{:S(2)}) copy-start(s32[1024,1]{1,0:T(8,128)S(1)} %get-tuple-element.56.slots) | copy-start | bytes 12292
  55.6 48.2 %copy-start.11 = (bf16[1,768,768]{2,1,0:T(8,128)(2,1)S(1)}, bf16[1,768,768]{2,1,0:T(8,128)(2,1)}, u32[]{:S(2)}) copy-start(bf16[1,768,768]{2,1,0:T(8,128)(2,1)} %param.25) | copy-start | bytes 3538948
  55.6 48.2 %copy-start.12 = (bf16[1,768,768]{2,1,0:T(8,128)(2,1)S(1)}, bf16[1,768,768]{2,1,0:T(8,128)(2,1)}, u32[]{:S(2)}) copy-start(bf16[1,768,768]{2,1,0:T(8,128)(2,1)} %param.26) | copy-start | bytes 3538948
  101.9 1.9 copy-start.2
  119.3 1.3 copy-start.5
  120.6 1.6 copy-start.8
  163.9 1.4 copy-start.3
  165.3 56.9 %copy-start.7 = (s32[1024,1]{1,0:T(8,128)S(1)}, s32[1024,1]{1,0:T(8,128)}, u32[]{:S(2)}) copy-start(s32[1024,1]{1,0:T(8,128)} %copy-done.6) | copy-start | bytes 12292
  222.3 1.3 copy-start.10
  223.5 0.9 copy-start.26
  224.4 38.2 %copy-start.1 = (bf16[1024,768]{1,0:T(8,128)(2,1)S(1)}, bf16[1024,768]{1,0:T(8,128)(2,1)}, u32[]{:S(2)}) copy-start(bf16[1024,768]{1,0:T(8,128)(2,1)} %rows.7) | copy-start | bytes 4718596
  224.4 38.2 %copy-start.4 = (f32[1024,768]{1,0:T(8,128)S(1)}, f32[1024,768]{1,0:T(8,128)}, u32[]{:S(2)}) copy-start(f32[1024,768]{1,0:T(8,128)} %get-tuple-element.75.residual_grad) | copy-start | bytes 9437188
  262.7 6.1 %copy-start.31 = (bf16[1024,768]{1,0:T(8,128)(2,1)S(1)}, bf16[1024,768]{1,0:T(8,128)(2,1)}, u32[]{:S(2)}) copy-start(bf16[1024,768]{1,0:T(8,128)(2,1)} %get-tuple-element.102) | copy-start | bytes 4718596

commit v3 on v2

--- a/solution.py
+++ b/solution.py
@@ -72,9 +72,12 @@
     if opposite:
         side = lax.rem(here + 2, ring_size)
         pl.semaphore_signal(barrier, inc=1, device_id={"tp": side}, device_id_type=MESH)
+    me = lax.axis_index("exp")
+    if same_core:
+        sibling = me + 1 - 2 * lax.rem(me, 2)
+        pl.semaphore_signal(barrier, inc=1, device_id={"exp": sibling}, device_id_type=MESH)
     if not batch_size:
-        return 2 + int(opposite)
-    me = lax.axis_index("exp")
+        return 2 + int(opposite) + int(same_core)
     stride = 2 if same_core else 1
     peers = batch_size // stride
 
@@ -84,9 +87,6 @@
         return carry
 
     lax.fori_loop(1, peers, hello, 0)
-    if same_core:
-        sibling = me + 1 - 2 * lax.rem(me, 2)
-        pl.semaphore_signal(barrier, inc=1, device_id={"exp": sibling}, device_id_type=MESH)
     return 2 + int(opposite) + peers - 1 + int(same_core)
 
 
@@ -200,62 +200,6 @@
     return pltpu.SemaphoreType.DMA(dims)
 
 
-def dispatch_body(batch_size, lanes, source, out, send, arrive, ring_sems):
-    signals = greet(4, batch_size)
-    me = lax.axis_index("exp")
-    here = lax.axis_index("tp")
-    part = batch_size // GROUPS
-    mine = pl.ds(pl.multiple_of(here * lanes, 128), lanes)
-    tail = pl.ds(4 * lanes, lanes)
-    own = pl.ds(pl.multiple_of(me * 16, 16), 16)
-    out[:, own, mine] = source[:, own, mine]
-    out[:, own, tail] = source[:, own, tail]
-    meet(signals)
-
-    def arriving(k):
-        return lax.rem(me // part + GROUPS - k, GROUPS) * (part * 16)
-
-    def span(k, who, begin, rows, array=slice(None)):
-        spot = pl.ds(pl.multiple_of(arriving(k) + begin, 16), rows)
-        return out.at[array, spot, pl.ds(pl.multiple_of(who * lanes, 128), lanes)]
-
-    gather = Gather(
-        lambda k, who: span(k, who, 0, part * 16),
-        lambda k, who, half: span(k, who, 0, part * 16, pl.ds(half, 1)),
-        ring_sems,
-    )
-
-    def scatter(columns, send_sem, sem_of):
-        for k in range(GROUPS):
-
-            def step(j, carry):
-                peer = lax.rem(me // part + k, GROUPS) * part + lax.rem(me + j, part)
-                rows = pl.ds(pl.multiple_of(peer * 16, 16), 16)
-                remote(source.at[:, rows, columns], out.at[:, own, columns], send_sem, sem_of(k), exp=peer).start()
-                return carry
-
-            lax.fori_loop(1 if k == 0 else 0, part, step, 0)
-
-    scatter(mine, send.at[0], lambda k: arrive.at[k])
-    scatter(tail, send.at[1], lambda k: arrive.at[GROUPS])
-    for k in range(GROUPS):
-        rows = (part - 1 if k == 0 else part) * 16
-        block = span(k, here, 0, rows)
-        remote(block, block, send.at[0], arrive.at[k], exp=me).wait_recv()
-        gather.start(k)
-        if k:
-            gather.forward(k - 1)
-    gather.forward(GROUPS - 1)
-    whole = out.at[:, pl.ds(0, (batch_size - 1) * 16), tail]
-    remote(whole, whole, send.at[1], arrive.at[GROUPS], exp=me).wait_recv()
-    for k in range(GROUPS):
-        gather.finish(k)
-    remote(whole, whole, send.at[0], arrive.at[0], exp=me).wait_send()
-    remote(whole, whole, send.at[1], arrive.at[0], exp=me).wait_send()
-    for k in range(GROUPS):
-        gather.drain(k)
-
-
 def return_parts(batch_size, lanes, source, out, stage, buffers, send, arrive, sum_sems, ring_sems):
     me = lax.axis_index("exp")
     here = lax.axis_index("tp")
@@ -264,10 +208,10 @@
     own = pl.ds(pl.multiple_of(me * 16, 16), 16)
 
     def leaving(k):
+        return lax.rem(me // part + GROUPS - k, GROUPS) * (part * 16)
+
+    def arriving(k):
         return lax.rem(me // part + k, GROUPS) * (part * 16)
-
-    def arriving(k):
-        return lax.rem(me // part + GROUPS - k, GROUPS) * (part * 16)
 
     def span(ref, base, who, begin, rows):
         spot = pl.ds(pl.multiple_of(base + begin, 16), rows)
@@ -294,7 +238,7 @@
             out[own, mine] = stage[own, :]
 
         def step(j, carry):
-            peer = lax.rem(me // part + k, GROUPS) * part + lax.rem(me + j, part)
+            peer = lax.rem(me // part + GROUPS - k, GROUPS) * part + lax.rem(me + j, part)
             rows = pl.ds(pl.multiple_of(peer * 16, 16), 16)
             remote(stage.at[rows, :], out.at[own, mine], send.at[0], arrive.at[k], exp=peer).start()
             return carry
@@ -315,30 +259,6 @@
             gather.drain(k)
 
     return reduce, gather, scatter, collect, drain
-
-
-def return_body(batch_size, lanes, source, out, stage, *rest):
-    buffers, (send, arrive, sum_sems, ring_sems) = rest[:6], rest[6:]
-    signals = greet(4, batch_size)
-    reduce, gather, scatter, collect, drain = return_parts(
-        batch_size, lanes, source, out, stage, buffers, send, arrive, sum_sems, ring_sems
-    )
-    meet(signals)
-    for k in range(GROUPS):
-        reduce.start(k)
-    for k in range(GROUPS):
-        reduce.middle(k)
-        if k:
-            scatter(k - 1)
-    scatter(GROUPS - 1)
-    for k in range(GROUPS):
-        collect(k)
-        if k:
-            gather.forward(k - 1)
-    gather.forward(GROUPS - 1)
-    for k in range(GROUPS):
-        gather.finish(k)
-    drain()
 
 
 def return_scratch(batch_size, lanes):
@@ -551,15 +471,18 @@
 def attend_body(
     head_width, rows, gain, query_w, key_w, value_w, proj, buckets, table,
     mixed, mixed_all, proj_all, normed, query, query_t, key, key_t, value_t, logsum,
-    bias, value, ring_sems, proj_sems,
+    bias, value, ring_sems, proj_sems, pair_sems,
 ):
     heads = bias.shape[0]
     tokens = rows.shape[0]
     width = query.shape[1]
     blocks = tokens // BLOCK
     pairs = blocks // 2
-    signals = greet(4, 0)
+    signals = greet(4, 0, same_core=True)
     here = lax.axis_index("tp")
+    me = lax.axis_index("exp")
+    core = lax.rem(me, 2)
+    sibling = me + 1 - 2 * core
     inputs = rows[...].astype(F32)
     low = (inputs * inverse_rms(inputs) * gain[...]).astype(BF)
     normed[...] = low
@@ -573,11 +496,22 @@
         ring_sems,
     )
     half_rows = proj.shape[0] // 2
+
+    def proj_part(who, side, begin, count):
+        spot = pl.multiple_of(side * half_rows + begin, 16)
+        return proj_all.at[who, pl.ds(spot, count), :]
+
     weights_gather = Gather(
-        lambda k, who: proj_all.at[who],
-        lambda k, who, half: proj_all.at[who, pl.ds(half * half_rows, half_rows), :],
+        lambda k, who: proj_part(who, core, 0, half_rows),
+        lambda k, who, half: proj_part(who, core, half * (half_rows // 2), half_rows // 2),
         proj_sems,
     )
+
+    def to_sibling(i, who, side):
+        part = proj_part(who, side, 0, half_rows)
+        return remote(part, part, pair_sems.at[i, 0], pair_sems.at[i, 1], exp=sibling)
+
+    foreign = (weights_gather.left, weights_gather.right, weights_gather.far)
     weights_gather.start(0)
     query[...] = cols_product(low, query_w[...]).astype(BF)
     key[...] = cols_product(low, key_w[...]).astype(BF)
@@ -587,6 +521,8 @@
     value_t[...] = cols_product(value_w[...], low).astype(BF)
     fill_bias(bias, buckets, table)
     weights_gather.forward(0)
+    for i in (0, 1):
+        to_sibling(i, foreign[i], core).start()
 
     def step(pair, carry):
         for side in (0, 1):
@@ -616,11 +552,16 @@
 
         return carry
 
-    lax.fori_loop(0, pairs, step, 0)
+    lax.fori_loop(0, pairs // 2, step, 0)
     weights_gather.finish(0)
+    to_sibling(2, foreign[2], core).start()
+    lax.fori_loop(pairs // 2, pairs, step, 0)
     gather.forward(pairs - 1)
     for k in range(pairs):
         gather.finish(k)
+    for i in range(3):
+        to_sibling(i, foreign[i], 1 - core).wait_recv()
+        to_sibling(i, foreign[i], core).wait_send()
     weights_gather.drain(0)
     for k in range(pairs):
         gather.drain(k)
@@ -647,19 +588,28 @@
     return jnp.where(row < body, first, jnp.where(row < 2 * body, second, third))
 
 
-def route_body(
-    capacity, rows, mixed, proj, gain, router_w, ids_row, cotangent,
-    residual, hidden, probs, send, slots, gates,
+def moe_body(
+    batch_size, capacity, lanes, back_lanes,
+    rows, mixed, proj, gain, router_w, ids_row, cotangent, weight_in, weight_out,
+    residual, hidden, probs, slots, gates, value, back_sum, in_grad, out_grad,
+    leave, arrived, back, stage, *rest,
 ):
+    buffers, (send_back, arrive_back, sum_sems, back_sems) = rest[:6], rest[6:10]
+    send, arrive, arrive_tail, ring_sems = rest[10:]
+    signals = greet(4, batch_size)
+    me = lax.axis_index("exp")
+    here = lax.axis_index("tp")
+    part = batch_size // GROUPS
+    zone_rows = part * 16
     tokens, width = rows.shape
     experts = router_w.shape[0]
-    body = 16 * experts
-    half, here = mixed.shape[1], mixed.shape[2] // 2
+    half, heads_here = mixed.shape[1], mixed.shape[2] // 2
     for side in (0, 1):
         spot = slice(side * half, (side + 1) * half)
         total = rows[spot, :].astype(F32)
         for i in range(mixed.shape[0]):
-            total = total + product(mixed[i, :, side * here : (side + 1) * here], proj[i])
+            lane = side * heads_here
+            total = total + product(mixed[i, :, lane : lane + heads_here], proj[i])
         residual[spot, :] = total
     res = residual[...]
     low = (res * inverse_rms(res) * gain[...]).astype(BF)
@@ -676,82 +626,171 @@
     gates[...] = gate
     across = lax.broadcasted_iota(jnp.int32, (tokens, tokens), 0)
     along = lax.broadcasted_iota(jnp.int32, (tokens, tokens), 1)
-    lower = jnp.where(across >= along, 1.0, 0.0).astype(BF)
     upper = jnp.where(across <= along, 1.0, 0.0).astype(BF)
-    counts = product(lower, jnp.where(hot, 1.0, 0.0).astype(BF))
     counts_t = product(ones_t.astype(BF), upper)
-    position = jnp.sum(jnp.where(hot, counts - 1.0, 0.0), axis=1, keepdims=True)
     position_t = jnp.sum(jnp.where(hot_t, counts_t - 1.0, 0.0), axis=0, keepdims=True)
-    expert = lax.broadcasted_iota(jnp.int32, (tokens, experts), 1)
-    chosen = jnp.sum(jnp.where(hot, expert.astype(F32), 0.0), axis=1, keepdims=True)
-    slots[...] = chosen.astype(jnp.int32) * capacity + position.astype(jnp.int32)
     slots_t = ids_row[...] * capacity + position_t.astype(jnp.int32)
+    spread = jnp.broadcast_to(slots_t.astype(F32), (128, tokens))
+    slots[...] = spread.T[:, 0:1].astype(jnp.int32)
     grads = (gate * cotangent[...].astype(F32)).astype(BF)
-
-    def group(begin, count):
-        number = slot_of_row(
-            lax.broadcasted_iota(jnp.int32, (count, 1), 0) + begin, experts, capacity
-        )
-        return jnp.where(number == slots_t, 1.0, 0.0).astype(BF)
-
-    for begin, count, lane in ((0, body, 0), (body, body, width)):
-        place = group(begin, count)
-        send[0, :, lane : lane + width] = product(place, low).astype(BF)
-        send[1, :, lane : lane + width] = product(place, grads).astype(BF)
-    place = group(2 * body, body // 2)
-    send[0, :, 2 * width :] = pack_third(product(place, low), experts).astype(BF)
-    send[1, :, 2 * width :] = pack_third(product(place, grads), experts).astype(BF)
-
-
-def expert_body(
-    packed, weight_in, weight_out,
-    value, back, in_grad, out_grad, tail_rows, tail_grads,
-):
-    width = weight_in.shape[0]
-    rows, grads = packed.at[0], packed.at[1]
-    body = packed.shape[1]
-    runs = body // 16
-    tail_rows[...] = unpack_third(rows[:, 2 * width :], runs).astype(BF)
-    tail_grads[...] = unpack_third(grads[:, 2 * width :], runs).astype(BF)
-    in_grad[...] = jnp.zeros(in_grad.shape, F32)
-    out_grad[...] = jnp.zeros(out_grad.shape, F32)
-
-    def chunk(x, g):
+    meet(signals)
+
+    mine = pl.ds(pl.multiple_of(here * lanes, 128), lanes)
+    tail = pl.ds(4 * lanes, leave.shape[2] - 4 * lanes)
+    own = pl.ds(pl.multiple_of(me * 16, 16), 16)
+    place_row = lax.broadcasted_iota(jnp.int32, (zone_rows * 5 // 2, 1), 0)
+    third = place_row - 2 * zone_rows
+    inside = jnp.where(
+        place_row < zone_rows,
+        place_row // 16 * capacity + place_row % 16,
+        jnp.where(
+            place_row < 2 * zone_rows,
+            (place_row - zone_rows) // 16 * capacity + 16 + place_row % 16,
+            third // 8 * capacity + 32 + third % 8,
+        ),
+    )
+    for k in range(GROUPS):
+        zone = lax.rem(me // part + k, GROUPS)
+        place = jnp.where(inside + zone * (part * capacity) == slots_t, 1.0, 0.0).astype(BF)
+        spot = pl.ds(pl.multiple_of(zone * zone_rows, 16), zone_rows)
+        for array, source in ((0, low), (1, grads)):
+            picked = product(place, source)
+            leave[array, spot, 0:width] = picked[:zone_rows].astype(BF)
+            leave[array, spot, width : 2 * width] = picked[zone_rows : 2 * zone_rows].astype(BF)
+            packed = pack_third(picked[2 * zone_rows :], part)
+            leave[array, spot, 2 * width :] = packed.astype(BF)
+        if k == 0:
+            arrived[:, own, mine] = leave[:, own, mine]
+            arrived[:, own, tail] = leave[:, own, tail]
+        for columns, sent, landed in ((mine, 0, arrive), (tail, 1, arrive_tail)):
+
+            def step(j, carry):
+                peer = zone * part + lax.rem(me + j, part)
+                block = pl.ds(pl.multiple_of(peer * 16, 16), 16)
+                remote(
+                    leave.at[:, block, columns], arrived.at[:, own, columns],
+                    send.at[sent], landed.at[k], exp=peer,
+                ).start()
+                return carry
+
+            lax.fori_loop(1 if k == 0 else 0, part, step, 0)
+
+    def arriving(k):
+        return lax.rem(me // part + GROUPS - k, GROUPS) * zone_rows
+
+    def span(k, who, count, array=slice(None)):
+        spot = pl.ds(pl.multiple_of(arriving(k), 16), count)
+        return arrived.at[array, spot, pl.ds(pl.multiple_of(who * lanes, 128), lanes)]
+
+    gather = Gather(
+        lambda k, who: span(k, who, zone_rows),
+        lambda k, who, side: span(k, who, zone_rows, pl.ds(side, 1)),
+        ring_sems,
+    )
+
+    def quarter(k):
+        block = span(k, here, zone_rows - 16 if k == 0 else zone_rows)
+        remote(block, block, send.at[0], arrive.at[k], exp=me).wait_recv()
+        gather.start(k)
+
+    def whole(k):
+        gather.finish(k)
+        count = zone_rows - 16 if k == 0 else zone_rows
+        block = arrived.at[:, pl.ds(pl.multiple_of(arriving(k), 16), count), tail]
+        remote(block, block, send.at[1], arrive_tail.at[k], exp=me).wait_recv()
+
+    def experts_on(k):
+        spot = pl.ds(pl.multiple_of(arriving(k), 16), zone_rows)
+
+        def rows_of(array):
+            last = unpack_third(arrived[array, spot, 2 * width :], part).astype(BF)
+            first = [arrived[array, spot, 0:width], arrived[array, spot, width : 2 * width]]
+            return jnp.concatenate(first + [last], axis=0)
+
+        x, g = rows_of(0), rows_of(1)
         pre = product(x, weight_in[...])
         inner = jnp.tanh(gelu_root * (pre + gelu_cube * pre * pre * pre))
         act = (0.5 * pre * (1.0 + inner)).astype(BF)
         slope = 0.5 * (1.0 + inner) + 0.5 * pre * (1.0 - inner * inner) * (
             gelu_root * (1.0 + 3.0 * gelu_cube * pre * pre)
         )
+        act_grad = cols_product(g, weight_out[...])
+        pre_grad = (act_grad * slope).astype(BF)
+        rows_back = cols_product(pre_grad, weight_in[...])
         out = product(act, weight_out[...])
         dots = jnp.sum(out * g.astype(F32), axis=1, keepdims=True)
-        out_grad[...] += rows_product(act, g)
-        act_grad = cols_product(g, weight_out[...])
-        pre_grad = (act_grad * slope).astype(BF)
-        in_grad[...] += rows_product(x, pre_grad)
-        rows_back = cols_product(pre_grad, weight_in[...])
-        return out, dots, rows_back
-
-    lane = lax.broadcasted_iota(jnp.int32, (1, 128), 1)
-    part = 256
-    for begin in range(0, body, part):
-        spot = pl.ds(begin, part)
-        marks = jnp.zeros((part, 128), F32)
-        for side in (0, 1):
-            lanes = slice(side * width, (side + 1) * width)
-            out, dots, rows_back = chunk(rows[spot, lanes], grads[spot, lanes])
-            value[spot, lanes] = out.astype(BF)
-            back[spot, lanes] = rows_back.astype(BF)
-            marks = marks + jnp.where(lane == side, dots, 0.0)
-        back[spot, 2 * width + width // 2 :] = marks.astype(BF)
-    out, dots, rows_back = chunk(tail_rows[...], tail_grads[...])
-    value[:, 2 * width + width // 2 :] = jnp.zeros((body, 128), BF)
-    value[:, 2 * width : 2 * width + width // 2] = pack_third(out, runs).astype(BF)
-    back[:, 2 * width : 2 * width + width // 2] = pack_third(rows_back, runs).astype(BF)
-    spread = jnp.where(lane == 2, dots, 0.0).reshape(runs, 8, 128)
-    spread = jnp.concatenate([spread, jnp.zeros_like(spread)], axis=1).reshape(body, 128)
-    marks = back[:, 2 * width + width // 2 :].astype(F32) + spread
-    back[:, 2 * width + width // 2 :] = marks.astype(BF)
+        lane = lax.broadcasted_iota(jnp.int32, (1, 128), 1)
+        marks = jnp.where(lane == 0, dots[:zone_rows], 0.0)
+        marks = marks + jnp.where(lane == 1, dots[zone_rows : 2 * zone_rows], 0.0)
+        last = jnp.where(lane == 2, dots[2 * zone_rows :], 0.0).reshape(part, 8, 128)
+        last = jnp.concatenate([last, jnp.zeros_like(last)], axis=1).reshape(zone_rows, 128)
+        for ref, result, extra in (
+            (back, rows_back, marks + last),
+            (value, out, jnp.zeros((zone_rows, 128), F32)),
+        ):
+            ref[spot, 0:width] = result[:zone_rows].astype(BF)
+            ref[spot, width : 2 * width] = result[zone_rows : 2 * zone_rows].astype(BF)
+            packed = pack_third(result[2 * zone_rows :], part)
+            ref[spot, 2 * width : 2 * width + width // 2] = packed.astype(BF)
+            ref[spot, 2 * width + width // 2 :] = extra.astype(BF)
+        return x, g, act, pre_grad
+
+    def weights_on(k, held):
+        x, g, act, pre_grad = held
+        if k == 0:
+            out_grad[...] = rows_product(act, g)
+            in_grad[...] = rows_product(x, pre_grad)
+        else:
+            out_grad[...] += rows_product(act, g)
+            in_grad[...] += rows_product(x, pre_grad)
+
+    reduce, gather_back, scatter, collect, drain = return_parts(
+        batch_size, back_lanes, back, back_sum, stage, buffers,
+        send_back, arrive_back, sum_sems, back_sems,
+    )
+
+    def work(k):
+        whole(k)
+        held = experts_on(k)
+        reduce.start(k)
+        weights_on(k, held)
+
+    quarter(0)
+    quarter(1)
+    gather.forward(0)
+    quarter(2)
+    gather.forward(1)
+    work(0)
+    quarter(3)
+    gather.forward(2)
+    reduce.middle(0)
+    work(1)
+    gather.forward(3)
+    reduce.middle(1)
+    scatter(0)
+    work(2)
+    reduce.middle(2)
+    scatter(1)
+    collect(0)
+    work(3)
+    reduce.middle(3)
+    scatter(2)
+    collect(1)
+    gather_back.forward(0)
+    scatter(3)
+    collect(2)
+    gather_back.forward(1)
+    collect(3)
+    gather_back.forward(2)
+    gather_back.forward(3)
+    for k in range(GROUPS):
+        gather_back.finish(k)
+    drain()
+    for k in range(GROUPS):
+        gather.drain(k)
+    for columns, sent in ((mine, 0), (tail, 1)):
+        block = leave.at[:, pl.ds(0, (batch_size - 1) * 16), columns]
+        remote(block, block, send.at[sent], arrive.at[0], exp=me).wait_send()
 
 
 def place_of(slots, experts, capacity, rows):
@@ -849,24 +888,26 @@
     def run(begin, end):
         lax.fori_loop(begin, end, step, 0)
 
-    run(0, 2)
+    run(0, 1)
     scatter(0)
+    run(1, 2)
     scatter(1)
     run(2, 3)
     scatter(2)
+    collect(0)
+    run(3, 4)
     scatter(3)
-    run(3, 5)
-    collect(0)
     collect(1)
+    gather.forward(0)
+    run(4, 5)
+    collect(2)
+    gather.forward(1)
     run(5, 6)
-    collect(2)
     collect(3)
+    gather.forward(2)
     run(6, 7)
-    gather.forward(0)
-    gather.forward(1)
+    gather.forward(3)
     run(7, blocks)
-    gather.forward(2)
-    gather.forward(3)
     backs = [query_back[...], key_acc[...].T.astype(BF), value_acc[...].T.astype(BF)]
     backs_t = [query_back[...].astype(F32).T.astype(BF)]
     backs_t += [key_acc[...].astype(BF), value_acc[...].astype(BF)]
@@ -926,7 +967,6 @@
     capacity = 5 * tokens // (4 * experts)
     body = 16 * experts
     packed = 2 * width + width // 2
-    quarter = width // 2
     span = 2 * tokens - BLOCK
     ring_size = width // here
     gain_one = first_gain[None, :]
@@ -956,55 +996,43 @@
             pltpu.VMEM((tokens, here), BF),
             sems(tokens // BLOCK // 2, 8),
             sems(1, 8),
+            sems(3, 2),
         ],
         layer_in, gain_one, *weights, proj_weight, buckets, table,
         number=1,
     )
-    residual, hidden, probs, leaving, slots, gates = call(
-        functools.partial(route_body, capacity),
-        "route",
+    wide_lanes = (packed + 128) // 4
+    residual, hidden, probs, slots, gates, value, back_sum, in_grad, out_grad = call(
+        functools.partial(moe_body, experts, capacity, 256, wide_lanes),
+        "experts",
         [
             ((tokens, width), F32),
             ((tokens, width), BF),
             ((tokens, experts), F32),
-            ((2, body, packed), BF),
             ((tokens, 1), jnp.int32),
             ((tokens, 1), F32),
-        ],
-        [],
-        layer_in, mixed_all, proj_all, gain_two, router, expert_ids.reshape(1, tokens), cotangent,
-    )
-    (arrived,) = call(
-        functools.partial(dispatch_body, experts, quarter),
-        "dispatch",
-        [((2, body, packed), BF)],
-        [sems(2), sems(GROUPS + 1), sems(GROUPS, 8)],
-        leaving,
-        number=2,
-    )
-    value, back, in_grad, out_grad = call(
-        expert_body,
-        "expert",
-        [
             ((body, packed + 128), BF),
             ((body, packed + 128), BF),
             ((width, expert_in.shape[2]), F32),
             ((expert_out.shape[1], width), F32),
         ],
-        [pltpu.VMEM((body // 2, width), BF)] * 2,
-        arrived, expert_in[0], expert_out[0],
-    )
-
-    (back_sum,) = call(
-        functools.partial(return_body, experts, (packed + 128) // 4),
-        "give_back",
-        [((body, packed + 128), BF)],
-        return_scratch(experts, (packed + 128) // 4),
-        back,
-        number=3,
+        [
+            pltpu.VMEM((2, body, packed), BF),
+            pltpu.VMEM((2, body, packed), BF),
+            pltpu.VMEM((body, packed + 128), BF),
+            *return_scratch(experts, wide_lanes),
+            sems(2),
+            sems(GROUPS),
+            sems(GROUPS),
+            sems(GROUPS, 8),
+        ],
+        layer_in, mixed_all, proj_all, gain_two, router, expert_ids.reshape(1, tokens), cotangent,
+        expert_in[0], expert_out[0],
+        number=2,
+        mib=60,
     )
     returned, residual_grad, normed_part, large, small = call(
-        functools.partial(backward_body, experts, capacity, head_width, (packed + 128) // 4),
+        functools.partial(backward_body, experts, capacity, head_width, wide_lanes),
         "backward",
         [
             ((body, packed + 128), BF),
@@ -1021,7 +1049,7 @@
             pltpu.VMEM((tokens, here), BF),
             pltpu.VMEM((here, tokens), F32),
             pltpu.VMEM((here, tokens), F32),
-            *return_scratch(experts, (packed + 128) // 4),
+            *return_scratch(experts, wide_lanes),
         ],
         value, back_sum, slots, residual, hidden, probs, gain_two, router, cotangent, mixed,
         proj_weight, normed, query, query_t, key, key_t, value_t, logsum, *weights, buckets, table,

time: 274 us -> 253 us (0.923)
  Pallas kernels: 247 us -> 225 us
    pallas_call x7 -> x4, Pallas kernels: 242 us -> 220 us  [call(): pl.pallas_call(body, name=name, out_shape=[jax.ShapeDtypeStruct(shape, dt...]
    unnamed x65 -> x49, local copies, waits for them, and re-layouts: 18.4 us -> 19.3 us
where the time goes in v3:
time: 253 us; the launch traced here: 249 us
  Pallas kernels  225 us (89%)
  local copies, waits for them, and re-layouts  21.9 us (9%)
    pallas_call x4, Pallas kernels, call(): pl.pallas_call(body, name=name, out_shape=[jax.ShapeDtypeStruct(shape, dt...  220 us
    unnamed x49, local copies, waits for them, and re-layouts  19.3 us

profile of v3, /device:TPU:1, one launch (start us, length us, event | category | flops | bytes accessed | tf_op | source)
XLA Modules:
  0.0 248.8 jit_solution(11463045934152881376)
XLA Ops:
  0.6 0.7 broadcast_in_dim.15.gain
  1.3 1.3 broadcast_in_dim.17.gain
  2.6 0.7 pad.4
  3.3 0.0 copy-start.5
  3.3 1.0 copy-done.5
  4.3 0.0 copy-start.6
  4.3 1.0 copy-done.6
  5.2 0.0 copy-start.7
  5.2 1.0 copy-done.7
  6.2 0.0 copy-start.8
  6.2 1.0 copy-done.8
  7.2 0.0 copy-start.19
  7.2 0.7 copy-done.19
  7.8 28.5 %attend.1 = (bf16[1024,192]{1,0:T(8,128)(2,1)S(1)}, bf16[4,512,384]{2,1,0:T(8,128)(2,1)}, bf16[4,192,768]{2,1,0:T(8,128)(2,1)S(1)}, bf16[1024,768]{1,0:T(8,128)(...) custom-call(bf16[1024,768]{1,0:T(8,128)(2,1)} %rows.7, ...), custom_call_target="tpu_custom_call" | custom-call | tf_op jit(solution)/shard_map/attend/pallas_call | solution.py:40
  36.4 0.0 copy-start.4
  36.4 1.0 copy-done.4
  37.4 0.0 copy-start.10
  37.4 0.8 copy-done.10
  38.2 0.0 copy-start.11
  38.2 0.8 copy-done.11
  39.0 0.8 copy-done.12
  39.8 0.8 copy-done.13
  40.6 0.7 copy-done.14
  41.3 0.7 copy-done.15
  42.1 0.7 copy-done.16
  42.8 98.8 %experts.1 = (f32[1024,768]{1,0:T(8,128)}, bf16[1024,768]{1,0:T(8,128)(2,1)}, f32[1024,32]{1,0:T(8,128)}, s32[1024,1]{1,0:T(8,128)}, f32[1024,1]{1,0:T(8,128)}, ...) custom-call(bf16[1024,768]{1,0:T(8,128)(2,1)} %rows.7, ...), custom_call_target="tpu_custom_call" | custom-call | tf_op jit(solution)/shard_map/experts/pallas_call | solution.py:40
  141.6 0.0 copy-done.18
  141.6 0.0 copy-start.2
  141.6 0.0 copy-start.9
  141.6 53.4 %backward.1 = (bf16[512,2048]{1,0:T(8,128)(2,1)}, f32[1024,768]{1,0:T(8,128)}, bf16[1024,768]{1,0:T(8,128)(2,1)}, bf16[768,768]{1,0:T(8,128)(2,1)}, bf16[64,1024]{1,0:T(8,128)(2,1)}) custom-call(bf16[512,2048]{1,0:T(8,128)(2,1)} %get-tuple-element.52.value_in, bf16[512,2048]{1,0:T(8,128)(2,1)} %get-tuple-element.53.back, s32[1024,1]{1,0:T(8,128)} %get-tuple-element.54.slots, ...), custom_call_target="tpu_custom_call" | custom-call | tf_op jit(solution)/shard_map/backward/pallas_call | solution.py:40
  195.0 0.0 copy-done.2
  195.0 0.0 copy-done.9
  195.0 0.0 copy-start.3
  195.0 1.3 copy-done.3
  196.3 0.9 copy-done.17
  197.2 39.1 %final.1 = (bf16[1024,768]{1,0:T(8,128)(2,1)S(1)}, bf16[768,768]{1,0:T(8,128)(2,1)S(1)}, bf16[64,1024]{1,0:T(8,128)(2,1)S(1)}, bf16[3,16,1024]{2,1,0:T(8,128)(2,1)S(1)}, bf16[1024,768]{1,0:T(8,128)(2,1)}) custom-call(bf16[1024,768]{1,0:T(8,128)(2,1)} %get-tuple-element.66.part_in, bf16[768,768]{1,0:T(8,128)(2,1)S(1)} %copy-done.3, ...), custom_call_target="tpu_custom_call" | custom-call | tf_op jit(solution)/shard_map/final/pallas_call | solution.py:40
  236.3 0.0 copy-done
  236.3 0.0 copy-done.1
  236.3 0.0 copy-start.22
  236.3 4.8 %finish.1 = (f32[1024,768]{1,0:T(8,128)}, f32[192,768]{1,0:T(8,128)}, f32[192,768]{1,0:T(8,128)}, f32[192,768]{1,0:T(8,128)}, f32[192,768]{1,0:T(8,128)}, /*inde...) custom-call(bf16[1024,768]{1,0:T(8,128)(2,1)S(1)} %get-tuple-element.72.summed, ...), custom_call_target="tpu_custom_call" | custom-call | tf_op jit(solution)/shard_map/finish/pallas_call | solution.py:1102
  241.2 0.6 reduce
  241.8 0.6 reduce.1
  242.4 0.0 copy-done.22
  242.4 1.1 copy.29
  243.6 1.1 copy-done.21
  244.6 1.4 copy.30
  246.1 1.1 copy-done.20
  247.2 1.4 copy.31
  (11 shorter events, 0.0 us)
Async XLA Ops:
  3.3 138.3 %copy-start.18 = (s32[2048]{0:T(1024)}, s32[2048]{0:T(1024)S(1)}, u32[]{:S(2)}) copy-start(s32[2048]{0:T(1024)S(1)} %pad.4) | copy-start | bytes 24580
  3.3 1.0 copy-start.5
  4.3 1.0 copy-start.6
  5.2 1.0 copy-start.7
  6.2 1.0 copy-start.8
  7.2 0.7 copy-start.19
  36.4 1.0 copy-start.4
  37.4 0.8 copy-start.10
  38.2 0.8 copy-start.11
  39.0 0.8 copy-start.12
  39.8 0.8 copy-start.13
  40.6 0.7 copy-start.14
  41.3 0.7 copy-start.15
  42.1 0.7 copy-start.16
  141.6 53.4 %copy-start.2 = (s32[1024,1]{1,0:T(8,128)S(1)}, s32[1024,1]{1,0:T(8,128)}, u32[]{:S(2)}) copy-start(s32[1024,1]{1,0:T(8,128)} %get-tuple-element.54.slots) | copy-start | bytes 12292
  141.6 53.4 %copy-start.9 = (f32[1024,1]{1,0:T(8,128)S(1)}, f32[1024,1]{1,0:T(8,128)}, u32[]{:S(2)}) copy-start(f32[1024,1]{1,0:T(8,128)} %get-tuple-element.70.gates) | copy-start | bytes 12292
  195.0 1.3 copy-start.3
  196.3 0.9 copy-start.17
  197.2 39.1 %copy-start = (bf16[1024,768]{1,0:T(8,128)(2,1)S(1)}, bf16[1024,768]{1,0:T(8,128)(2,1)}, u32[]{:S(2)}) copy-start(bf16[1024,768]{1,0:T(8,128)(2,1)} %rows.7) | copy-start | bytes 4718596
  197.2 39.1 %copy-start.1 = (f32[1024,768]{1,0:T(8,128)S(1)}, f32[1024,768]{1,0:T(8,128)}, u32[]{:S(2)}) copy-start(f32[1024,768]{1,0:T(8,128)} %get-tuple-element.73.residual_grad) | copy-start | bytes 9437188
  236.3 6.1 %copy-start.22 = (bf16[1024,768]{1,0:T(8,128)(2,1)S(1)}, bf16[1024,768]{1,0:T(8,128)(2,1)}, u32[]{:S(2)}) copy-start(bf16[1024,768]{1,0:T(8,128)(2,1)} %get-tuple-element.100) | copy-start | bytes 4718596
  242.4 2.2 copy-start.21
  244.6 2.5 %copy-start.20 = (f32[768,768]{1,0:T(8,128)S(1)}, f32[768,768]{1,0:T(8,128)}, u32[]{:S(2)}) copy-start(f32[768,768]{1,0:T(8,128)} %get-tuple-element.87) | copy-start | bytes 7077892

commit v4 on v3

--- a/solution.py
+++ b/solution.py
@@ -34,15 +34,16 @@
     return lax.rsqrt(jnp.mean(values * values, axis=-1, keepdims=True) + epsilon)
 
 
-def call(body, name, outs, scratch, *operands, mib=48, number=None):
+def call(body, name, outs, scratch, *operands, mib=48, number=None, far_in=(), far_out=()):
     vmem = pl.BlockSpec(memory_space=pltpu.VMEM)
+    far = pl.BlockSpec(memory_space=pltpu.HBM)
     extra = {} if number is None else {"collective_id": number, "has_side_effects": True}
     return pl.pallas_call(
         body,
         name=name,
         out_shape=[jax.ShapeDtypeStruct(shape, dtype) for shape, dtype in outs],
-        in_specs=[vmem] * len(operands),
-        out_specs=[vmem] * len(outs),
+        in_specs=[far if i in far_in else vmem for i in range(len(operands))],
+        out_specs=[far if i in far_out else vmem for i in range(len(outs))],
         scratch_shapes=scratch,
         compiler_params=pltpu.CompilerParams(vmem_limit_bytes=mib * MIB, **extra),
     )(*operands)
@@ -94,6 +95,16 @@
     pl.semaphore_wait(pltpu.get_barrier_semaphore(), signals)
 
 
+def place_index(device):
+    z, y, core = device // 8, device // 2 % 4, device % 2
+    return (z + y) % 4 * 8 + z * 2 + core
+
+
+def device_at(place):
+    group, z, core = place // 8, place % 8 // 2, place % 2
+    return z * 8 + (group + 4 - z) % 4 * 2 + core
+
+
 class Gather:
     def __init__(self, region, half, sems):
         self.region, self.half, self.sems = region, half, sems
@@ -202,16 +213,17 @@
 
 def return_parts(batch_size, lanes, source, out, stage, buffers, send, arrive, sum_sems, ring_sems):
     me = lax.axis_index("exp")
+    position = place_index(me)
     here = lax.axis_index("tp")
     part = batch_size // GROUPS
     mine = pl.ds(pl.multiple_of(here * lanes, 128), lanes)
-    own = pl.ds(pl.multiple_of(me * 16, 16), 16)
+    own = pl.ds(pl.multiple_of(position * 16, 16), 16)
 
     def leaving(k):
-        return lax.rem(me // part + GROUPS - k, GROUPS) * (part * 16)
+        return lax.rem(position // part + GROUPS - k, GROUPS) * (part * 16)
 
     def arriving(k):
-        return lax.rem(me // part + k, GROUPS) * (part * 16)
+        return lax.rem(position // part + k, GROUPS) * (part * 16)
 
     def span(ref, base, who, begin, rows):
         spot = pl.ds(pl.multiple_of(base + begin, 16), rows)
@@ -238,9 +250,12 @@
             out[own, mine] = stage[own, :]
 
         def step(j, carry):
-            peer = lax.rem(me // part + GROUPS - k, GROUPS) * part + lax.rem(me + j, part)
+            group = lax.rem(position // part + GROUPS - k, GROUPS)
+            peer = group * part + lax.rem(position + j, part)
             rows = pl.ds(pl.multiple_of(peer * 16, 16), 16)
-            remote(stage.at[rows, :], out.at[own, mine], send.at[0], arrive.at[k], exp=peer).start()
+            remote(
+                stage.at[rows, :], out.at[own, mine], send.at[0], arrive.at[k], exp=device_at(peer)
+            ).start()
             return carry
 
         lax.fori_loop(1 if k == 0 else 0, part, step, 0)
@@ -273,9 +288,9 @@
 
 
 def final_body(
-    batch_size, capacity, part_in, large, small, returned, slots, gates, residual,
-    summed, large_out, small_out, lines, output,
-    large_side, small_side, large_in, small_in, *rest,
+    batch_size, capacity, part_in, large, small, returned_far, slots, gates, residual_far,
+    summed, large_out, small_out, lines, output_far,
+    large_side, small_side, large_in, small_in, returned, residual, output, far_sems, *rest,
 ):
     buffers, (send, arrive, line_sems, sum_sems, ring_sems) = rest[:6], rest[6:]
     signals = greet(4, batch_size, opposite=True, same_core=True)
@@ -326,6 +341,12 @@
         lane = core * half_lanes + lax.rem(who, small_across) * 128
         return small_out.at[down, pl.ds(pl.multiple_of(lane, 128), 128)]
 
+    late = [
+        pltpu.make_async_copy(returned_far, returned, far_sems.at[0]),
+        pltpu.make_async_copy(residual_far, residual, far_sems.at[1]),
+    ]
+    for copy in late:
+        copy.start()
     meet(signals)
     pair = [
         remote(large_half(large, 1 - core), large_side, send.at[0], arrive.at[0], exp=sibling),
@@ -359,8 +380,12 @@
     experts = batch_size
     body = 16 * experts
     place = place_of(slots[...], experts, capacity, 5 * body // 2)
+    for copy in late:
+        copy.wait()
     token_rows = fetch(place, returned, width, experts)
     output[...] = (residual[...] + gates[...] * token_rows).astype(BF)
+    kept = pltpu.make_async_copy(output, output_far, far_sems.at[2])
+    kept.start()
 
     large_rest = large_in.at[pl.ds(1, peers - 1)]
     small_rest = small_in.at[pl.ds(1, peers - 1)]
@@ -413,6 +438,7 @@
         gather.finish(k)
     for copy in copies:
         copy.wait_recv()
+    kept.wait()
     for copy in copies + pair + back:
         copy.wait_send()
     for i, ref in ((2, large_rest), (3, small_rest), (4, large_rest), (5, small_rest)):
@@ -423,10 +449,22 @@
 
 
 def finish_body(
-    summed, rows, residual_grad, gain, large, small, lines,
+    summed, rows, residual_grad, gain, large, small, lines, output, in_grad, out_grad,
     input_grad, query_grad, key_grad, value_grad, proj_grad, router_grad, gain_grad, first_grad,
-    table_grad,
+    table_grad, output_last, in_grad_last, out_grad_last, far_sems,
 ):
+    passed = [
+        pltpu.make_async_copy(source, target, far_sems.at[i])
+        for i, (source, target) in enumerate(
+            ((output, output_last), (in_grad, in_grad_last), (out_grad, out_grad_last))
+        )
+    ]
+
+    @pl.when(pl.program_id(0) == 0)
+    def _():
+        for copy in passed:
+            copy.start()
+
     inputs = rows[...].astype(F32)
     scale = inverse_rms(inputs)
     scaled = summed[...].astype(F32) * gain[...]
@@ -448,6 +486,11 @@
             total = total + lines[i][:, 0:width].astype(F32)
         first_grad[...] = total[8:9]
 
+    @pl.when(pl.program_id(0) == pl.num_programs(0) - 1)
+    def _():
+        for copy in passed:
+            copy.wait()
+
 
 def head_mask(head, head_width, width):
     lane = lax.broadcasted_iota(jnp.int32, (1, width), 1)
@@ -469,9 +512,12 @@
 
 
 def attend_body(
-    head_width, rows, gain, query_w, key_w, value_w, proj, buckets, table,
-    mixed, mixed_all, proj_all, normed, query, query_t, key, key_t, value_t, logsum,
-    bias, value, ring_sems, proj_sems, pair_sems,
+    head_width, capacity,
+    rows, gain, query_w, key_w, value_w, proj, buckets, table, second_gain, router_w, ids_row,
+    mixed_far, normed_far, query_far, query_t_far, key_far, key_t_far, value_t_far, logsum_far,
+    residual, hidden, probs, slots, slots_row, gates,
+    mixed, normed, query, query_t, key, key_t, value_t, logsum,
+    mixed_all, proj_all, bias, value, ring_sems, proj_sems, pair_sems, far_sems,
 ):
     heads = bias.shape[0]
     tokens = rows.shape[0]
@@ -519,6 +565,19 @@
     query_t[...] = cols_product(query_w[...], low).astype(BF)
     key_t[...] = cols_product(key_w[...], low).astype(BF)
     value_t[...] = cols_product(value_w[...], low).astype(BF)
+    def keep(ref, far, i):
+        copy = pltpu.make_async_copy(ref, far, far_sems.at[i])
+        copy.start()
+        return [copy]
+
+    early_copies = []
+    for i, (ref, far) in enumerate(
+        (
+            (normed, normed_far), (query, query_far), (query_t, query_t_far), (key, key_far),
+            (key_t, key_t_far), (value_t, value_t_far),
+        )
+    ):
+        early_copies += keep(ref, far, i)
     fill_bias(bias, buckets, table)
     weights_gather.forward(0)
     for i in (0, 1):
@@ -557,11 +616,46 @@
     to_sibling(2, foreign[2], core).start()
     lax.fori_loop(pairs // 2, pairs, step, 0)
     gather.forward(pairs - 1)
+    out_copies = keep(mixed, mixed_far, 6) + keep(logsum, logsum_far, 7)
+    experts = router_w.shape[0]
+    number = lax.broadcasted_iota(jnp.int32, (experts, tokens), 0)
+    hot_t = ids_row[...] == number
+    ones_t = jnp.where(hot_t, 1.0, 0.0)
+    across = lax.broadcasted_iota(jnp.int32, (tokens, tokens), 0)
+    along = lax.broadcasted_iota(jnp.int32, (tokens, tokens), 1)
+    upper = jnp.where(across <= along, 1.0, 0.0).astype(BF)
+    counts_t = product(ones_t.astype(BF), upper)
+    position_t = jnp.sum(jnp.where(hot_t, counts_t - 1.0, 0.0), axis=0, keepdims=True)
+    line = ids_row[...] * capacity + position_t.astype(jnp.int32)
+    slots_row[...] = line
+    slots[...] = jnp.broadcast_to(line.astype(F32), (128, tokens)).T[:, 0:1].astype(jnp.int32)
+    for i in range(3):
+        to_sibling(i, foreign[i], 1 - core).wait_recv()
     for k in range(pairs):
         gather.finish(k)
+        halves = [pl.ds(side * (tokens // 2) + k * BLOCK, BLOCK) for side in (0, 1)]
+        res = jnp.concatenate([rows[spot, :] for spot in halves], axis=0).astype(F32)
+        for i in range(mixed_all.shape[0]):
+            both = mixed_all[i, k * BLOCK : (k + 1) * BLOCK, :]
+            both = jnp.concatenate([both[:, :width], both[:, width:]], axis=0)
+            res = res + product(both, proj_all[i])
+        low = (res * inverse_rms(res) * second_gain[...]).astype(BF)
+        logits = cols_product(low, router_w[...])
+        shifted = jnp.exp(logits - jnp.max(logits, axis=-1, keepdims=True))
+        chances = shifted / jnp.sum(shifted, axis=-1, keepdims=True)
+        for side in (0, 1):
+            spot, part = halves[side], slice(side * BLOCK, (side + 1) * BLOCK)
+            residual[spot, :] = res[part]
+            hidden[spot, :] = low[part]
+            probs[spot, :] = chances[part]
+            expert = lax.broadcasted_iota(jnp.int32, (BLOCK, experts), 1)
+            hot = slots[spot, :] // capacity == expert
+            chosen = jnp.sum(jnp.where(hot, chances[part], 0.0), axis=1, keepdims=True)
+            gates[spot, :] = chosen
     for i in range(3):
-        to_sibling(i, foreign[i], 1 - core).wait_recv()
         to_sibling(i, foreign[i], core).wait_send()
+    for copy in early_copies + out_copies:
+        copy.wait()
     weights_gather.drain(0)
     for k in range(pairs):
         gather.drain(k)
@@ -582,76 +676,48 @@
 
 def slot_of_row(row, experts, capacity):
     body = 16 * experts
-    first = (row // 16) * capacity + row % 16
-    second = ((row - body) // 16) * capacity + 16 + (row - body) % 16
-    third = ((row - 2 * body) // 8) * capacity + 32 + (row - 2 * body) % 8
+    first = device_at(row // 16) * capacity + row % 16
+    second = device_at((row - body) // 16) * capacity + 16 + (row - body) % 16
+    third = device_at((row - 2 * body) // 8) * capacity + 32 + (row - 2 * body) % 8
     return jnp.where(row < body, first, jnp.where(row < 2 * body, second, third))
 
 
 def moe_body(
     batch_size, capacity, lanes, back_lanes,
-    rows, mixed, proj, gain, router_w, ids_row, cotangent, weight_in, weight_out,
-    residual, hidden, probs, slots, gates, value, back_sum, in_grad, out_grad,
-    leave, arrived, back, stage, *rest,
+    hidden, gates, slots_row, cotangent, weight_in, weight_out,
+    value, back_sum, in_grad_far, out_grad_far,
+    leave, arrived, back, in_grad, out_grad, far_sems, stage, *rest,
 ):
     buffers, (send_back, arrive_back, sum_sems, back_sems) = rest[:6], rest[6:10]
     send, arrive, arrive_tail, ring_sems = rest[10:]
     signals = greet(4, batch_size)
     me = lax.axis_index("exp")
     here = lax.axis_index("tp")
+    position = place_index(me)
     part = batch_size // GROUPS
     zone_rows = part * 16
-    tokens, width = rows.shape
-    experts = router_w.shape[0]
-    half, heads_here = mixed.shape[1], mixed.shape[2] // 2
-    for side in (0, 1):
-        spot = slice(side * half, (side + 1) * half)
-        total = rows[spot, :].astype(F32)
-        for i in range(mixed.shape[0]):
-            lane = side * heads_here
-            total = total + product(mixed[i, :, lane : lane + heads_here], proj[i])
-        residual[spot, :] = total
-    res = residual[...]
-    low = (res * inverse_rms(res) * gain[...]).astype(BF)
-    hidden[...] = low
-    logits = cols_product(low, router_w[...])
-    shifted = jnp.exp(logits - jnp.max(logits, axis=-1, keepdims=True))
-    chances = shifted / jnp.sum(shifted, axis=-1, keepdims=True)
-    probs[...] = chances
-    number = lax.broadcasted_iota(jnp.int32, (experts, tokens), 0)
-    hot_t = ids_row[...] == number
-    ones_t = jnp.where(hot_t, 1.0, 0.0)
-    hot = ones_t.T > 0.5
-    gate = jnp.sum(jnp.where(hot, chances, 0.0), axis=1, keepdims=True)
-    gates[...] = gate
-    across = lax.broadcasted_iota(jnp.int32, (tokens, tokens), 0)
-    along = lax.broadcasted_iota(jnp.int32, (tokens, tokens), 1)
-    upper = jnp.where(across <= along, 1.0, 0.0).astype(BF)
-    counts_t = product(ones_t.astype(BF), upper)
-    position_t = jnp.sum(jnp.where(hot_t, counts_t - 1.0, 0.0), axis=0, keepdims=True)
-    slots_t = ids_row[...] * capacity + position_t.astype(jnp.int32)
-    spread = jnp.broadcast_to(slots_t.astype(F32), (128, tokens))
-    slots[...] = spread.T[:, 0:1].astype(jnp.int32)
+    width = hidden.shape[1]
+    slots_t = slots_row[...]
+    low = hidden[...]
+    gate = gates[...]
     grads = (gate * cotangent[...].astype(F32)).astype(BF)
     meet(signals)
 
     mine = pl.ds(pl.multiple_of(here * lanes, 128), lanes)
     tail = pl.ds(4 * lanes, leave.shape[2] - 4 * lanes)
-    own = pl.ds(pl.multiple_of(me * 16, 16), 16)
+    own = pl.ds(pl.multiple_of(position * 16, 16), 16)
     place_row = lax.broadcasted_iota(jnp.int32, (zone_rows * 5 // 2, 1), 0)
     third = place_row - 2 * zone_rows
+    member = jnp.where(third < 0, place_row % zone_rows // 16, third // 8)
     inside = jnp.where(
         place_row < zone_rows,
-        place_row // 16 * capacity + place_row % 16,
-        jnp.where(
-            place_row < 2 * zone_rows,
-            (place_row - zone_rows) // 16 * capacity + 16 + place_row % 16,
-            third // 8 * capacity + 32 + third % 8,
-        ),
+        place_row % 16,
+        jnp.where(third < 0, 16 + place_row % 16, 32 + third % 8),
     )
     for k in range(GROUPS):
-        zone = lax.rem(me // part + k, GROUPS)
-        place = jnp.where(inside + zone * (part * capacity) == slots_t, 1.0, 0.0).astype(BF)
+        zone = lax.rem(position // part + k, GROUPS)
+        wanted = device_at(zone * part + member) * capacity + inside
+        place = jnp.where(wanted == slots_t, 1.0, 0.0).astype(BF)
         spot = pl.ds(pl.multiple_of(zone * zone_rows, 16), zone_rows)
         for array, source in ((0, low), (1, grads)):
             picked = product(place, source)
@@ -665,18 +731,18 @@
         for columns, sent, landed in ((mine, 0, arrive), (tail, 1, arrive_tail)):
 
             def step(j, carry):
-                peer = zone * part + lax.rem(me + j, part)
+                peer = zone * part + lax.rem(position + j, part)
                 block = pl.ds(pl.multiple_of(peer * 16, 16), 16)
                 remote(
                     leave.at[:, block, columns], arrived.at[:, own, columns],
-                    send.at[sent], landed.at[k], exp=peer,
+                    send.at[sent], landed.at[k], exp=device_at(peer),
                 ).start()
                 return carry
 
             lax.fori_loop(1 if k == 0 else 0, part, step, 0)
 
     def arriving(k):
-        return lax.rem(me // part + GROUPS - k, GROUPS) * zone_rows
+        return lax.rem(position // part + GROUPS - k, GROUPS) * zone_rows
 
     def span(k, who, count, array=slice(None)):
         spot = pl.ds(pl.multiple_of(arriving(k), 16), count)
@@ -773,6 +839,12 @@
     scatter(1)
     collect(0)
     work(3)
+    far_copies = [
+        pltpu.make_async_copy(in_grad, in_grad_far, far_sems.at[0]),
+        pltpu.make_async_copy(out_grad, out_grad_far, far_sems.at[1]),
+    ]
+    for copy in far_copies:
+        copy.start()
     reduce.middle(3)
     scatter(2)
     collect(1)
@@ -785,6 +857,8 @@
     gather_back.forward(3)
     for k in range(GROUPS):
         gather_back.finish(k)
+    for copy in far_copies:
+        copy.wait()
     drain()
     for k in range(GROUPS):
         gather.drain(k)
@@ -809,9 +883,10 @@
 def backward_body(
     batch_size, capacity, head_width, lanes,
     value_in, back, slots, residual, hidden, probs, gain, router_w, cotangent, mixed, proj,
-    normed, query, query_t, key, key_t, value_t, logsum,
-    query_w, key_w, value_w, buckets, table, rows,
-    returned, residual_grad, normed_part, large, small,
+    normed_far, query_far, query_t_far, key_far, key_t_far, value_t_far, logsum_far,
+    query_w, key_w, value_w, buckets, table, rows_far,
+    returned, residual_grad_far, normed_part, large, small,
+    normed, query, query_t, key, key_t, value_t, logsum, rows, residual_grad, far_sems,
     grad, grad_t, bias, sums, query_back, key_acc, value_acc, stage, *rest,
 ):
     buffers, (send, arrive, sum_sems, ring_sems) = rest[:6], rest[6:]
@@ -825,6 +900,18 @@
     heads = bias.shape[0]
     width = query.shape[1]
     blocks = tokens // BLOCK
+    late = [
+        pltpu.make_async_copy(far, ref, far_sems.at[i])
+        for i, (far, ref) in enumerate(
+            (
+                (query_far, query), (query_t_far, query_t), (key_far, key), (key_t_far, key_t),
+                (value_t_far, value_t), (logsum_far, logsum), (normed_far, normed),
+                (rows_far, rows),
+            )
+        )
+    ]
+    for copy in late:
+        copy.start()
     place = place_of(slots[...], experts, capacity, 5 * body // 2)
     meet(signals)
     for k in range(GROUPS):
@@ -851,12 +938,16 @@
     total = cotangent[...].astype(F32) + scale * scaled - res * (scale * scale * scale * middle)
     low = total.astype(BF)
     residual_grad[...] = total
+    kept = pltpu.make_async_copy(residual_grad, residual_grad_far, far_sems.at[len(late)])
+    kept.start()
     for k in range(GROUPS // 2, GROUPS):
         reduce.middle(k)
     large[3 * width :, :] = rows_product(mixed[...], low).astype(BF)
     grad[...] = cols_product(low, proj[...]).astype(BF)
     grad_t[...] = cols_product(proj[...], low).astype(BF)
 
+    for copy in late:
+        copy.wait()
     fill_bias(bias, buckets, table)
     sums[...] = jnp.zeros(sums.shape, F32)
     key_acc[...] = jnp.zeros(key_acc.shape, F32)
@@ -952,6 +1043,7 @@
     small[48:64, 0:128] = jnp.concatenate([sums_of, blank], axis=1).astype(BF)
     for k in range(GROUPS):
         gather.finish(k)
+    kept.wait()
     drain()
 
 
@@ -976,41 +1068,52 @@
     table = rel_table.T
     router = router_weight.T
 
-    mixed, mixed_all, proj_all, normed, query, query_t, key, key_t, value_t, logsum = call(
-        functools.partial(attend_body, head_width),
+    wide_lanes = (packed + 128) // 4
+    kept = [
+        ((tokens, here), BF),
+        ((tokens, width), BF),
+        ((tokens, here), BF),
+        ((here, tokens), BF),
+        ((tokens, here), BF),
+        ((here, tokens), BF),
+        ((here, tokens), BF),
+        ((tokens, 128), F32),
+    ]
+    (
+        mixed, normed, query, query_t, key, key_t, value_t, logsum,
+        residual, hidden, probs, slots, slots_row, gates,
+    ) = call(
+        functools.partial(attend_body, head_width, capacity),
         "attend",
-        [
-            ((tokens, here), BF),
-            ((ring_size, tokens // 2, 2 * here), BF),
-            ((ring_size, here, width), BF),
+        kept
+        + [
+            ((tokens, width), F32),
             ((tokens, width), BF),
-            ((tokens, here), BF),
-            ((here, tokens), BF),
-            ((tokens, here), BF),
-            ((here, tokens), BF),
-            ((here, tokens), BF),
-            ((tokens, 128), F32),
+            ((tokens, experts), F32),
+            ((tokens, 1), jnp.int32),
+            ((1, tokens), jnp.int32),
+            ((tokens, 1), F32),
         ],
-        [
+        [pltpu.VMEM(*entry) for entry in kept]
+        + [
+            pltpu.VMEM((ring_size, tokens // 2, 2 * here), BF),
+            pltpu.VMEM((ring_size, here, width), BF),
             pltpu.VMEM((heads, BLOCK, span), F32),
             pltpu.VMEM((tokens, here), BF),
             sems(tokens // BLOCK // 2, 8),
             sems(1, 8),
             sems(3, 2),
+            sems(len(kept)),
         ],
-        layer_in, gain_one, *weights, proj_weight, buckets, table,
+        layer_in, gain_one, *weights, proj_weight, buckets, table, gain_two, router,
+        expert_ids.reshape(1, tokens),
         number=1,
-    )
-    wide_lanes = (packed + 128) // 4
-    residual, hidden, probs, slots, gates, value, back_sum, in_grad, out_grad = call(
-        functools.partial(moe_body, experts, capacity, 256, wide_lanes),
+        far_out=range(len(kept)),
+    )
+    value, back_sum, in_grad, out_grad = call(
+        functools.partial(moe_body, experts, capacity, 384, wide_lanes),
         "experts",
         [
-            ((tokens, width), F32),
-            ((tokens, width), BF),
-            ((tokens, experts), F32),
-            ((tokens, 1), jnp.int32),
-            ((tokens, 1), F32),
             ((body, packed + 128), BF),
             ((body, packed + 128), BF),
             ((width, expert_in.shape[2]), F32),
@@ -1020,16 +1123,18 @@
             pltpu.VMEM((2, body, packed), BF),
             pltpu.VMEM((2, body, packed), BF),
             pltpu.VMEM((body, packed + 128), BF),
+            pltpu.VMEM((width, expert_in.shape[2]), F32),
+            pltpu.VMEM((expert_out.shape[1], width), F32),
+            sems(2),
             *return_scratch(experts, wide_lanes),
             sems(2),
             sems(GROUPS),
             sems(GROUPS),
             sems(GROUPS, 8),
         ],
-        layer_in, mixed_all, proj_all, gain_two, router, expert_ids.reshape(1, tokens), cotangent,
-        expert_in[0], expert_out[0],
+        hidden, gates, slots_row, cotangent, expert_in[0], expert_out[0],
         number=2,
-        mib=60,
+        far_out=(2, 3),
     )
     returned, residual_grad, normed_part, large, small = call(
         functools.partial(backward_body, experts, capacity, head_width, wide_lanes),
@@ -1042,6 +1147,16 @@
             ((64, 1024), BF),
         ],
         [
+            pltpu.VMEM((tokens, width), BF),
+            pltpu.VMEM((tokens, here), BF),
+            pltpu.VMEM((here, tokens), BF),
+            pltpu.VMEM((tokens, here), BF),
+            pltpu.VMEM((here, tokens), BF),
+            pltpu.VMEM((here, tokens), BF),
+            pltpu.VMEM((tokens, 128), F32),
+            pltpu.VMEM((tokens, width), BF),
+            pltpu.VMEM((tokens, width), F32),
+            sems(9),
             pltpu.VMEM((tokens, here), BF),
             pltpu.VMEM((here, tokens), BF),
             pltpu.VMEM((heads, BLOCK, span), F32),
@@ -1055,7 +1170,9 @@
         proj_weight, normed, query, query_t, key, key_t, value_t, logsum, *weights, buckets, table,
         layer_in,
         number=5,
-        mib=58,
+        mib=56,
+        far_in=(*range(11, 18), 23),
+        far_out=(1,),
     )
     peers = experts // 2
     tall, wide = 4 * here // peers, width // 2
@@ -1074,6 +1191,10 @@
             pltpu.VMEM((64, 512), BF),
             pltpu.VMEM((peers, tall, wide), BF),
             pltpu.VMEM((peers, 16, 128), BF),
+            pltpu.VMEM((body, packed + 128), BF),
+            pltpu.VMEM((tokens, width), F32),
+            pltpu.VMEM((tokens, width), BF),
+            sems(3),
             *reduce_scratch(4, tokens // 32, width),
             sems(8),
             sems(8),
@@ -1083,6 +1204,8 @@
         ],
         normed_part, large, small, returned, slots, gates, residual,
         number=4,
+        far_in=(3, 6),
+        far_out=(4,),
     )
 
     def whole(array):
@@ -1096,21 +1219,24 @@
         for shape in [(tokens, width)] + [(here, width)] * 4
         + [(experts, width), (1, width), (1, width), table.shape]
     ]
+    passed = (output, in_grad, out_grad)
+    far = pl.BlockSpec(memory_space=pltpu.HBM)
     (
         input_grad, query_grad, key_grad, value_grad, proj_total, router_total, gain_total,
-        first_total, table_total,
+        first_total, table_total, output, in_grad, out_grad,
     ) = pl.pallas_call(
         finish_body,
         name="finish",
         grid=(tokens // 128,),
-        out_shape=results,
+        out_shape=results + [jax.ShapeDtypeStruct(one.shape, one.dtype) for one in passed],
         in_specs=[
             strip(summed), strip(layer_in), strip(residual_grad), whole(gain_one),
-            whole(large_sum), whole(small_sum), whole(lines),
+            whole(large_sum), whole(small_sum), whole(lines), far, far, far,
         ],
-        out_specs=[strip(results[0])] + [whole(result) for result in results[1:]],
+        out_specs=[strip(results[0])] + [whole(result) for result in results[1:]] + [far] * 3,
+        scratch_shapes=[sems(3)],
         compiler_params=pltpu.CompilerParams(vmem_limit_bytes=32 * MIB),
-    )(summed, layer_in, residual_grad, gain_one, large_sum, small_sum, lines)
+    )(summed, layer_in, residual_grad, gain_one, large_sum, small_sum, lines, *passed)
     return (
         output,
         input_grad,

time: 253 us -> 236 us (0.933)
  Pallas kernels: 225 us -> 212 us
  local copies, waits for them, and re-layouts: 21.9 us -> 19.1 us
    pallas_call x4, Pallas kernels: 220 us -> 205 us  [call(): pl.pallas_call(body, name=name, out_shape=[jax.ShapeDtypeStruct(shape, dt...]
    unnamed x49 -> x60, local copies, waits for them, and re-layouts: 19.3 us -> 16.9 us
where the time goes in v4:
time: 236 us; the launch traced here: 233 us
  Pallas kernels  212 us (90%)
  local copies, waits for them, and re-layouts  19.1 us (8%)
    pallas_call x4, Pallas kernels, call(): pl.pallas_call(body, name=name, out_shape=[jax.ShapeDtypeStruct(shape, dt...  205 us
    unnamed x60, local copies, waits for them, and re-layouts  16.9 us
    pallas_call x1, Pallas kernels, per_device(): pl.pallas_call(finish_body, name='finish', grid=(tokens // 128,), out_sha...  6.62 us

profile of v4, /device:TPU:1, one launch (start us, length us, event | category | flops | bytes accessed | tf_op | source)
XLA Modules:
  0.0 233.0 jit_solution(16309880338701649631)
XLA Ops:
  0.6 0.0 copy-start.1
  0.7 0.0 copy-start.10
  0.7 0.8 broadcast_in_dim.15.gain
  1.5 0.7 broadcast_in_dim.17.second_gain.gain
  2.2 0.7 pad.4
  2.9 1.0 copy-done.12
  3.9 1.0 copy-done.13
  4.8 1.0 copy-done.14
  5.8 1.0 copy-done.15
  6.8 0.8 copy-done.24
  7.6 0.7 copy-done.28
  8.2 0.7 copy-done.29
  8.9 32.3 %attend.1 = (bf16[1024,192]{1,0:T(8,128)(2,1)S(1)}, bf16[1024,768]{1,0:T(8,128)(2,1)}, bf16[1024,192]{1,0:T(8,128)(2,1)S(1)}, bf16[192,1024]{1,0:T(8,128)(2,1)S(...) custom-call(bf16[1024,768]{1,0:T(8,128)(2,1)} %rows.3, ...), custom_call_target="tpu_custom_call" | custom-call | tf_op jit(solution)/shard_map/attend/pallas_call | solution.py:41
  41.3 0.0 copy-start.6
  41.3 0.8 copy-done.6
  42.1 0.8 copy-done.16
  42.9 0.8 copy-done.17
  43.7 0.8 copy-done.18
  44.5 0.7 copy-done.21
  45.2 0.0 copy-done.1
  45.2 0.0 copy-done.10
  45.2 0.0 copy-start.2
  45.2 2.0 copy-done.2
  47.3 1.3 copy-done.11
  48.6 84.6 %experts.1 = (bf16[512,2048]{1,0:T(8,128)(2,1)}, bf16[512,2048]{1,0:T(8,128)(2,1)}, f32[768,768]{1,0:T(8,128)}, f32[768,768]{1,0:T(8,128)}) custom-call(bf16[1024,768]{1,0:T(8,128)(2,1)S(1)} %copy-done.2, f32[1024,1]{1,0:T(8,128)S(1)} %get-tuple-element.53.gates, s32[1,1024]{1,0:T(1,128)S(1)} %get-tuple-element.54.slots_row, ...), custom_call_target="tpu_custom_call" | custom-call | tf_op jit(solution)/shard_map/experts/pallas_call | solution.py:41
  133.2 0.0 copy-done.27
  133.2 0.0 copy-done.26
  133.2 0.0 copy-done.19
  133.2 0.0 copy-done.20
  133.3 0.0 copy-done.22
  133.3 0.0 copy-done.23
  133.3 0.0 copy-start.7
  133.3 0.0 copy-start.5
  133.3 50.4 %backward.1 = (bf16[512,2048]{1,0:T(8,128)(2,1)}, f32[1024,768]{1,0:T(8,128)}, bf16[1024,768]{1,0:T(8,128)(2,1)}, bf16[768,768]{1,0:T(8,128)(2,1)}, bf16[64,1024]{1,0:T(8,128)(2,1)}) custom-call(bf16[512,2048]{1,0:T(8,128)(2,1)} %get-tuple-element.55.value_in, bf16[512,2048]{1,0:T(8,128)(2,1)} %get-tuple-element.56.back, s32[1024,1]{1,0:T(8,128)} %copy-done.6, ...), custom_call_target="tpu_custom_call" | custom-call | tf_op jit(solution)/shard_map/backward/pallas_call | solution.py:41
  183.7 0.0 copy-done.7
  183.7 0.0 copy-start.9
  183.7 1.3 copy-done.9
  185.0 0.9 copy-done.25
  185.9 37.6 %final.1 = (bf16[1024,768]{1,0:T(8,128)(2,1)S(1)}, bf16[768,768]{1,0:T(8,128)(2,1)S(1)}, bf16[64,1024]{1,0:T(8,128)(2,1)S(1)}, bf16[3,16,1024]{2,1,0:T(8,128)(2,1)S(1)}, bf16[1024,768]{1,0:T(8,128)(2,1)}) custom-call(bf16[1024,768]{1,0:T(8,128)(2,1)} %get-tuple-element.68.part_in, bf16[768,768]{1,0:T(8,128)(2,1)S(1)} %copy-done.9, ...), custom_call_target="tpu_custom_call" | custom-call | tf_op jit(solution)/shard_map/final/pallas_call | solution.py:41
  223.4 0.0 copy-done.5
  223.5 0.0 copy-done
  223.5 0.0 copy-done.3
  223.5 0.0 copy-done.4
  223.5 0.0 copy-start.8
  223.5 1.4 copy-done.8
  224.9 6.6 %finish.1 = (f32[1024,768]{1,0:T(8,128)}, f32[192,768]{1,0:T(8,128)}, f32[192,768]{1,0:T(8,128)}, f32[192,768]{1,0:T(8,128)}, f32[192,768]{1,0:T(8,128)}, /*inde...) custom-call(bf16[1024,768]{1,0:T(8,128)(2,1)S(1)} %get-tuple-element, ...), custom_call_target="tpu_custom_call" | custom-call | tf_op jit(solution)/shard_map/finish/pallas_call | solution.py:1227
  231.5 0.6 reduce
  232.1 0.6 reduce.1
  (22 shorter events, 0.0 us)
Async XLA Ops:
  0.6 44.6 %copy-start.1 = (bf16[1024,768]{1,0:T(8,128)(2,1)S(1)}, bf16[1024,768]{1,0:T(8,128)(2,1)}, u32[]{:S(2)}) copy-start(bf16[1024,768]{1,0:T(8,128)(2,1)} %cotangent.3) | copy-start | bytes 4718596
  0.7 44.6 %copy-start.10 = (bf16[1,768,768]{2,1,0:T(8,128)(2,1)S(1)}, bf16[1,768,768]{2,1,0:T(8,128)(2,1)}, u32[]{:S(2)}) copy-start(bf16[1,768,768]{2,1,0:T(8,128)(2,1)} %param.25) | copy-start | bytes 3538948
  2.2 131.0 %copy-start.27 = (f32[1,768]{1,0:T(1,128)}, f32[1,768]{1,0:T(1,128)S(1)}, u32[]{:S(2)}) copy-start(f32[1,768]{1,0:T(1,128)S(1)} %broadcast_in_dim.17.second_gain.gain) | copy-start | bytes 9220
  2.9 130.3 %copy-start.26 = (s32[2048]{0:T(1024)}, s32[2048]{0:T(1024)S(1)}, u32[]{:S(2)}) copy-start(s32[2048]{0:T(1024)S(1)} %pad.4) | copy-start | bytes 24580
  2.9 1.0 copy-start.12
  3.9 1.0 copy-start.13
  4.8 1.0 copy-start.14
  5.8 1.0 copy-start.15
  6.8 0.8 copy-start.24
  7.6 0.7 copy-start.28
  8.2 0.7 copy-start.29
  41.3 0.8 copy-start.6
  42.1 0.8 copy-start.16
  42.9 0.8 copy-start.17
  43.7 0.8 copy-start.18
  44.5 0.7 copy-start.21
  45.2 88.0 %copy-start.19 = (f32[1024,128]{1,0:T(8,128)}, f32[1024,128]{1,0:T(8,128)S(1)}, u32[]{:S(2)}) copy-start(f32[1024,128]{1,0:T(8,128)S(1)} %get-tuple-element.67.logsum_far) | copy-start | bytes 1572868
  45.2 88.0 %copy-start.20 = (f32[1024,32]{1,0:T(8,128)}, f32[1024,32]{1,0:T(8,128)S(1)}, u32[]{:S(2)}) copy-start(f32[1024,32]{1,0:T(8,128)S(1)} %get-tuple-element.59.probs) | copy-start | bytes 393220
  45.2 88.1 %copy-start.22 = (bf16[192,1024]{1,0:T(8,128)(2,1)}, bf16[192,1024]{1,0:T(8,128)(2,1)S(1)}, u32[]{:S(2)}) copy-start(bf16[192,1024]{1,0:T(8,128)(2,1)S(1)} %get-tuple-element.65.key_t_far) | copy-start | bytes 1179652
  45.2 88.1 %copy-start.23 = (bf16[192,1024]{1,0:T(8,128)(2,1)}, bf16[192,1024]{1,0:T(8,128)(2,1)S(1)}, u32[]{:S(2)}) copy-start(bf16[192,1024]{1,0:T(8,128)(2,1)S(1)} %get-tuple-element.66.value_t_far) | copy-start | bytes 1179652
  45.2 2.1 copy-start.2
  47.3 1.3 copy-start.11
  133.3 50.4 %copy-start.7 = (s32[1024,1]{1,0:T(8,128)S(1)}, s32[1024,1]{1,0:T(8,128)}, u32[]{:S(2)}) copy-start(s32[1024,1]{1,0:T(8,128)} %copy-done.6) | copy-start | bytes 12292
  133.3 90.2 %copy-start.5 = (f32[768,768]{1,0:T(8,128)S(1)}, f32[768,768]{1,0:T(8,128)}, u32[]{:S(2)}) copy-start(f32[768,768]{1,0:T(8,128)} %get-tuple-element.79.out_grad) | copy-start | bytes 7077892
  183.7 1.3 copy-start.9
  184.9 0.9 copy-start.25
  185.9 37.6 %copy-start = (bf16[1024,768]{1,0:T(8,128)(2,1)S(1)}, bf16[1024,768]{1,0:T(8,128)(2,1)}, u32[]{:S(2)}) copy-start(bf16[1024,768]{1,0:T(8,128)(2,1)} %rows.3) | copy-start | bytes 4718596
  185.9 37.6 %copy-start.3 = (f32[1024,768]{1,0:T(8,128)S(1)}, f32[1024,768]{1,0:T(8,128)}, u32[]{:S(2)}) copy-start(f32[1024,768]{1,0:T(8,128)} %get-tuple-element.73.residual_grad) | copy-start | bytes 9437188
  185.9 37.6 %copy-start.4 = (f32[768,768]{1,0:T(8,128)S(1)}, f32[768,768]{1,0:T(8,128)}, u32[]{:S(2)}) copy-start(f32[768,768]{1,0:T(8,128)} %get-tuple-element.78.in_grad) | copy-start | bytes 7077892
  223.5 1.4 copy-start.8

commit v5 on v4

--- a/solution.py
+++ b/solution.py
@@ -451,20 +451,11 @@
 def finish_body(
     summed, rows, residual_grad, gain, large, small, lines, output, in_grad, out_grad,
     input_grad, query_grad, key_grad, value_grad, proj_grad, router_grad, gain_grad, first_grad,
-    table_grad, output_last, in_grad_last, out_grad_last, far_sems,
+    table_grad, output_last, in_grad_last, out_grad_last,
 ):
-    passed = [
-        pltpu.make_async_copy(source, target, far_sems.at[i])
-        for i, (source, target) in enumerate(
-            ((output, output_last), (in_grad, in_grad_last), (out_grad, out_grad_last))
-        )
-    ]
-
-    @pl.when(pl.program_id(0) == 0)
-    def _():
-        for copy in passed:
-            copy.start()
-
+    output_last[...] = output[...]
+    in_grad_last[...] = in_grad[...]
+    out_grad_last[...] = out_grad[...]
     inputs = rows[...].astype(F32)
     scale = inverse_rms(inputs)
     scaled = summed[...].astype(F32) * gain[...]
@@ -480,16 +471,11 @@
             ref[...] = large[i * high : (i + 1) * high, :].astype(F32)
         router_grad[...] = small[0 : router_grad.shape[0], 0:width].astype(F32)
         total = small[32:48, 0:width].astype(F32)
-        gain_grad[...] = total[0:1]
+        gain_grad[...] = total[0]
         table_grad[...] = small[48:64, 0:128].astype(F32)[0:3, 0:32]
         for i in range(3):
             total = total + lines[i][:, 0:width].astype(F32)
-        first_grad[...] = total[8:9]
-
-    @pl.when(pl.program_id(0) == pl.num_programs(0) - 1)
-    def _():
-        for copy in passed:
-            copy.wait()
+        first_grad[...] = total[8]
 
 
 def head_mask(head, head_width, width):
@@ -714,6 +700,21 @@
         place_row % 16,
         jnp.where(third < 0, 16 + place_row % 16, 32 + third % 8),
     )
+
+    def scatter_rows(k, columns, sent, landed):
+        zone = lax.rem(position // part + k, GROUPS)
+
+        def step(j, carry):
+            peer = zone * part + lax.rem(position + j, part)
+            block = pl.ds(pl.multiple_of(peer * 16, 16), 16)
+            remote(
+                leave.at[:, block, columns], arrived.at[:, own, columns],
+                send.at[sent], landed.at[k], exp=device_at(peer),
+            ).start()
+            return carry
+
+        lax.fori_loop(1 if k == 0 else 0, part, step, 0)
+
     for k in range(GROUPS):
         zone = lax.rem(position // part + k, GROUPS)
         wanted = device_at(zone * part + member) * capacity + inside
@@ -728,18 +729,9 @@
         if k == 0:
             arrived[:, own, mine] = leave[:, own, mine]
             arrived[:, own, tail] = leave[:, own, tail]
-        for columns, sent, landed in ((mine, 0, arrive), (tail, 1, arrive_tail)):
-
-            def step(j, carry):
-                peer = zone * part + lax.rem(position + j, part)
-                block = pl.ds(pl.multiple_of(peer * 16, 16), 16)
-                remote(
-                    leave.at[:, block, columns], arrived.at[:, own, columns],
-                    send.at[sent], landed.at[k], exp=device_at(peer),
-                ).start()
-                return carry
-
-            lax.fori_loop(1 if k == 0 else 0, part, step, 0)
+        scatter_rows(k, mine, 0, arrive)
+    for k in range(GROUPS):
+        scatter_rows(k, tail, 1, arrive_tail)
 
     def arriving(k):
         return lax.rem(position // part + GROUPS - k, GROUPS) * zone_rows
@@ -1061,8 +1053,8 @@
     packed = 2 * width + width // 2
     span = 2 * tokens - BLOCK
     ring_size = width // here
-    gain_one = first_gain[None, :]
-    gain_two = second_gain[None, :]
+    gain_one = first_gain
+    gain_two = second_gain
     buckets = jnp.pad(rel_buckets, (0, 1), constant_values=-1)[None, :]
     weights = (query_weight.T, key_weight.T, value_weight.T)
     table = rel_table.T
@@ -1107,6 +1099,7 @@
         ],
         layer_in, gain_one, *weights, proj_weight, buckets, table, gain_two, router,
         expert_ids.reshape(1, tokens),
+        mib=62,
         number=1,
         far_out=range(len(kept)),
     )
@@ -1169,8 +1162,8 @@
         value, back_sum, slots, residual, hidden, probs, gain_two, router, cotangent, mixed,
         proj_weight, normed, query, query_t, key, key_t, value_t, logsum, *weights, buckets, table,
         layer_in,
+        mib=56,
         number=5,
-        mib=56,
         far_in=(*range(11, 18), 23),
         far_out=(1,),
     )
@@ -1212,41 +1205,40 @@
         return pl.BlockSpec(array.shape, lambda i: (0,) * len(array.shape))
 
     def strip(array):
-        return pl.BlockSpec((128, array.shape[1]), lambda i: (i, 0))
+        return pl.BlockSpec((array.shape[0] // 8, array.shape[1]), lambda i: (i, 0))
 
     results = [
         jax.ShapeDtypeStruct(shape, F32)
         for shape in [(tokens, width)] + [(here, width)] * 4
-        + [(experts, width), (1, width), (1, width), table.shape]
+        + [(experts, width), (width,), (width,), table.shape]
     ]
     passed = (output, in_grad, out_grad)
-    far = pl.BlockSpec(memory_space=pltpu.HBM)
+    strips = [strip(one) for one in passed]
     (
         input_grad, query_grad, key_grad, value_grad, proj_total, router_total, gain_total,
         first_total, table_total, output, in_grad, out_grad,
     ) = pl.pallas_call(
         finish_body,
         name="finish",
-        grid=(tokens // 128,),
+        grid=(8,),
         out_shape=results + [jax.ShapeDtypeStruct(one.shape, one.dtype) for one in passed],
         in_specs=[
             strip(summed), strip(layer_in), strip(residual_grad), whole(gain_one),
-            whole(large_sum), whole(small_sum), whole(lines), far, far, far,
+            whole(large_sum), whole(small_sum), whole(lines), *strips,
         ],
-        out_specs=[strip(results[0])] + [whole(result) for result in results[1:]] + [far] * 3,
-        scratch_shapes=[sems(3)],
+        out_specs=[strip(results[0])] + [whole(result) for result in results[1:]] + strips,
         compiler_params=pltpu.CompilerParams(vmem_limit_bytes=32 * MIB),
     )(summed, layer_in, residual_grad, gain_one, large_sum, small_sum, lines, *passed)
     return (
         output,
         input_grad,
-        first_total[0],
+        first_total,
         query_grad.T,
         key_grad.T,
         value_grad.T,
         proj_total,
         table_total.T,
-        gain_total[0],
+        gain_total,
         router_total.T,
         in_grad[None],
         out_grad[None],

time: 236 us -> 228 us (0.966)
  local copies, waits for them, and re-layouts: 19.1 us -> 10.7 us
    unnamed x60 -> x32, local copies, waits for them, and re-layouts: 16.9 us -> 9.26 us
where the time goes in v5:
time: 228 us; the launch traced here: 225 us
  Pallas kernels  213 us (93%)
  local copies, waits for them, and re-layouts  10.7 us (5%)
    pallas_call x4, Pallas kernels, call(): pl.pallas_call(body, name=name, out_shape=[jax.ShapeDtypeStruct(shape, dt...  207 us
    unnamed x32, local copies, waits for them, and re-layouts  9.26 us
    pallas_call x1, Pallas kernels, per_device(): pl.pallas_call(finish_body, name='finish', grid=(8,), out_shape=results +...  6.16 us

profile of v5, /device:TPU:1, one launch (start us, length us, event | category | flops | bytes accessed | tf_op | source)
XLA Modules:
  0.0 224.6 jit_solution(6616192138986168554)
XLA Ops:
  0.6 0.0 copy-start.1
  0.7 1.4 pad.4
  2.1 32.7 %attend.1 = (bf16[1024,192]{1,0:T(8,128)(2,1)}, bf16[1024,768]{1,0:T(8,128)(2,1)}, bf16[1024,192]{1,0:T(8,128)(2,1)}, bf16[192,1024]{1,0:T(8,128)(2,1)}, bf16[10...) custom-call(bf16[1024,768]{1,0:T(8,128)(2,1)} %rows.3, ...), custom_call_target="tpu_custom_call" | custom-call | tf_op jit(solution)/shard_map/attend/pallas_call | solution.py:41
  34.8 0.0 copy-done.1
  34.8 0.0 copy-start.2
  34.8 1.4 copy-done.2
  36.2 0.0 copy-start.7
  36.2 1.0 copy-done.7
  37.3 0.0 copy-start.11
  37.3 1.3 copy-done.11
  38.6 0.0 copy-start.12
  38.6 1.3 copy-done.12
  39.8 0.0 copy-start.15
  39.8 0.7 copy-done.15
  40.5 85.3 %experts.1 = (bf16[512,2048]{1,0:T(8,128)(2,1)}, bf16[512,2048]{1,0:T(8,128)(2,1)}, f32[768,768]{1,0:T(8,128)}, f32[768,768]{1,0:T(8,128)}) custom-call(bf16[1024,768]{1,0:T(8,128)(2,1)S(1)} %copy-done.2, f32[1024,1]{1,0:T(8,128)S(1)} %copy-done.7, s32[1,1024]{1,0:T(1,128)S(1)} %copy-done.15, bf16[1024,768]{1,0:T(8,128)(2,1)S(1)} %copy-done.1, ...), custom_call_target="tpu_custom_call" | custom-call | tf_op jit(solution)/shard_map/experts/pallas_call | solution.py:41
  125.8 0.0 copy-start.6
  125.8 0.0 copy-start.8
  125.8 0.0 copy-start.5
  125.9 52.1 %backward.1 = (bf16[512,2048]{1,0:T(8,128)(2,1)}, f32[1024,768]{1,0:T(8,128)}, bf16[1024,768]{1,0:T(8,128)(2,1)}, bf16[768,768]{1,0:T(8,128)(2,1)}, bf16[64,1024]{1,0:T(8,128)(2,1)}) custom-call(bf16[512,2048]{1,0:T(8,128)(2,1)} %get-tuple-element.55.value_in, bf16[512,2048]{1,0:T(8,128)(2,1)} %get-tuple-element.56.back, s32[1024,1]{1,0:T(8,128)} %get-tuple-element.57.slots, ...), custom_call_target="tpu_custom_call" | custom-call | tf_op jit(solution)/shard_map/backward/pallas_call | solution.py:41
  178.0 0.0 copy-done.6
  178.0 0.0 copy-done.8
  178.0 0.0 copy-start.10
  178.0 1.3 copy-done.10
  179.3 0.0 copy-start.13
  179.3 0.9 copy-done.13
  180.2 0.0 copy-start
  180.2 0.0 copy-start.3
  180.2 0.0 copy-start.4
  180.2 0.0 copy-start.14
  180.2 36.5 %final.1 = (bf16[1024,768]{1,0:T(8,128)(2,1)S(1)}, bf16[768,768]{1,0:T(8,128)(2,1)S(1)}, bf16[64,1024]{1,0:T(8,128)(2,1)S(1)}, bf16[3,16,1024]{2,1,0:T(8,128)(2,1)S(1)}, bf16[1024,768]{1,0:T(8,128)(2,1)}) custom-call(bf16[1024,768]{1,0:T(8,128)(2,1)} %get-tuple-element.68.part_in, bf16[768,768]{1,0:T(8,128)(2,1)S(1)} %copy-done.10, ...), custom_call_target="tpu_custom_call" | custom-call | tf_op jit(solution)/shard_map/final/pallas_call | solution.py:41
  216.7 0.0 copy-done.5
  216.7 0.0 copy-done
  216.8 0.0 copy-done.3
  216.8 0.0 copy-done.4
  216.8 0.0 copy-done.14
  216.8 0.0 copy-start.9
  216.8 1.4 copy-done.9
  218.2 6.2 %finish.1 = (f32[1024,768]{1,0:T(8,128)}, f32[192,768]{1,0:T(8,128)}, f32[192,768]{1,0:T(8,128)}, f32[192,768]{1,0:T(8,128)}, f32[192,768]{1,0:T(8,128)}, /*inde...) custom-call(bf16[1024,768]{1,0:T(8,128)(2,1)S(1)} %get-tuple-element, ...), custom_call_target="tpu_custom_call" | custom-call | tf_op jit(solution)/shard_map/finish/pallas_call | solution.py:1220
Async XLA Ops:
  0.6 34.2 %copy-start.1 = (bf16[1024,768]{1,0:T(8,128)(2,1)S(1)}, bf16[1024,768]{1,0:T(8,128)(2,1)}, u32[]{:S(2)}) copy-start(bf16[1024,768]{1,0:T(8,128)(2,1)} %cotangent.3) | copy-start | bytes 4718596
  34.8 1.4 copy-start.2
  36.2 1.0 copy-start.7
  37.3 1.3 copy-start.11
  38.6 1.3 copy-start.12
  39.8 0.7 copy-start.15
  125.8 52.2 %copy-start.6 = (s32[1024,1]{1,0:T(8,128)S(1)}, s32[1024,1]{1,0:T(8,128)}, u32[]{:S(2)}) copy-start(s32[1024,1]{1,0:T(8,128)} %get-tuple-element.57.slots) | copy-start | bytes 12292
  125.8 52.2 %copy-start.8 = (f32[1024,1]{1,0:T(8,128)S(1)}, f32[1024,1]{1,0:T(8,128)}, u32[]{:S(2)}) copy-start(f32[1024,1]{1,0:T(8,128)} %get-tuple-element.53.gates) | copy-start | bytes 12292
  125.8 90.9 %copy-start.5 = (f32[768,768]{1,0:T(8,128)S(1)}, f32[768,768]{1,0:T(8,128)}, u32[]{:S(2)}) copy-start(f32[768,768]{1,0:T(8,128)} %get-tuple-element.79.out_grad) | copy-start | bytes 7077892
  178.0 1.3 copy-start.10
  179.3 0.9 copy-start.13
  180.2 36.6 %copy-start = (bf16[1024,768]{1,0:T(8,128)(2,1)S(1)}, bf16[1024,768]{1,0:T(8,128)(2,1)}, u32[]{:S(2)}) copy-start(bf16[1024,768]{1,0:T(8,128)(2,1)} %rows.3) | copy-start | bytes 4718596
  180.2 36.6 %copy-start.3 = (f32[1024,768]{1,0:T(8,128)S(1)}, f32[1024,768]{1,0:T(8,128)}, u32[]{:S(2)}) copy-start(f32[1024,768]{1,0:T(8,128)} %get-tuple-element.73.residual_grad) | copy-start | bytes 9437188
  180.2 36.6 %copy-start.4 = (f32[768,768]{1,0:T(8,128)S(1)}, f32[768,768]{1,0:T(8,128)}, u32[]{:S(2)}) copy-start(f32[768,768]{1,0:T(8,128)} %get-tuple-element.78.in_grad) | copy-start | bytes 7077892
  180.2 36.6 %copy-start.14 = (f32[768]{0:T(1024)S(1)}, f32[768]{0:T(1024)}, u32[]{:S(2)}) copy-start(f32[768]{0:T(1024)} %gain.5) | copy-start | bytes 9220
  216.8 1.4 copy-start.9
